TPU v7x, 512 devices: a whole 4x8x8 slice. The times are simulated.
512 devices in a mesh: rows: 64 (over z, y), rep: 8 (over x, core).
Axes of the slice: x: 4, y: 8, z: 8, core: 2. Of those that a mesh axis runs over, the one named last changes fastest.
Arguments:
- nodes: bfloat16 [8192, 512], P('rows'), may hold values from -6 to 6
- adjacency: bfloat16 [8192, 8192], P('rows', 'rep'), may hold values from 0 to 2, as said below
- gain: float32 [512], replicated, may hold values from 0.1 to 1.9
- w_in: bfloat16 [512, 512], replicated, may hold values from -0.25 to 0.25
- w_out: bfloat16 [512, 512], replicated, may hold values from -0.25 to 0.25
- cotangent: bfloat16 [8192, 512], P('rows'), may hold values from -2 to 2
Outputs:
- node_out: bfloat16 [8192, 512], P('rows')
- node_grad: bfloat16 [8192, 512], P('rows')
- grad_w_in: float32 [512, 512], replicated
- grad_w_out: float32 [512, 512], replicated
- grad_gain: float32 [512], replicated
Inputs may be any that keep to these rules, and one draw needn't show every extreme that they name: adjacency holds whole numbers, is symmetric, every diagonal entry is 1, and off the diagonal it is zero outside a set of live 128 x 128 blocks.
All inputs are finite; a program needn't handle non-finite values.
Results may differ from a plain program's by a relative error of at most 0.0054.
Values may be sent and summed in bfloat16 or wider, within the bound.
No kernel may reach another device: no remote copies, remote signals or barrier semaphores. Data moves between devices by JAX's collectives and lax.ppermute only.
A program may use at most 64 MiB of HBM per device.

v0:
```python
import jax
import jax.numpy as jnp
from jax import lax
from jax.sharding import PartitionSpec as P


def broadcast(x, axis, root):
    mine = lax.axis_index(axis) == root
    return lax.psum(jnp.where(mine, x, jnp.zeros_like(x)), axis)


def aggregate(strip_half, field):
    owners = lax.axis_size("rows") // lax.axis_size("rep")
    group = field.shape[0]
    first_owner = lax.axis_index("rep") * owners
    total = jnp.zeros((group, field.shape[1]), jnp.float32)
    for step in range(owners):
        owner_block = broadcast(field, "rows", first_owner + step)
        columns = strip_half[:, step * group : (step + 1) * group]
        total = total + jnp.dot(columns, owner_block, preferred_element_type=jnp.float32)
    return total


def node_update(summed, nodes, cotangent, gain, w_in, w_out):
    scale = lax.rsqrt(jnp.mean(summed * summed, axis=-1, keepdims=True) + 1e-05)
    normed = summed * scale
    lifted = (normed * gain).astype(jnp.bfloat16)
    pre = jnp.dot(lifted, w_in, preferred_element_type=jnp.float32)
    sigma = jax.nn.sigmoid(pre)
    hidden = (pre * sigma).astype(jnp.bfloat16)
    node_out = (
        nodes.astype(jnp.float32) + jnp.dot(hidden, w_out, preferred_element_type=jnp.float32)
    ).astype(jnp.bfloat16)
    grad_hidden = jnp.dot(cotangent, w_out.T, preferred_element_type=jnp.float32)
    grad_pre = (grad_hidden * sigma * (1.0 + pre * (1.0 - sigma))).astype(jnp.bfloat16)
    grad_w_out = jnp.dot(hidden.T, cotangent, preferred_element_type=jnp.float32)
    grad_w_in = jnp.dot(lifted.T, grad_pre, preferred_element_type=jnp.float32)
    grad_lifted = jnp.dot(grad_pre, w_in.T, preferred_element_type=jnp.float32)
    grad_gain = jnp.sum(grad_lifted * normed, axis=0)
    grad_normed = grad_lifted * gain
    grad_summed = (
        scale * (grad_normed - normed * jnp.mean(grad_normed * normed, axis=-1, keepdims=True))
    ).astype(jnp.bfloat16)
    return (node_out, grad_summed, grad_w_in, grad_w_out, grad_gain)


def shards(nodes, adjacency, gain, w_in, w_out, cotangent):
    partial_value = aggregate(adjacency, nodes)

    def reduce_full(terms):
        return lax.psum(terms, "rep")

    summed = reduce_full(partial_value)
    node_out, grad_summed, grad_w_in, grad_w_out, grad_gain = node_update(
        summed, nodes, cotangent, gain, w_in, w_out
    )
    back_full = reduce_full(aggregate(adjacency, grad_summed))
    node_grad = (cotangent.astype(jnp.float32) + back_full).astype(jnp.bfloat16)
    grad_w_in, grad_w_out, grad_gain = lax.psum((grad_w_in, grad_w_out, grad_gain), "rows")
    return (node_out, node_grad, grad_w_in, grad_w_out, grad_gain)


def solution(mesh):
    return jax.shard_map(
        shards,
        mesh=mesh,
        in_specs=(P("rows", None), P("rows", "rep"), P(), P(), P(), P("rows", None)),
        out_specs=(P("rows", None), P("rows", None), P(), P(), P()),
        check_vma=False,
    )
```

profile of v0, /device:TPU:1, one launch (start us, length us, event | category | flops | bytes accessed | tf_op | source)
XLA Modules:
  0.0 666.5 jit_solution(6623236035741863277)
XLA Ops:
  7.2 1.1 copy.11
  8.3 1.0 broadcast_select_fusion.1
  9.4 166.3 %all-reduce.17.cloned.1.call-done = (bf16[128,512]{0,1:T(8,128)(2,1)}, bf16[128,512]{0,1:T(8,128)(2,1)}, bf16[128,512]{0,1:T(8,128)(2,1)}, bf16[128,512]{0,1:T(8...) async-done(((bf16[128,512]{0,1:T(8,128)(2,1)}, bf16[128,512]{0,1:T(8,128)(2,1)}, ...) | async-done | bytes 1048592 | tf_op jit(solution)/shard_map/psum | solution.py:9
  175.7 1.1 fusion.21
  178.9 0.7 copy-done.14
  180.7 0.7 copy-done.10
  182.3 0.9 fusion.1
  183.2 69.4 %all-reduce.9.cloned.1.call-done = f32[128,512]{0,1:T(8,128)} async-done(((f32[128,512]{0,1:T(8,128)}), f32[128,512]{0,1:T(8,128)}) %all-reduce.9.cloned.1.call-update) | async-done | bytes 262160 | tf_op jit(solution)/shard_map/psum | solution.py:51
  252.7 1.1 multiply_reduce_fusion.2
  255.6 0.8 broadcast_select_fusion
  256.4 0.9 broadcast_select_fusion.2
  257.4 1.3 fusion.23
  258.8 156.8 %all-reduce.15.cloned.1.call-done = (bf16[128,512]{0,1:T(8,128)(2,1)}, bf16[128,512]{0,1:T(8,128)(2,1)}, bf16[128,512]{0,1:T(8,128)(2,1)}, bf16[128,512]{0,1:T(8...) async-done(((bf16[128,512]{0,1:T(8,128)(2,1)}, bf16[128,512]{0,1:T(8,128)(2,1)}, ...) | async-done | bytes 1048592 | tf_op jit(solution)/shard_map/psum | solution.py:9
  415.6 1.1 fusion.19
  420.6 0.7 copy-done.7
  422.2 0.9 fusion
  423.1 1.3 fusion.25
  424.6 113.9 %psum.167 = f32[512]{0:T(512)} all-reduce(f32[512]{0:T(512)S(1)} %get-tuple-element.10), channel_id=1, replica_groups=mesh['rows'=64,'rep'=8] {'rows'}, use_global_device_ids=true, to_apply=%region_23.24 | all-reduce | flops 512 | bytes 4096 | tf_op jit(solution)/shard_map/psum | solution.py:59
  538.5 0.9 fusion.3
  539.4 1.0 add_convert_fusion
  540.4 0.8 copy.22
  541.2 115.5 %all-reduce.13.cloned.1.call-done = (f32[512,512]{1,0:T(8,128)}, f32[512,512]{1,0:T(8,128)}) async-done(((f32[512,512]{1,0:T(8,128)}, f32[512,512]{1,0:T(8,128)}), (f32[512,512]{1,0:T(8,128)}, f32[512,512]{1,0:T(8,128)})) %all-reduce.13.cloned.1.call-update) | async-done | bytes 2097168 | tf_op jit(solution)/shard_map/psum | solution.py:59
  656.7 2.4 copy.44
  659.0 1.0 copy.45
  (70 shorter events, 10.9 us)
Async XLA Ops:
  7.2 246.6 %copy-start = (bf16[512,512]{1,0:T(8,128)(2,1)S(1)}, bf16[512,512]{1,0:T(8,128)(2,1)}, u32[]{:S(2)}) copy-start(bf16[512,512]{1,0:T(8,128)(2,1)} %param.9) | copy-start | bytes 1572868
  7.2 168.5 %all-reduce.17.cloned.1.call-start = ((), (), s32[]{:S(2)}) async-start(), calls=%async_computation.4 | async-start | bytes 2097152 | tf_op jit(solution)/shard_map/psum | solution.py:9
  9.3 166.4 %copy-start.3 = (bf16[128,1024]{1,0:T(8,128)(2,1)S(1)}, bf16[128,1024]{1,0:T(8,128)(2,1)}, u32[]{:S(2)}) copy-start(bf16[128,1024]{1,0:T(8,128)(2,1)} %param.7) | copy-start | bytes 786436
  9.3 243.3 %all-reduce.9.cloned.1.call-start = ((), (), s32[]{:S(2)}) async-start(), calls=%async_computation | async-start | bytes 524288 | tf_op jit(solution)/shard_map/psum | solution.py:51
  175.7 1.1 copy-start.19
  176.9 0.9 copy-start.18
  177.8 0.9 copy-start.16
  180.5 0.9 copy-start.10
  181.4 0.9 copy-start.8
  183.2 232.4 %all-reduce.15.cloned.1.call-start = ((), (), s32[]{:S(2)}) async-start(), calls=%async_computation.3 | async-start | bytes 2097152 | tf_op jit(solution)/shard_map/psum | solution.py:9
  252.7 1.1 copy-start.1
  252.7 1.1 copy-start.20
  253.8 0.9 copy-start.4
  253.8 1.1 copy-start.21
  257.4 282.0 %all-reduce.11.cloned.1.call-start = ((), (), s32[]{:S(2)}) async-start(), calls=%async_computation.1 | async-start | bytes 524288 | tf_op jit(solution)/shard_map/psum | solution.py:51
  415.6 1.1 copy-start.17
  416.7 0.9 copy-start.15
  417.7 0.9 copy-start.13
  418.6 0.9 copy-start.11
  419.5 0.9 copy-start.9
  420.4 0.9 copy-start.7
  423.1 233.6 %all-reduce.13.cloned.1.call-start = ((), (), s32[]{:S(2)}) async-start(), calls=%async_computation.2 | async-start | bytes 4194304 | tf_op jit(solution)/shard_map/psum | solution.py:59
  424.5 114.1 %copy-start.5 = (bf16[128,512]{1,0:T(8,128)(2,1)S(1)}, bf16[128,512]{1,0:T(8,128)(2,1)}, u32[]{:S(2)}) copy-start(bf16[128,512]{1,0:T(8,128)(2,1)} %param.6) | copy-start | bytes 393220
  656.7 2.4 copy-start.2
  (3 other events, 2.7 us)
Sparse Core Ops, SparseCore 0:
  12.7 162.9 all-reduce.16
  183.3 69.2 all-reduce.8
  257.5 158.0 all-reduce.14
  423.2 69.5 all-reduce.10
  496.6 160.0 all-reduce.12
where the time goes:
time: 670 us; the launch traced here: 667 us
  waiting for transfers between devices  508 us (76%)
  blocking collectives  114 us (17%)
  local copies, waits for them, and re-layouts  14.5 us (2%)
  between operations  14 us (2%)
  matrix products  10.9 us (2%)
    psum x2, waiting for transfers between devices, broadcast(): return lax.psum(jnp.where(mine, x, jnp.zeros_like(x)), axis)  323 us
    psum x1, waiting for transfers between devices, shards(): lax.psum((grad_w_in, grad_w_out, grad_gain), 'rows')  115 us
    psum x1, blocking collectives, shards(): lax.psum((grad_w_in, grad_w_out, grad_gain), 'rows')  114 us
    psum x2, waiting for transfers between devices, reduce_full(): return lax.psum(terms, 'rep')  69.4 us
    unnamed x49, local copies, waits for them, and re-layouts  14.5 us
  transfers between devices with their start and end apart: 5, of which 4 were waited for; matrix products, arithmetic and copies ran while one was open for 1% of the time, Pallas kernels for 0%

commit v1 on v0

v1 whole, which is shorter than its diff:
```python
import jax
import jax.numpy as jnp
from jax import lax
from jax.sharding import PartitionSpec as P

BF = jnp.bfloat16
F32 = jnp.float32
NR = 64
NP = 8
S = 16


def index(z, y, p):
    return (z * 8 + y) * NP + p


TRIPLES = [(z, y, p) for z in range(8) for y in range(8) for p in range(8)]
OUT = [(index(z, y, p), index(y, p, z)) for z, y, p in TRIPLES]
BACK = [(b, a) for a, b in OUT]


def dot(a, b, ca, cb):
    return lax.dot_general(a, b, (((ca,), (cb,)), ((), ())), preferred_element_type=F32)


def spread(x, axis, n):
    return lax.all_to_all(jnp.broadcast_to(x, (n,) + x.shape), axis, 0, 0)


def shards(nodes, adjacency, gain, w_in, w_out, cotangent):
    p = lax.axis_index("rep")
    own = lambda a: lax.dynamic_slice_in_dim(a, p * S, S, 0)
    cot_piece = own(cotangent)
    moved = lax.ppermute(jnp.stack([own(nodes), cot_piece]), ("rows", "rep"), OUT)
    x, cot = moved[0], moved[1]

    part = dot(adjacency, nodes, 0, 0).astype(BF).reshape(NR, S, 512)
    got = lax.all_to_all(part, "rows", 0, 0)
    summed = jnp.sum(got.astype(F32), axis=0)

    scale = lax.rsqrt(jnp.mean(summed * summed, axis=-1, keepdims=True) + 1e-05)
    normed = summed * scale
    lifted = (normed * gain).astype(BF)
    pre = dot(lifted, w_in, 1, 0)
    sigma = jax.nn.sigmoid(pre)
    hidden = (pre * sigma).astype(BF)
    node_out = (x.astype(F32) + dot(hidden, w_out, 1, 0)).astype(BF)
    grad_hidden = dot(cot, w_out, 1, 1)
    grad_pre = (grad_hidden * sigma * (1.0 + pre * (1.0 - sigma))).astype(BF)
    grad_lifted = dot(grad_pre, w_in, 1, 1)
    gain_part = jnp.sum(grad_lifted * normed, axis=0)
    grad_normed = grad_lifted * gain
    grad_summed = (
        scale * (grad_normed - normed * jnp.mean(grad_normed * normed, axis=-1, keepdims=True))
    ).astype(BF)

    field = spread(grad_summed, "rows", NR).reshape(NR * S, 512)
    back = dot(adjacency, field, 1, 0).reshape(NP, S, 512)

    acts = jnp.stack(
        [
            jnp.concatenate(
                [lifted[:, 128 * i : 128 * i + 128], hidden[:, 128 * i : 128 * i + 128],
                 grad_pre[:, 256 * c : 256 * c + 256], cot[:, 256 * c : 256 * c + 256]], axis=1)
            for i in range(4) for c in range(2)
        ]
    )
    acts = lax.all_to_all(acts, "rep", 0, 0).reshape(NP * S, 768)
    w2 = jnp.concatenate(
        [dot(acts[:, 0:128], acts[:, 256:512], 0, 0), dot(acts[:, 128:256], acts[:, 512:768], 0, 0)], axis=0
    )
    blocks = w2.reshape(32, 8, 2, 128).transpose(0, 2, 1, 3).reshape(NR, 8, 128)
    gain_rows = jnp.broadcast_to(jnp.pad(gain_part.reshape(4, 128), ((0, 4), (0, 0))), (NR, 8, 128))
    terms = jnp.concatenate([blocks, gain_rows], axis=1).astype(BF)
    terms = jnp.sum(lax.all_to_all(terms, "rows", 0, 0).astype(F32), axis=0)
    mine = spread(terms[:8].astype(BF), "rows", NR)

    back = lax.all_to_all(back, "rep", 0, 0)
    node_grad = (cot_piece.astype(F32) + jnp.sum(back, axis=0)).astype(BF)

    node_out = lax.ppermute(node_out, ("rows", "rep"), BACK)
    gain_row = jnp.pad(terms[8:12].reshape(1, 512), ((0, 15), (0, 0))).astype(BF)
    table = mine.reshape(16, 4, 8, 128).transpose(0, 2, 1, 3).reshape(128, 512)
    last = spread(jnp.concatenate([table, node_grad, node_out, gain_row], axis=0), "rep", NP)
    node_grad = last[:, 128:144].reshape(128, 512)
    node_out = last[:, 144:160].reshape(128, 512)
    grad_gain = jnp.sum(last[:, 160].astype(F32), axis=0)
    w2 = last[:, :128].reshape(4, 2, 16, 8, 4, 128).transpose(0, 1, 2, 4, 3, 5).reshape(4, 2, 2, 16, 2, 8, 128)
    w2 = w2.transpose(2, 0, 3, 5, 1, 4, 6).reshape(2, 512, 512).astype(F32)
    return (node_out, node_grad, w2[0], w2[1], grad_gain)


def solution(mesh):
    return jax.shard_map(
        shards,
        mesh=mesh,
        in_specs=(P("rows", None), P("rows", "rep"), P(), P(), P(), P("rows", None)),
        out_specs=(P("rows", None), P("rows", None), P(), P(), P()),
        check_vma=False,
    )
```

time: 670 us -> 187 us (0.28)
  waiting for transfers between devices: 508 us -> 80 us
  blocking collectives: 114 us -> 23.9 us
  starting transfers between devices: 0.21 us -> 62.4 us
  between operations: 14 us -> 0.88 us
  local copies, waits for them, and re-layouts: 14.5 us -> 6.56 us
    psum x5 -> x0, waiting for transfers between devices: 508 us -> none  [the longest x2 323 us: broadcast(): return lax.psum(jnp.where(mine, x, jnp.zeros_like(x)), axis)]
    psum x1 -> x0, blocking collectives: 114 us -> none  [shards(): lax.psum((grad_w_in, grad_w_out, grad_gain), 'rows')]
    all_to_all x0 -> x6, waiting for transfers between devices: none -> 65.4 us  [the longest x2 36.7 us: spread(): return lax.all_to_all(jnp.broadcast_to(x, (n,) + x.shape), axis, 0, 0)]
    all_to_all x0 -> x6, starting transfers between devices: none -> 56.1 us  [the longest x1 17.3 us: shards(): got = lax.all_to_all(part, 'rows', 0, 0)]
    all_to_all x0 -> x1, blocking collectives: none -> 23.9 us  [spread(): return lax.all_to_all(jnp.broadcast_to(x, (n,) + x.shape), axis, 0, 0)]
    ppermute x0 -> x2, waiting for transfers between devices: none -> 14.6 us  [the longest x1 14.6 us: shards(): lax.ppermute(jnp.stack([own(nodes), cot_piece]), ('rows', 'rep'), OUT)]
    unnamed x49 -> x10, local copies, waits for them, and re-layouts: 14.5 us -> 0.03 us
  transfers between devices with their start and end apart: 5 -> 8, of which waited for: 4 -> 7; matrix products, arithmetic and copies ran while one was open for 1% -> 3% of each run, Pallas kernels for 0% -> 0%
where the time goes in v1:
time: 187 us; the launch traced here: 186 us
  waiting for transfers between devices  80 us (43%)
  starting transfers between devices  62.4 us (33%)
  blocking collectives  23.9 us (13%)
  other arithmetic  7.83 us (4%)
  local copies, waits for them, and re-layouts  6.56 us (4%)
  matrix products  4.87 us (3%)
    all_to_all x2, waiting for transfers between devices, spread(): return lax.all_to_all(jnp.broadcast_to(x, (n,) + x.shape), axis, 0, 0)  36.7 us
    all_to_all x1, blocking collectives, spread(): return lax.all_to_all(jnp.broadcast_to(x, (n,) + x.shape), axis, 0, 0)  23.9 us
    all_to_all x1, starting transfers between devices, shards(): got = lax.all_to_all(part, 'rows', 0, 0)  17.3 us
    all_to_all x2, starting transfers between devices, spread(): return lax.all_to_all(jnp.broadcast_to(x, (n,) + x.shape), axis, 0, 0)  16.1 us
    ppermute x1, waiting for transfers between devices, shards(): lax.ppermute(jnp.stack([own(nodes), cot_piece]), ('rows', 'rep'), OUT)  14.6 us
    all_to_all x1, waiting for transfers between devices, shards(): terms = jnp.sum(lax.all_to_all(terms, 'rows', 0, 0).astype(F32), axis=0)  11.5 us
    all_to_all x1, starting transfers between devices, shards(): acts = lax.all_to_all(acts, 'rep', 0, 0).reshape(NP * S, 768)  8.08 us
    all_to_all x1, starting transfers between devices, shards(): terms = jnp.sum(lax.all_to_all(terms, 'rows', 0, 0).astype(F32), axis=0)  7.95 us
  transfers between devices with their start and end apart: 8, of which 7 were waited for; matrix products, arithmetic and copies ran while one was open for 3% of the time, Pallas kernels for 0%

profile of v1, /device:TPU:1, one launch (start us, length us, event | category | flops | bytes accessed | tf_op | source)
XLA Modules:
  0.0 186.4 jit_solution(15792962334224752502)
XLA Ops:
  0.7 2.5 %convolution_convert_fusion = bf16[1024,512]{1,0:T(8,128)(2,1)} fusion(bf16[128,1024]{1,0:T(8,128)(2,1)} %param.7, bf16[128,512]{1,0:T(8,128)(2,1)} %param.6), kind=kOutput, calls=%fused_computation.1 | convolution fusion | flops 134742016 | bytes 1441792 | tf_op jit(solution)/shard_map/dot_general | solution.py:23
  3.1 17.3 %all-to-all-start = ((bf16[64,16,512]{2,1,0:T(8,128)(2,1)}), bf16[64,16,512]{2,1,0:T(8,128)(2,1)S(1)}, u32[]{:S(2)}, u32[]{:S(2)}) async-start(bf16[64,16,512]{2,1,0:T(8,128)(2,1)} %bitcast), calls=%async_computation | async-start | bytes 2097152 | tf_op jit(solution)/shard_map/all_to_all | solution.py:38
  20.4 0.7 dynamic-slice_bitcast_fusion
  21.9 4.0 %collective-permute-start = (bf16[2,16,512]{2,1,0:T(8,128)(2,1)S(1)}, bf16[2,16,512]{2,1,0:T(8,128)(2,1)S(1)}, u32[]{:S(2)}, u32[]{:S(2)}) collective-permute-start(bf16[2,16,512]{2,1,0:T(8,128)(2,1)S(1)} %pad_maximum_fusion.18), channel_id=1, source_target_pairs={{0,0},{1,8},{2,16},{3,24},{4,32},{5,40},{6,48},{7,56},{8,64},{9,72... | collective-permute-start | bytes 98312 | tf_op jit(solution)/shard_map/ppermute | solution.py:34
  25.9 14.6 %collective-permute-done = bf16[2,16,512]{2,1,0:T(8,128)(2,1)S(1)} collective-permute-done((bf16[2,16,512]{2,1,0:T(8,128)(2,1)S(1)}, bf16[2,16,512]{2,1,0:T(8,128)(2,1)S(1)}, u32[]{:S(2)}, u32[]{:S(2)}) %collective-permute-start) | collective-permute-done | bytes 32800 | tf_op jit(solution)/shard_map/ppermute | solution.py:34
  40.5 7.4 %all-to-all-done = bf16[64,16,512]{2,1,0:T(8,128)(2,1)S(1)} async-done(((bf16[64,16,512]{2,1,0:T(8,128)(2,1)}), bf16[64,16,512]{2,1,0:T(8,128)(2,1)S(1)}, u32[]{:S(2)}, u32[]{:S(2)}) %all-to-all-start) | async-done | bytes 1048608 | tf_op jit(solution)/shard_map/all_to_all | solution.py:38
  54.0 8.1 %all-to-all-start.1 = ((bf16[8,16,768]{2,1,0:T(8,128)(2,1)}), bf16[8,16,768]{2,1,0:T(8,128)(2,1)S(1)}, u32[]{:S(2)}, u32[]{:S(2)}) async-start(bf16[8,16,768]{2,1,0:T(8,128)(2,1)} %fusion.16), calls=%async_computation.1 | async-start | bytes 393216 | tf_op jit(solution)/shard_map/all_to_all | solution.py:68
  62.2 5.8 %all-to-all-done.1 = bf16[8,16,768]{2,1,0:T(8,128)(2,1)S(1)} async-done(((bf16[8,16,768]{2,1,0:T(8,128)(2,1)}), bf16[8,16,768]{2,1,0:T(8,128)(2,1)S(1)}, u32[]{:S(2)}, u32[]{:S(2)}) %all-to-all-start.1) | async-done | bytes 196640 | tf_op jit(solution)/shard_map/all_to_all | solution.py:68
  68.0 1.1 broadcast_in_dim.18
  69.1 9.0 %all-to-all-start.4 = ((bf16[64,16,512]{2,1,0:T(8,128)(2,1)}), bf16[64,16,512]{2,1,0:T(8,128)(2,1)S(1)}, u32[]{:S(2)}, u32[]{:S(2)}) async-start(bf16[64,16,512]{2,1,0:T(8,128)(2,1)} %broadcast_in_dim.18), calls=%async_computation.4 | async-start | bytes 2097152 | tf_op jit(solution)/shard_map/all_to_all | solution.py:27
  78.6 0.7 pad_maximum_fusion
  79.3 25.9 %all-to-all-done.4 = bf16[64,16,512]{2,1,0:T(8,128)(2,1)S(1)} async-done(((bf16[64,16,512]{2,1,0:T(8,128)(2,1)}), bf16[64,16,512]{2,1,0:T(8,128)(2,1)S(1)}, u32[]{:S(2)}, u32[]{:S(2)}) %all-to-all-start.4) | async-done | bytes 1048608 | tf_op jit(solution)/shard_map/all_to_all | solution.py:27
  105.2 8.0 %all-to-all-start.2 = ((bf16[64,16,128]{2,1,0:T(8,128)(2,1)}), bf16[64,16,128]{2,1,0:T(8,128)(2,1)S(1)}, u32[]{:S(2)}, u32[]{:S(2)}) async-start(bf16[64,16,128]{2,1,0:T(8,128)(2,1)} %pad_maximum_fusion), calls=%async_computation.2 | async-start | bytes 524288 | tf_op jit(solution)/shard_map/all_to_all | solution.py:75
  113.2 1.0 fusion.32
  114.2 11.5 %all-to-all-done.2 = bf16[64,16,128]{2,1,0:T(8,128)(2,1)S(1)} async-done(((bf16[64,16,128]{2,1,0:T(8,128)(2,1)}), bf16[64,16,128]{2,1,0:T(8,128)(2,1)S(1)}, u32[]{:S(2)}, u32[]{:S(2)}) %all-to-all-start.2) | async-done | bytes 262176 | tf_op jit(solution)/shard_map/all_to_all | solution.py:75
  125.7 6.7 %all-to-all-start.5 = ((f32[8,16,512]{2,1,0:T(8,128)}), f32[8,16,512]{2,1,0:T(8,128)S(1)}, u32[]{:S(2)}, u32[]{:S(2)}) async-start(f32[8,16,512]{2,1,0:T(8,128)} %bitcast.22), calls=%async_computation.5 | async-start | bytes 524288 | tf_op jit(solution)/shard_map/all_to_all | solution.py:78
  132.6 2.2 %collective-permute-start.1 = (bf16[16,512]{1,0:T(8,128)(2,1)S(1)}, bf16[16,512]{1,0:T(8,128)(2,1)S(1)}, u32[]{:S(2)}, u32[]{:S(2)}) collective-permute-start(bf16[16,512]{1,0:T(8,128)(2,1)S(1)} %fusion.8), channel_id=1, source_target_pairs={{0,0},{8,1},{16,2},{24,3},{32,4},{40,5},{48,6},{56,7},{64,8},{72,9... | collective-permute-start | bytes 49160 | tf_op jit(solution)/shard_map/ppermute | solution.py:81
  135.0 4.0 %all-to-all-done.5 = f32[8,16,512]{2,1,0:T(8,128)S(1)} async-done(((f32[8,16,512]{2,1,0:T(8,128)}), f32[8,16,512]{2,1,0:T(8,128)S(1)}, u32[]{:S(2)}, u32[]{:S(2)}) %all-to-all-start.5) | async-done | bytes 262176 | tf_op jit(solution)/shard_map/all_to_all | solution.py:78
  139.6 7.1 %all-to-all-start.3 = ((bf16[64,8,128]{2,1,0:T(8,128)(2,1)}), bf16[64,8,128]{2,1,0:T(8,128)(2,1)S(1)}, u32[]{:S(2)}, u32[]{:S(2)}) async-start(bf16[64,8,128]{2,1,0:T(8,128)(2,1)} %broadcast_in_dim.17), calls=%async_computation.3 | async-start | bytes 262144 | tf_op jit(solution)/shard_map/all_to_all | solution.py:27
  146.8 0.7 add_convert_fusion
  147.5 10.8 %all-to-all-done.3 = bf16[64,8,128]{2,1,0:T(8,128)(2,1)S(1)} async-done(((bf16[64,8,128]{2,1,0:T(8,128)(2,1)}), bf16[64,8,128]{2,1,0:T(8,128)(2,1)S(1)}, u32[]{:S(2)}, u32[]{:S(2)}) %all-to-all-start.3) | async-done | bytes 131104 | tf_op jit(solution)/shard_map/all_to_all | solution.py:27
  158.4 23.9 %all_to_all.35 = bf16[8,176,512]{2,1,0:T(8,128)(2,1)S(1)} all-to-all(bf16[8,176,512]{2,1,0:T(8,128)(2,1)S(1)} %broadcast_in_dim.19), channel_id=1, replica_groups=mesh['rows'=64,'rep'=8] {'rep'}, dimensions={0} | all-to-all | bytes 2883584 | tf_op jit(solution)/shard_map/all_to_all | solution.py:27
  182.8 1.1 copy.12
  183.9 1.1 copy.11
  (51 shorter events, 10.3 us)
Async XLA Ops:
  0.6 47.6 %copy-start = (bf16[512,512]{1,0:T(8,128)(2,1)S(1)}, bf16[512,512]{1,0:T(8,128)(2,1)}, u32[]{:S(2)}) copy-start(bf16[512,512]{1,0:T(8,128)(2,1)} %param.9) | copy-start | bytes 1572868
  0.6 47.5 %copy-start.3 = (f32[512]{0:T(512)S(1)}, f32[512]{0:T(512)}, u32[]{:S(2)}) copy-start(f32[512]{0:T(512)} %param.8) | copy-start | bytes 6148
  3.1 45.4 %copy-start.1 = (bf16[512,512]{1,0:T(8,128)(2,1)S(1)}, bf16[512,512]{1,0:T(8,128)(2,1)}, u32[]{:S(2)}) copy-start(bf16[512,512]{1,0:T(8,128)(2,1)} %param.10) | copy-start | bytes 1572868
  3.1 44.7 %all-to-all-start = ((bf16[64,16,512]{2,1,0:T(8,128)(2,1)}), bf16[64,16,512]{2,1,0:T(8,128)(2,1)S(1)}, u32[]{:S(2)}, u32[]{:S(2)}) async-start(bf16[64,16,512]{2,1,0:T(8,128)(2,1)} %bitcast), calls=%async_computation | async-start | bytes 2097152 | tf_op jit(solution)/shard_map/all_to_all | solution.py:38
  21.9 18.6 %collective-permute-start = (bf16[2,16,512]{2,1,0:T(8,128)(2,1)S(1)}, bf16[2,16,512]{2,1,0:T(8,128)(2,1)S(1)}, u32[]{:S(2)}, u32[]{:S(2)}) collective-permute-start(bf16[2,16,512]{2,1,0:T(8,128)(2,1)S(1)} %pad_maximum_fusion.18), channel_id=1, source_target_pairs={{0,0},{1,8},{2,16},{3,24},{4,32},{5,40},{6,48},{7,56},{8,64},{9,72... | collective-permute-start | bytes 98312 | tf_op jit(solution)/shard_map/ppermute | solution.py:34
  54.0 14.0 %all-to-all-start.1 = ((bf16[8,16,768]{2,1,0:T(8,128)(2,1)}), bf16[8,16,768]{2,1,0:T(8,128)(2,1)S(1)}, u32[]{:S(2)}, u32[]{:S(2)}) async-start(bf16[8,16,768]{2,1,0:T(8,128)(2,1)} %fusion.16), calls=%async_computation.1 | async-start | bytes 393216 | tf_op jit(solution)/shard_map/all_to_all | solution.py:68
  69.1 44.1 %copy-start.2 = (bf16[128,1024]{1,0:T(8,128)(2,1)S(1)}, bf16[128,1024]{1,0:T(8,128)(2,1)}, u32[]{:S(2)}) copy-start(bf16[128,1024]{1,0:T(8,128)(2,1)} %param.7) | copy-start | bytes 786436
  69.1 36.1 %all-to-all-start.4 = ((bf16[64,16,512]{2,1,0:T(8,128)(2,1)}), bf16[64,16,512]{2,1,0:T(8,128)(2,1)S(1)}, u32[]{:S(2)}, u32[]{:S(2)}) async-start(bf16[64,16,512]{2,1,0:T(8,128)(2,1)} %broadcast_in_dim.18), calls=%async_computation.4 | async-start | bytes 2097152 | tf_op jit(solution)/shard_map/all_to_all | solution.py:27
  105.2 20.5 %all-to-all-start.2 = ((bf16[64,16,128]{2,1,0:T(8,128)(2,1)}), bf16[64,16,128]{2,1,0:T(8,128)(2,1)S(1)}, u32[]{:S(2)}, u32[]{:S(2)}) async-start(bf16[64,16,128]{2,1,0:T(8,128)(2,1)} %pad_maximum_fusion), calls=%async_computation.2 | async-start | bytes 524288 | tf_op jit(solution)/shard_map/all_to_all | solution.py:75
  125.7 13.3 %all-to-all-start.5 = ((f32[8,16,512]{2,1,0:T(8,128)}), f32[8,16,512]{2,1,0:T(8,128)S(1)}, u32[]{:S(2)}, u32[]{:S(2)}) async-start(f32[8,16,512]{2,1,0:T(8,128)} %bitcast.22), calls=%async_computation.5 | async-start | bytes 524288 | tf_op jit(solution)/shard_map/all_to_all | solution.py:78
  132.6 14.9 %collective-permute-start.1 = (bf16[16,512]{1,0:T(8,128)(2,1)S(1)}, bf16[16,512]{1,0:T(8,128)(2,1)S(1)}, u32[]{:S(2)}, u32[]{:S(2)}) collective-permute-start(bf16[16,512]{1,0:T(8,128)(2,1)S(1)} %fusion.8), channel_id=1, source_target_pairs={{0,0},{8,1},{16,2},{24,3},{32,4},{40,5},{48,6},{56,7},{64,8},{72,9... | collective-permute-start | bytes 49160 | tf_op jit(solution)/shard_map/ppermute | solution.py:81
  139.6 18.6 %all-to-all-start.3 = ((bf16[64,8,128]{2,1,0:T(8,128)(2,1)}), bf16[64,8,128]{2,1,0:T(8,128)(2,1)S(1)}, u32[]{:S(2)}, u32[]{:S(2)}) async-start(bf16[64,8,128]{2,1,0:T(8,128)(2,1)} %broadcast_in_dim.17), calls=%async_computation.3 | async-start | bytes 262144 | tf_op jit(solution)/shard_map/all_to_all | solution.py:27

commit v2 on v0

v2 whole, which is shorter than its diff:
```python
import jax
import jax.numpy as jnp
from jax import lax
from jax.experimental import pallas as pl
from jax.experimental.pallas import tpu as pltpu
from jax.sharding import PartitionSpec as P


BF = jnp.bfloat16
F32 = jnp.float32
ALL = ("rows", "rep")


def place(u, v, p):
    z, y = (v, u) if p % 2 == 0 else (u, v)
    return (8 * z + y) * 8 + p


E8 = range(8)
ALONG_U = [[place(u, v, p) for u in E8] for v in E8 for p in E8]
ALONG_V = [[place(u, v, p) for v in E8] for u in E8 for p in E8]
ALONG_X = [[r * 8 + 2 * x + c for x in range(4)] for r in range(64) for c in range(2)]
OUT = [((8 * z + y) * 8 + t, place(t, y, z)) for z in E8 for y in E8 for t in E8]
BACK = [(b, a) for a, b in OUT]
CORE = [(i, i ^ 1) for i in range(512)]


def dot(a, b, ca, cb):
    return lax.dot_general(a, b, (((ca,), (cb,)), ((), ())), preferred_element_type=F32)


def trade(x, groups):
    return lax.all_to_all(x, ALL, 0, 0, axis_index_groups=groups)


def call(body, outs, *args, scalar=None):
    specs = [pl.BlockSpec(memory_space=pltpu.VMEM)] * len(args)
    if scalar is not None:
        args = (scalar,) + args
        specs = [pl.BlockSpec(memory_space=pltpu.SMEM)] + specs
    return pl.pallas_call(
        body,
        out_shape=[jax.ShapeDtypeStruct(s, d) for s, d in outs],
        in_specs=specs,
        out_specs=[pl.BlockSpec(memory_space=pltpu.VMEM)] * len(outs),
        compiler_params=pltpu.CompilerParams(vmem_limit_bytes=40 * 1024 * 1024),
    )(*args)


def left_half():
    return lax.broadcasted_iota(jnp.int32, (1, 128), 1) < 64


def update(c_ref, got, gain_ref, w_in_ref, w_out_ref, moved, out_ref, send, gain_part):
    summed = got[0]
    for i in range(1, 8):
        summed = summed + got[i]
    gain = gain_ref[...]
    w_in, w_out = w_in_ref[...], w_out_ref[...]
    cot = moved[1]
    scale = lax.rsqrt(jnp.mean(summed * summed, axis=-1, keepdims=True) + 1e-05)
    normed = summed * scale
    lifted = (normed * gain).astype(BF)
    pre = dot(lifted, w_in, 1, 0)
    grad_hidden = dot(cot, w_out, 1, 1)
    sigma = jax.nn.sigmoid(pre)
    hidden = (pre * sigma).astype(BF)
    grad_pre = (grad_hidden * sigma * (1.0 + pre * (1.0 - sigma))).astype(BF)
    grad_lifted = dot(grad_pre, w_in, 1, 1)
    out_ref[...] = (moved[0].astype(F32) + dot(hidden, w_out, 1, 0)).astype(BF)
    gain_row = jnp.sum(grad_lifted * normed, axis=0, keepdims=True)
    gain_part[...] = jnp.zeros_like(gain_part)
    for j in range(4):
        gain_part[j : j + 1, :] = gain_row[:, 128 * j : 128 * j + 128]
    grad_normed = grad_lifted * gain
    grad_summed = (
        scale * (grad_normed - normed * jnp.mean(grad_normed * normed, axis=-1, keepdims=True))
    ).astype(BF)
    for u in E8:
        send[u, :, 0:512] = grad_summed
    left = left_half()
    first = c_ref[0] == 0

    def pairs(a, b):
        a, b = a.astype(F32), b.astype(F32)
        blocks = []
        for m in range(4):
            one, two = a[:, 128 * m : 128 * m + 128], b[:, 128 * m : 128 * m + 128]
            blocks.append(jnp.where(left, one, pltpu.roll(two, 64, 1)))
            blocks.append(jnp.where(left, pltpu.roll(one, 64, 1), two))
        return blocks

    rows, columns = pairs(lifted, hidden), pairs(grad_pre, cot)
    for k in E8:
        by_v = jnp.where(first, rows[k], columns[k]).astype(BF)
        by_u = jnp.where(first, columns[k], rows[k]).astype(BF)
        for u in E8:
            send[u, :, 512 + 128 * k : 640 + 128 * k] = by_v
        send[k, :, 1536:1664] = by_u


def forward_on(got, send):
    for u in E8:
        field, by_u = got[u, :, 0:512], got[u, :, 1536:1664]
        for v in E8:
            send[v, 16 * u : 16 * u + 16, 0:512] = field
            send[v, 16 * u : 16 * u + 16, 512:640] = got[u, :, 512 + 128 * v : 640 + 128 * v]
            send[v, 16 * u : 16 * u + 16, 640:768] = by_u


def back_and_tile(c_ref, adjacency, got, gain_part, send):
    table = got[...].reshape(1024, 768)
    back = dot(adjacency[...], table[:, 0:512], 1, 0)
    for q in E8:
        for j in range(4):
            send[q, 16 * j : 16 * j + 16, :] = back[16 * q : 16 * q + 16, 128 * j : 128 * j + 128]
    by_v, by_u = table[:, 512:640], table[:, 640:768]
    first = c_ref[0] == 0
    rows = jnp.where(first, by_v, by_u)
    columns = jnp.where(first, by_u, by_v)
    tile = dot(rows, columns, 0, 0)
    tile = jnp.where(left_half(), tile[0:64], tile[64:128])
    part = gain_part[...]
    for q in E8:
        send[q, 64:72, :] = tile[8 * q : 8 * q + 8]
        send[q, 72:80, :] = part


def add_up(p_ref, got, cotangent, grad, send):
    total = got[0]
    for i in range(1, 8):
        total = total + got[i]
    own = cotangent[pl.ds(pl.multiple_of(p_ref[0] * 16, 16), 16), :].astype(F32)
    for j in range(4):
        grad[16 * j : 16 * j + 16, :] = (
            own[:, 128 * j : 128 * j + 128] + total[16 * j : 16 * j + 16]
        ).astype(BF)
    block = total[64:80].astype(BF)
    for u in E8:
        send[u] = block


def pack(got, grad, out, send, gain):
    total = jnp.zeros((8, 128), F32)
    for i in range(32):
        one, two = got[2 * i].astype(F32), got[2 * i + 1].astype(F32)
        total = total + one[8:16] + two[8:16]
        both = jnp.concatenate([one[0:8], two[0:8]], axis=0).astype(BF)
        for x in range(4):
            send[x, 16 * i : 16 * i + 16, :] = both
    gain[...] = total
    grad = grad[...]
    for x in range(4):
        send[x, 512:576, :] = grad
        for j in range(4):
            send[x, 576 + 16 * j : 592 + 16 * j, :] = out[:, 128 * j : 128 * j + 128]


def unpack(c_ref, mine, other, grad_in, grad_out, node_grad, node_out):
    left = left_half()

    def lay(src, c):
        for x in range(4):
            q = 2 * x + c
            for z in E8:
                at = slice(64 * z + 8 * q, 64 * z + 8 * q + 8)
                for m in range(4):
                    if c == 0:
                        both = src[x, 64 * z + 16 * m : 64 * z + 16 * m + 16, :].astype(F32)
                        even, odd = both[0:8], both[8:16]
                    else:
                        k, half = 8 * (z // 2) * 2, 8 * (z % 2)
                        even = src[x, 128 * m + k : 128 * m + k + 16, :].astype(F32)[half : half + 8]
                        odd = src[x, 128 * m + 64 + k : 128 * m + 64 + k + 16, :].astype(F32)[half : half + 8]
                    cols = slice(128 * m, 128 * m + 128)
                    grad_in[at, cols] = jnp.where(left, even, pltpu.roll(odd, 64, 1))
                    grad_out[at, cols] = jnp.where(left, pltpu.roll(even, 64, 1), odd)
            for j in range(4):
                rows, cols = slice(16 * q, 16 * q + 16), slice(128 * j, 128 * j + 128)
                node_grad[rows, cols] = src[x, 512 + 16 * j : 528 + 16 * j, :]
                node_out[rows, cols] = src[x, 576 + 16 * j : 592 + 16 * j, :]

    @pl.when(c_ref[0] == 0)
    def _():
        lay(mine, 0)
        lay(other, 1)

    @pl.when(c_ref[0] == 1)
    def _():
        lay(other, 0)
        lay(mine, 1)


def shards(nodes, adjacency, gain, w_in, w_out, cotangent):
    p = lax.axis_index("rep")
    own = lambda a: lax.dynamic_slice_in_dim(a, p * 16, 16, 0)
    at = p.reshape(1)
    core = (p % 2).reshape(1)
    moved = lax.ppermute(jnp.stack([own(nodes), own(cotangent)]), ALL, OUT)

    part = dot(adjacency, nodes, 0, 0).astype(BF).reshape(8, 128, 512)
    part = jnp.sum(trade(part, ALONG_V).astype(F32), axis=0).reshape(8, 16, 512)
    got = trade(part, ALONG_U)

    out, send, gain_part = call(
        update,
        [((16, 512), BF), ((8, 16, 1664), BF), ((8, 128), F32)],
        got, gain.reshape(1, 512), w_in, w_out, moved,
        scalar=core,
    )
    out = lax.ppermute(out, ALL, BACK)
    (send,) = call(forward_on, [((8, 128, 768), BF)], trade(send, ALONG_U))
    (send,) = call(
        back_and_tile, [((8, 80, 128), F32)], adjacency, trade(send, ALONG_V), gain_part, scalar=core
    )
    grad, send = call(
        add_up, [((64, 128), BF), ((8, 16, 128), BF)],
        lax.all_to_all(send, "rep", 0, 0), cotangent,
        scalar=at,
    )
    table = trade(send, ALONG_U)
    table = trade(jnp.broadcast_to(table, (8, 8, 16, 128)), ALONG_V).reshape(64, 16, 128)
    send, grad_gain = call(pack, [((4, 640, 128), BF), ((8, 128), F32)], table, grad, out)
    mine = trade(send, ALONG_X)
    other = lax.ppermute(mine, ALL, CORE)
    grad_in, grad_out, node_grad, node_out = call(
        unpack,
        [((512, 512), F32), ((512, 512), F32), ((128, 512), BF), ((128, 512), BF)],
        mine, other,
        scalar=core,
    )
    return (node_out, node_grad, grad_in, grad_out, grad_gain[:4].reshape(512))


def solution(mesh):
    return jax.shard_map(
        shards,
        mesh=mesh,
        in_specs=(P("rows", None), P("rows", "rep"), P(), P(), P(), P("rows", None)),
        out_specs=(P("rows", None), P("rows", None), P(), P(), P()),
        check_vma=False,
    )
```

time: 670 us -> 161 us (0.24)
  waiting for transfers between devices: 508 us -> 8.41 us
  starting transfers between devices: 0.21 us -> 30.7 us
  between operations: 14 us -> 0.79 us
  local copies, waits for them, and re-layouts: 14.5 us -> 2.27 us
  matrix products: 10.9 us -> 1.4 us
    psum x5 -> x0, waiting for transfers between devices: 508 us -> none  [the longest x2 323 us: broadcast(): return lax.psum(jnp.where(mine, x, jnp.zeros_like(x)), axis)]
    psum x1 -> x0, blocking collectives: 114 us -> none  [shards(): lax.psum((grad_w_in, grad_w_out, grad_gain), 'rows')]
    all_to_all x0 -> x6, blocking collectives: none -> 112 us  [the longest x5 92.1 us: trade(): return lax.all_to_all(x, ALL, 0, 0, axis_index_groups=groups)]
    ppermute x0 -> x3, starting transfers between devices: none -> 17.3 us  [the longest x1 6.05 us: shards(): other = lax.ppermute(mine, ALL, CORE)]
    unnamed x49 -> x12, local copies, waits for them, and re-layouts: 14.5 us -> 0.93 us
    all_to_all x0 -> x2, starting transfers between devices: none -> 13.5 us  [trade(): return lax.all_to_all(x, ALL, 0, 0, axis_index_groups=groups)]
    dot_general x22 -> x1, matrix products: 10.9 us -> 1.4 us  [dot(): lax.dot_general(a, b, (((ca,), (cb,)), ((), ())), preferred_element_type=...]
  transfers between devices with their start and end apart: 5 -> 5, of which waited for: 4 -> 5; matrix products, arithmetic and copies ran while one was open for 1% -> 0% of each run, Pallas kernels for 0% -> 0%
where the time goes in v2:
time: 161 us; the launch traced here: 160 us
  blocking collectives  112 us (70%)
  starting transfers between devices  30.7 us (19%)
  waiting for transfers between devices  8.41 us (5%)
  Pallas kernels  3.18 us (2%)
  local copies, waits for them, and re-layouts  2.27 us (1%)
    all_to_all x5, blocking collectives, trade(): return lax.all_to_all(x, ALL, 0, 0, axis_index_groups=groups)  92.1 us
    all_to_all x1, blocking collectives, shards(): lax.all_to_all(send, 'rep', 0, 0)  20 us
    all_to_all x2, starting transfers between devices, trade(): return lax.all_to_all(x, ALL, 0, 0, axis_index_groups=groups)  13.5 us
    ppermute x1, starting transfers between devices, shards(): other = lax.ppermute(mine, ALL, CORE)  6.05 us
    ppermute x1, starting transfers between devices, shards(): moved = lax.ppermute(jnp.stack([own(nodes), own(cotangent)]), ALL, OUT)  5.91 us
    ppermute x1, starting transfers between devices, shards(): out = lax.ppermute(out, ALL, BACK)  5.32 us
    all_to_all x2, waiting for transfers between devices, trade(): return lax.all_to_all(x, ALL, 0, 0, axis_index_groups=groups)  4.77 us
  transfers between devices with their start and end apart: 5, of which 5 were waited for; matrix products, arithmetic and copies ran while one was open for 0% of the time, Pallas kernels for 0%

profile of v2, /device:TPU:1, one launch (start us, length us, event | category | flops | bytes accessed | tf_op | source)
XLA Modules:
  0.0 159.7 jit_solution(4251299702073159495)
XLA Ops:
  0.6 0.9 copy-done
  1.5 1.4 convolution_convert_fusion
  3.0 25.3 %all_to_all.40 = bf16[8,128,512]{2,1,0:T(8,128)(2,1)S(1)} all-to-all(bf16[8,128,512]{2,1,0:T(8,128)(2,1)S(1)} %bitcast.16), channel_id=1, replica_groups={{0,64,128,192,256,320,384,448},{1,9,17,25,33,41,49,57},{2,66,130,194,25..., dimensions={0} | all-to-all | bytes 2097152 | tf_op jit(solution)/shard_map/all_to_all | solution.py:33
  28.3 0.8 convert_reduce_fusion
  29.2 10.0 %all-to-all-start.1 = ((f32[8,16,512]{2,1,0:T(8,128)}), f32[8,16,512]{2,1,0:T(8,128)S(1)}, u32[]{:S(2)}, u32[]{:S(2)}) async-start(f32[8,16,512]{2,1,0:T(8,128)} %bitcast.3), calls=%async_computation.1 | async-start | bytes 524288 | tf_op jit(solution)/shard_map/all_to_all | solution.py:33
  39.3 5.9 %collective-permute-start = (bf16[2,16,512]{2,1,0:T(8,128)(2,1)S(1)}, bf16[2,16,512]{2,1,0:T(8,128)(2,1)S(1)}, u32[]{:S(2)}, u32[]{:S(2)}) collective-permute-start(bf16[2,16,512]{2,1,0:T(8,128)(2,1)S(1)} %pad_maximum_fusion), channel_id=1, source_target_pairs={{0,0},{1,8},{2,16},{3,24},{4,32},{5,40},{6,48},{7,56},{8,64},{9,72... | collective-permute-start | bytes 98312 | tf_op jit(solution)/shard_map/ppermute | solution.py:199
  45.2 1.7 %collective-permute-done.moved = bf16[2,16,512]{2,1,0:T(8,128)(2,1)S(1)} collective-permute-done((bf16[2,16,512]{2,1,0:T(8,128)(2,1)S(1)}, bf16[2,16,512]{2,1,0:T(8,128)(2,1)S(1)}, u32[]{:S(2)}, u32[]{:S(2)}) %collective-permute-start) | collective-permute-done | bytes 32800 | tf_op jit(solution)/shard_map/ppermute | solution.py:199
  46.9 1.7 %all-to-all-done.1.got = f32[8,16,512]{2,1,0:T(8,128)S(1)} async-done(((f32[8,16,512]{2,1,0:T(8,128)}), f32[8,16,512]{2,1,0:T(8,128)S(1)}, u32[]{:S(2)}, u32[]{:S(2)}) %all-to-all-start.1) | async-done | bytes 262176 | tf_op jit(solution)/shard_map/all_to_all | solution.py:33
  48.6 0.7 shard_map.101
  49.3 18.9 %all_to_all.41.got = bf16[8,16,1664]{2,1,0:T(8,128)(2,1)S(1)} all-to-all(bf16[8,16,1664]{2,1,0:T(8,128)(2,1)S(1)} %get-tuple-element.16), channel_id=1, replica_groups={{0,8,16,24,32,40,48,56},{1,65,129,193,257,321,385,449},{2,10,18,26,34,4..., dimensions={0} | all-to-all | bytes 851968 | tf_op jit(solution)/shard_map/all_to_all | solution.py:33
  68.3 27.2 %all_to_all.42.got = bf16[8,128,768]{2,1,0:T(8,128)(2,1)S(1)} all-to-all(bf16[8,128,768]{2,1,0:T(8,128)(2,1)S(1)} %shard_map.102), channel_id=1, replica_groups={{0,64,128,192,256,320,384,448},{1,9,17,25,33,41,49,57},{2,66,130,194,25..., dimensions={0} | all-to-all | bytes 3145728 | tf_op jit(solution)/shard_map/all_to_all | solution.py:33
  95.5 0.4 shard_map.103
  95.9 20.0 %all_to_all.43.got = f32[8,80,128]{2,1,0:T(8,128)S(1)} all-to-all(f32[8,80,128]{2,1,0:T(8,128)S(1)} %shard_map.103), channel_id=1, replica_groups=mesh['rows'=64,'rep'=8] {'rep'}, dimensions={0} | all-to-all | bytes 655360 | tf_op jit(solution)/shard_map/all_to_all | solution.py:218
  116.0 9.2 %all_to_all.44 = bf16[8,16,128]{2,1,0:T(8,128)(2,1)S(1)} all-to-all(bf16[8,16,128]{2,1,0:T(8,128)(2,1)S(1)} %get-tuple-element.18), channel_id=1, replica_groups={{0,8,16,24,32,40,48,56},{1,65,129,193,257,321,385,449},{2,10,18,26,34,4..., dimensions={0} | all-to-all | bytes 65536 | tf_op jit(solution)/shard_map/all_to_all | solution.py:33
  125.2 0.7 broadcast_in_dim.3
  125.9 3.4 %all-to-all-start.6 = ((bf16[8,8,16,128]{3,2,1,0:T(8,128)(2,1)}), bf16[8,8,16,128]{3,2,1,0:T(8,128)(2,1)S(1)}, u32[]{:S(2)}, u32[]{:S(2)}) async-start(bf16[8,8,16,128]{3,2,1,0:T(8,128)(2,1)} %broadcast_in_dim.3), calls=%async_computation.6 | async-start | bytes 524288 | tf_op jit(solution)/shard_map/all_to_all | solution.py:33
  129.4 5.3 %collective-permute-start.1 = (bf16[16,512]{1,0:T(8,128)(2,1)S(1)}, bf16[16,512]{1,0:T(8,128)(2,1)S(1)}, u32[]{:S(2)}, u32[]{:S(2)}) collective-permute-start(bf16[16,512]{1,0:T(8,128)(2,1)S(1)} %get-tuple-element.20), channel_id=1, source_target_pairs={{0,0},{8,1},{16,2},{24,3},{32,4},{40,5},{48,6},{56,7},{64,8},{72,9... | collective-permute-start | bytes 49160 | tf_op jit(solution)/shard_map/ppermute | solution.py:211
  134.7 0.8 collective-permute-done.1.out
  135.5 3.1 %all-to-all-done.6 = bf16[8,8,16,128]{3,2,1,0:T(8,128)(2,1)S(1)} async-done(((bf16[8,8,16,128]{3,2,1,0:T(8,128)(2,1)}), bf16[8,8,16,128]{3,2,1,0:T(8,128)(2,1)S(1)}, u32[]{:S(2)}, u32[]{:S(2)}) %all-to-all-start.6) | async-done | bytes 262176 | tf_op jit(solution)/shard_map/all_to_all | solution.py:33
  138.7 11.4 %all_to_all.45.mine = bf16[4,640,128]{2,1,0:T(8,128)(2,1)S(1)} all-to-all(bf16[4,640,128]{2,1,0:T(8,128)(2,1)S(1)} %get-tuple-element.21), channel_id=1, replica_groups={{0,2,4,6},{1,3,5,7},{8,10,12,14},{9,11,13,15},{16,18,20,22},{17,19,21,2..., dimensions={0} | all-to-all | bytes 1310720 | tf_op jit(solution)/shard_map/all_to_all | solution.py:33
  150.1 6.0 %collective-permute-start.2 = (bf16[4,640,128]{2,1,0:T(8,128)(2,1)S(1)}, bf16[4,640,128]{2,1,0:T(8,128)(2,1)S(1)}, u32[]{:S(2)}, u32[]{:S(2)}) collective-permute-start(bf16[4,640,128]{2,1,0:T(8,128)(2,1)S(1)} %all_to_all.45.mine), channel_id=1, source_target_pairs={{0,1},{1,0},{2,3},{3,2},{4,5},{5,4},{6,7},{7,6},{8,9},{9,8},{10,11... | collective-permute-start | bytes 1966088 | tf_op jit(solution)/shard_map/ppermute | solution.py:225
  156.2 0.6 slice_bitcast_fusion
  156.8 1.1 collective-permute-done.2.other
  157.9 1.8 %shard_map.106 = (f32[512,512]{1,0:T(8,128)}, f32[512,512]{1,0:T(8,128)}, bf16[128,512]{1,0:T(8,128)(2,1)}, bf16[128,512]{1,0:T(8,128)(2,1)}) custom-call(s32[1]{0:T(128)} %bitcast.c_ref, bf16[4,640,128]{2,1,0:T(8,128)(2,1)S(1)} %all_to_all.45.mine, bf16[4,640,128]{2,1,0:T(8,128)(2,1)S(1)} %collective-permute-done.2.other), custom_call_target="tpu_custom_call" | custom-call | tf_op jit(solution)/shard_map/pallas_call | solution.py:41
  (17 shorter events, 0.3 us)
Async XLA Ops:
  0.6 0.9 copy-start
  2.9 36.3 %copy-start.4 = (bf16[128,512]{1,0:T(8,128)(2,1)S(1)}, bf16[128,512]{1,0:T(8,128)(2,1)}, u32[]{:S(2)}) copy-start(bf16[128,512]{1,0:T(8,128)(2,1)} %cotangent.1) | copy-start | bytes 393220
  3.0 45.6 %copy-start.2 = (bf16[512,512]{1,0:T(8,128)(2,1)S(1)}, bf16[512,512]{1,0:T(8,128)(2,1)}, u32[]{:S(2)}) copy-start(bf16[512,512]{1,0:T(8,128)(2,1)} %w_in_ref.1) | copy-start | bytes 1572868
  3.0 45.6 %copy-start.3 = (bf16[512,512]{1,0:T(8,128)(2,1)S(1)}, bf16[512,512]{1,0:T(8,128)(2,1)}, u32[]{:S(2)}) copy-start(bf16[512,512]{1,0:T(8,128)(2,1)} %w_out_ref.1) | copy-start | bytes 1572868
  3.0 45.6 %copy-start.5 = (f32[512]{0:T(512)S(1)}, f32[512]{0:T(512)}, u32[]{:S(2)}) copy-start(f32[512]{0:T(512)} %param.8) | copy-start | bytes 6148
  29.2 19.4 %all-to-all-start.1 = ((f32[8,16,512]{2,1,0:T(8,128)}), f32[8,16,512]{2,1,0:T(8,128)S(1)}, u32[]{:S(2)}, u32[]{:S(2)}) async-start(f32[8,16,512]{2,1,0:T(8,128)} %bitcast.3), calls=%async_computation.1 | async-start | bytes 524288 | tf_op jit(solution)/shard_map/all_to_all | solution.py:33
  39.3 7.6 %collective-permute-start = (bf16[2,16,512]{2,1,0:T(8,128)(2,1)S(1)}, bf16[2,16,512]{2,1,0:T(8,128)(2,1)S(1)}, u32[]{:S(2)}, u32[]{:S(2)}) collective-permute-start(bf16[2,16,512]{2,1,0:T(8,128)(2,1)S(1)} %pad_maximum_fusion), channel_id=1, source_target_pairs={{0,0},{1,8},{2,16},{3,24},{4,32},{5,40},{6,48},{7,56},{8,64},{9,72... | collective-permute-start | bytes 98312 | tf_op jit(solution)/shard_map/ppermute | solution.py:199
  68.3 27.2 %copy-start.1 = (bf16[128,1024]{1,0:T(8,128)(2,1)S(1)}, bf16[128,1024]{1,0:T(8,128)(2,1)}, u32[]{:S(2)}) copy-start(bf16[128,1024]{1,0:T(8,128)(2,1)} %adjacency.1) | copy-start | bytes 786436
  125.9 12.7 %all-to-all-start.6 = ((bf16[8,8,16,128]{3,2,1,0:T(8,128)(2,1)}), bf16[8,8,16,128]{3,2,1,0:T(8,128)(2,1)S(1)}, u32[]{:S(2)}, u32[]{:S(2)}) async-start(bf16[8,8,16,128]{3,2,1,0:T(8,128)(2,1)} %broadcast_in_dim.3), calls=%async_computation.6 | async-start | bytes 524288 | tf_op jit(solution)/shard_map/all_to_all | solution.py:33
  129.4 6.2 %collective-permute-start.1 = (bf16[16,512]{1,0:T(8,128)(2,1)S(1)}, bf16[16,512]{1,0:T(8,128)(2,1)S(1)}, u32[]{:S(2)}, u32[]{:S(2)}) collective-permute-start(bf16[16,512]{1,0:T(8,128)(2,1)S(1)} %get-tuple-element.20), channel_id=1, source_target_pairs={{0,0},{8,1},{16,2},{24,3},{32,4},{40,5},{48,6},{56,7},{64,8},{72,9... | collective-permute-start | bytes 49160 | tf_op jit(solution)/shard_map/ppermute | solution.py:211
  150.1 7.8 %collective-permute-start.2 = (bf16[4,640,128]{2,1,0:T(8,128)(2,1)S(1)}, bf16[4,640,128]{2,1,0:T(8,128)(2,1)S(1)}, u32[]{:S(2)}, u32[]{:S(2)}) collective-permute-start(bf16[4,640,128]{2,1,0:T(8,128)(2,1)S(1)} %all_to_all.45.mine), channel_id=1, source_target_pairs={{0,1},{1,0},{2,3},{3,2},{4,5},{5,4},{6,7},{7,6},{8,9},{9,8},{10,11... | collective-permute-start | bytes 1966088 | tf_op jit(solution)/shard_map/ppermute | solution.py:225

commit v3 on v2

v3 whole, which is shorter than its diff:
```python
import jax
import jax.numpy as jnp
from jax import lax
from jax.experimental import pallas as pl
from jax.experimental.pallas import tpu as pltpu
from jax.sharding import PartitionSpec as P


BF = jnp.bfloat16
F32 = jnp.float32
ALL = ("rows", "rep")


def place(u, v, p):
    z, y = (v, u) if p % 2 == 0 else (u, v)
    return (8 * z + y) * 8 + p


E8 = range(8)
ALONG_U = [[place(u, v, p) for u in E8] for v in E8 for p in E8]
ALONG_V = [[place(u, v, p) for v in E8] for u in E8 for p in E8]
ALONG_X = [[r * 8 + 2 * x + c for x in range(4)] for r in range(64) for c in range(2)]
OUT = [((8 * z + y) * 8 + t, place(t, y, z)) for z in E8 for y in E8 for t in E8]
BACK = [(b, a) for a, b in OUT]
CORE = [(i, i ^ 1) for i in range(512)]


def dot(a, b, ca, cb):
    return lax.dot_general(a, b, (((ca,), (cb,)), ((), ())), preferred_element_type=F32)


def trade(x, groups):
    return lax.all_to_all(x, ALL, 0, 0, axis_index_groups=groups)


def call(body, outs, *args, scalar=None, scratch=()):
    specs = [pl.BlockSpec(memory_space=pltpu.VMEM)] * len(args)
    if scalar is not None:
        args = (scalar,) + args
        specs = [pl.BlockSpec(memory_space=pltpu.SMEM)] + specs
    return pl.pallas_call(
        body,
        out_shape=[jax.ShapeDtypeStruct(s, d) for s, d in outs],
        in_specs=specs,
        out_specs=[pl.BlockSpec(memory_space=pltpu.VMEM)] * len(outs),
        scratch_shapes=list(scratch),
        compiler_params=pltpu.CompilerParams(vmem_limit_bytes=40 * 1024 * 1024),
    )(*args)


def left_half():
    return lax.broadcasted_iota(jnp.int32, (1, 128), 1) < 64


def total_of(got):
    total = got[0].astype(F32)
    for i in range(1, 8):
        total = total + got[i].astype(F32)
    return total


def sum_and_copy(got, send):
    total = total_of(got).astype(BF)
    for u in E8:
        send[u] = total


def update(at_ref, got, gain_ref, w_in_ref, w_out_ref, cot_ref, out_ref, send, gain_part, rows, columns):
    summed = total_of(got)
    gain = gain_ref[...]
    w_in, w_out = w_in_ref[...], w_out_ref[...]
    cot = cot_ref[...]
    scale = lax.rsqrt(jnp.mean(summed * summed, axis=-1, keepdims=True) + 1e-05)
    normed = summed * scale
    lifted = (normed * gain).astype(BF)
    pre = dot(lifted, w_in, 1, 0)
    grad_hidden = dot(cot, w_out, 1, 1)
    sigma = jax.nn.sigmoid(pre)
    hidden = (pre * sigma).astype(BF)
    grad_pre = (grad_hidden * sigma * (1.0 + pre * (1.0 - sigma))).astype(BF)
    grad_lifted = dot(grad_pre, w_in, 1, 1)
    out_ref[...] = dot(hidden, w_out, 1, 0).astype(BF)
    gain_row = jnp.sum(grad_lifted * normed, axis=0, keepdims=True) * 0.125
    gain_part[...] = jnp.zeros_like(gain_part)
    for j in range(4):
        gain_part[j : j + 1, :] = gain_row[:, 128 * j : 128 * j + 128]
    grad_normed = grad_lifted * gain
    grad_summed = (
        scale * (grad_normed - normed * jnp.mean(grad_normed * normed, axis=-1, keepdims=True))
    ).astype(BF)
    for v in E8:
        send[v, 0:128, :] = grad_summed
    left = left_half()

    def pairs(a, b, ref):
        a, b = a.astype(F32), b.astype(F32)
        for m in range(4):
            one, two = a[:, 128 * m : 128 * m + 128], b[:, 128 * m : 128 * m + 128]
            ref[2 * m] = jnp.where(left, one, pltpu.roll(two, 64, 1)).astype(BF)
            ref[2 * m + 1] = jnp.where(left, pltpu.roll(one, 64, 1), two).astype(BF)

    pairs(lifted, hidden, rows)
    pairs(grad_pre, cot, columns)
    first, u = at_ref[0] == 0, at_ref[1]
    for k in E8:
        tile = dot(rows[jnp.where(first, k, u)], columns[jnp.where(first, u, k)], 0, 0)
        tile = jnp.where(left, tile[0:64], tile[64:128])
        high = tile.astype(BF)
        low = (tile - high.astype(F32)).astype(BF)
        for j in range(4):
            at = slice(128 * j, 128 * j + 128)
            send[k, 128:144, at] = high[16 * j : 16 * j + 16]
            send[k, 144:160, at] = low[16 * j : 16 * j + 16]


def back_and_tile(adjacency, got, gain_part, send):
    field = got[:, 0:128, :].reshape(1024, 512)
    back = dot(adjacency[...], field, 1, 0)
    for q in E8:
        for j in range(4):
            send[q, 16 * j : 16 * j + 16, :] = back[16 * q : 16 * q + 16, 128 * j : 128 * j + 128]
    tile = jnp.zeros((16, 512), F32)
    for v in E8:
        tile = tile + (got[v, 128:144, :].astype(F32) + got[v, 144:160, :].astype(F32))
    part = gain_part[...]
    for q in E8:
        at = slice(128 * (q // 2), 128 * (q // 2) + 128)
        send[q, 64:72, :] = tile[8 * (q % 2) : 8 * (q % 2) + 8, at]
        send[q, 72:80, :] = part


def add_up(p_ref, got, cotangent, grad, send):
    total = total_of(got)
    own = cotangent[pl.ds(pl.multiple_of(p_ref[0] * 16, 16), 16), :].astype(F32)
    for j in range(4):
        grad[16 * j : 16 * j + 16, :] = (
            own[:, 128 * j : 128 * j + 128] + total[16 * j : 16 * j + 16]
        ).astype(BF)
    block = total[64:80].astype(BF)
    for r in range(64):
        send[r] = block


def pack(got, grad, send, gain):
    total = jnp.zeros((8, 128), F32)
    for i in range(32):
        one, two = got[2 * i].astype(F32), got[2 * i + 1].astype(F32)
        total = total + one[8:16] + two[8:16]
        both = jnp.concatenate([one[0:8], two[0:8]], axis=0).astype(BF)
        for x in range(4):
            send[x, 16 * i : 16 * i + 16, :] = both
    gain[...] = total
    grad = grad[...]
    for x in range(4):
        send[x, 512:576, :] = grad


def unpack(c_ref, mine, other, nodes, change, grad_in, grad_out, node_grad, node_out):
    node_out[...] = (nodes[...].astype(F32) + change[...].astype(F32)).astype(BF)
    left = left_half()

    def lay(src, c):
        for x in range(4):
            q = 2 * x + c
            for z in E8:
                at = slice(64 * z + 8 * q, 64 * z + 8 * q + 8)
                for m in range(4):
                    both = src[x, 64 * z + 16 * m : 64 * z + 16 * m + 16, :].astype(F32)
                    even, odd = both[0:8], both[8:16]
                    cols = slice(128 * m, 128 * m + 128)
                    grad_in[at, cols] = jnp.where(left, even, pltpu.roll(odd, 64, 1))
                    grad_out[at, cols] = jnp.where(left, pltpu.roll(even, 64, 1), odd)
            for j in range(4):
                rows, cols = slice(16 * q, 16 * q + 16), slice(128 * j, 128 * j + 128)
                node_grad[rows, cols] = src[x, 512 + 16 * j : 528 + 16 * j, :]

    @pl.when(c_ref[0] == 0)
    def _():
        lay(mine, 0)
        lay(other, 1)

    @pl.when(c_ref[0] == 1)
    def _():
        lay(other, 0)
        lay(mine, 1)


def shards(nodes, adjacency, gain, w_in, w_out, cotangent):
    r, p = lax.axis_index("rows"), lax.axis_index("rep")
    core = p % 2
    u = jnp.where(core == 0, r % 8, r // 8)
    cot = lax.ppermute(cotangent, ALL, OUT)

    part = dot(adjacency, nodes, 0, 0).astype(BF).reshape(8, 128, 512)
    (part,) = call(sum_and_copy, [((8, 128, 512), BF)], trade(part, ALONG_V))
    got = trade(part, ALONG_U)

    change, send, gain_part = call(
        update,
        [((128, 512), BF), ((8, 160, 512), BF), ((8, 128), F32)],
        got, gain.reshape(1, 512), w_in, w_out, cot,
        scalar=jnp.stack([core, u]),
        scratch=[pltpu.VMEM((8, 128, 128), BF)] * 2,
    )
    change = lax.ppermute(change, ALL, BACK)
    (send,) = call(back_and_tile, [((8, 80, 128), F32)], adjacency, trade(send, ALONG_V), gain_part)
    grad, send = call(
        add_up, [((64, 128), BF), ((64, 16, 128), BF)],
        lax.all_to_all(send, "rep", 0, 0), cotangent,
        scalar=p.reshape(1),
    )
    table = lax.all_to_all(send, "rows", 0, 0)
    send, grad_gain = call(pack, [((4, 576, 128), BF), ((8, 128), F32)], table, grad)
    mine = trade(send, ALONG_X)
    other = lax.ppermute(mine, ALL, CORE)
    grad_in, grad_out, node_grad, node_out = call(
        unpack,
        [((512, 512), F32), ((512, 512), F32), ((128, 512), BF), ((128, 512), BF)],
        mine, other, nodes, change,
        scalar=core.reshape(1),
    )
    return (node_out, node_grad, grad_in, grad_out, grad_gain[:4].reshape(512))


def solution(mesh):
    return jax.shard_map(
        shards,
        mesh=mesh,
        in_specs=(P("rows", None), P("rows", "rep"), P(), P(), P(), P("rows", None)),
        out_specs=(P("rows", None), P("rows", None), P(), P(), P()),
        check_vma=False,
    )
```

time: 161 us -> 163 us (1.012)
  the two profiles are of different devices: /device:TPU:1 before, /device:TPU:18 now
where the time goes in v3:
time: 163 us; the launch traced here: 162 us
  blocking collectives  103 us (63%)
  waiting for transfers between devices  35.3 us (22%)
  starting transfers between devices  16.2 us (10%)
  Pallas kernels  5.01 us (3%)
    all_to_all x3, blocking collectives, trade(): return lax.all_to_all(x, ALL, 0, 0, axis_index_groups=groups)  71 us
    all_to_all x1, blocking collectives, shards(): table = lax.all_to_all(send, 'rows', 0, 0)  19.1 us
    ppermute x1, waiting for transfers between devices, shards(): change = lax.ppermute(change, ALL, BACK)  17.5 us
    ppermute x1, waiting for transfers between devices, shards(): cot = lax.ppermute(cotangent, ALL, OUT)  16.6 us
    all_to_all x1, blocking collectives, shards(): lax.all_to_all(send, 'rep', 0, 0)  12.8 us
    all_to_all x1, starting transfers between devices, trade(): return lax.all_to_all(x, ALL, 0, 0, axis_index_groups=groups)  7.57 us
    pallas_call x6, Pallas kernels, call(): pl.pallas_call(body, out_shape=[jax.ShapeDtypeStruct(s, d) for s, d in ou...  5.01 us
    ppermute x1, starting transfers between devices, shards(): change = lax.ppermute(change, ALL, BACK)  4.64 us
  transfers between devices with their start and end apart: 4, of which 3 were waited for; matrix products, arithmetic and copies ran while one was open for 0% of the time, Pallas kernels for 0%

profile of v3, /device:TPU:18, one launch (start us, length us, event | category | flops | bytes accessed | tf_op | source)
XLA Modules:
  0.0 162.2 jit_solution(10030000861680080697)
XLA Ops:
  0.6 1.4 convolution_convert_fusion
  2.1 29.0 %all_to_all.30.got = bf16[8,128,512]{2,1,0:T(8,128)(2,1)S(1)} all-to-all(bf16[8,128,512]{2,1,0:T(8,128)(2,1)S(1)} %bitcast.10), channel_id=1, replica_groups={{0,64,128,192,256,320,384,448},{1,9,17,25,33,41,49,57},{2,66,130,194,25..., dimensions={0} | all-to-all | bytes 2097152 | tf_op jit(solution)/shard_map/all_to_all | solution.py:33
  31.1 1.1 shard_map.101
  32.2 7.6 %all-to-all-start.1 = ((bf16[8,128,512]{2,1,0:T(8,128)(2,1)}), bf16[8,128,512]{2,1,0:T(8,128)(2,1)S(1)}, u32[]{:S(2)}, u32[]{:S(2)}) async-start(bf16[8,128,512]{2,1,0:T(8,128)(2,1)} %shard_map.101), calls=%async_computation.1 | async-start | bytes 2097152 | tf_op jit(solution)/shard_map/all_to_all | solution.py:33
  39.8 2.1 %collective-permute-start = (bf16[128,512]{1,0:T(8,128)(2,1)S(1)}, bf16[128,512]{1,0:T(8,128)(2,1)S(1)}, u32[]{:S(2)}, u32[]{:S(2)}) collective-permute-start(bf16[128,512]{1,0:T(8,128)(2,1)S(1)} %copy-done.4), channel_id=1, source_target_pairs={{0,0},{1,8},{2,16},{3,24},{4,32},{5,40},{6,48},{7,56},{8,64},{9,72... | collective-permute-start | bytes 393224 | tf_op jit(solution)/shard_map/ppermute | solution.py:192
  41.9 0.1 pad_add_fusion.at_ref
  42.0 16.6 %collective-permute-done.cot_ref = bf16[128,512]{1,0:T(8,128)(2,1)S(1)} collective-permute-done((bf16[128,512]{1,0:T(8,128)(2,1)S(1)}, bf16[128,512]{1,0:T(8,128)(2,1)S(1)}, u32[]{:S(2)}, u32[]{:S(2)}) %collective-permute-start) | collective-permute-done | bytes 131104 | tf_op jit(solution)/shard_map/ppermute | solution.py:192
  58.6 1.2 all-to-all-done.1.got
  59.8 0.0 copy-done.1
  59.8 1.6 shard_map.102
  61.4 0.0 copy-start
  61.4 31.1 %all_to_all.31.got = bf16[8,160,512]{2,1,0:T(8,128)(2,1)S(1)} all-to-all(bf16[8,160,512]{2,1,0:T(8,128)(2,1)S(1)} %get-tuple-element.16), channel_id=1, replica_groups={{0,64,128,192,256,320,384,448},{1,9,17,25,33,41,49,57},{2,66,130,194,25..., dimensions={0} | all-to-all | bytes 2621440 | tf_op jit(solution)/shard_map/all_to_all | solution.py:33
  92.6 0.0 copy-done
  92.6 0.3 shard_map.103
  92.9 12.8 %all_to_all.32.got = f32[8,80,128]{2,1,0:T(8,128)S(1)} all-to-all(f32[8,80,128]{2,1,0:T(8,128)S(1)} %shard_map.103), channel_id=1, replica_groups=mesh['rows'=64,'rep'=8] {'rep'}, dimensions={0} | all-to-all | bytes 655360 | tf_op jit(solution)/shard_map/all_to_all | solution.py:209
  105.7 19.1 %all_to_all.33.got = bf16[64,16,128]{2,1,0:T(8,128)(2,1)S(1)} all-to-all(bf16[64,16,128]{2,1,0:T(8,128)(2,1)S(1)} %get-tuple-element.18), channel_id=1, replica_groups=mesh['rows'=64,'rep'=8] {'rows'}, dimensions={0} | all-to-all | bytes 524288 | tf_op jit(solution)/shard_map/all_to_all | solution.py:212
  124.8 0.1 shard_map.105
  124.9 10.8 %all_to_all.34.mine = bf16[4,576,128]{2,1,0:T(8,128)(2,1)S(1)} all-to-all(bf16[4,576,128]{2,1,0:T(8,128)(2,1)S(1)} %get-tuple-element.20), channel_id=1, replica_groups={{0,2,4,6},{1,3,5,7},{8,10,12,14},{9,11,13,15},{16,18,20,22},{17,19,21,2..., dimensions={0} | all-to-all | bytes 1179648 | tf_op jit(solution)/shard_map/all_to_all | solution.py:33
  135.7 1.9 %collective-permute-start.1 = (bf16[4,576,128]{2,1,0:T(8,128)(2,1)S(1)}, bf16[4,576,128]{2,1,0:T(8,128)(2,1)S(1)}, u32[]{:S(2)}, u32[]{:S(2)}) collective-permute-start(bf16[4,576,128]{2,1,0:T(8,128)(2,1)S(1)} %all_to_all.34.mine), channel_id=1, source_target_pairs={{0,1},{1,0},{2,3},{3,2},{4,5},{5,4},{6,7},{7,6},{8,9},{9,8},{10,11... | collective-permute-start | bytes 1769480 | tf_op jit(solution)/shard_map/ppermute | solution.py:215
  137.6 4.6 %collective-permute-start.2 = (bf16[128,512]{1,0:T(8,128)(2,1)S(1)}, bf16[128,512]{1,0:T(8,128)(2,1)S(1)}, u32[]{:S(2)}, u32[]{:S(2)}) collective-permute-start(bf16[128,512]{1,0:T(8,128)(2,1)S(1)} %get-tuple-element.21), channel_id=1, source_target_pairs={{0,0},{8,1},{16,2},{24,3},{32,4},{40,5},{48,6},{56,7},{64,8},{72,9... | collective-permute-start | bytes 393224 | tf_op jit(solution)/shard_map/ppermute | solution.py:205
  142.3 0.6 slice_bitcast_fusion
  142.9 17.5 %collective-permute-done.2.change = bf16[128,512]{1,0:T(8,128)(2,1)S(1)} collective-permute-done((bf16[128,512]{1,0:T(8,128)(2,1)S(1)}, bf16[128,512]{1,0:T(8,128)(2,1)S(1)}, u32[]{:S(2)}, u32[]{:S(2)}) %collective-permute-start.2) | collective-permute-done | bytes 131104 | tf_op jit(solution)/shard_map/ppermute | solution.py:205
  160.4 0.0 collective-permute-done.1.other
  160.4 1.8 %shard_map.106 = (f32[512,512]{1,0:T(8,128)}, f32[512,512]{1,0:T(8,128)}, bf16[128,512]{1,0:T(8,128)(2,1)}, bf16[128,512]{1,0:T(8,128)(2,1)}) custom-call(s32[1]{0:T(128)} %bitcast.c_ref, bf16[4,576,128]{2,1,0:T(8,128)(2,1)S(1)} %all_to_all.34.mine, bf16[4,576,128]{2,1,0:T(8,128)(2,1)S(1)} %collective-permute-done.1.other, bf16[128,512]{1,0:T(8,128)(2,1)S(1)} %copy-done.3, ...), custom_call_target="tpu_custom_call" | custom-call | tf_op jit(solution)/shard_map/pallas_call | solution.py:41
  (10 shorter events, 0.1 us)
Async XLA Ops:
  32.2 7.6 %copy-start.4 = (bf16[128,512]{1,0:T(8,128)(2,1)S(1)}, bf16[128,512]{1,0:T(8,128)(2,1)}, u32[]{:S(2)}) copy-start(bf16[128,512]{1,0:T(8,128)(2,1)} %cotangent.1) | copy-start | bytes 393220
  32.2 27.6 %copy-start.1 = (bf16[512,512]{1,0:T(8,128)(2,1)S(1)}, bf16[512,512]{1,0:T(8,128)(2,1)}, u32[]{:S(2)}) copy-start(bf16[512,512]{1,0:T(8,128)(2,1)} %w_in_ref.1) | copy-start | bytes 1572868
  32.2 27.6 %copy-start.2 = (bf16[512,512]{1,0:T(8,128)(2,1)S(1)}, bf16[512,512]{1,0:T(8,128)(2,1)}, u32[]{:S(2)}) copy-start(bf16[512,512]{1,0:T(8,128)(2,1)} %w_out_ref.1) | copy-start | bytes 1572868
  32.2 27.6 %copy-start.5 = (f32[512]{0:T(512)S(1)}, f32[512]{0:T(512)}, u32[]{:S(2)}) copy-start(f32[512]{0:T(512)} %param.8) | copy-start | bytes 6148
  32.2 27.6 %all-to-all-start.1 = ((bf16[8,128,512]{2,1,0:T(8,128)(2,1)}), bf16[8,128,512]{2,1,0:T(8,128)(2,1)S(1)}, u32[]{:S(2)}, u32[]{:S(2)}) async-start(bf16[8,128,512]{2,1,0:T(8,128)(2,1)} %shard_map.101), calls=%async_computation.1 | async-start | bytes 2097152 | tf_op jit(solution)/shard_map/all_to_all | solution.py:33
  39.8 18.8 %collective-permute-start = (bf16[128,512]{1,0:T(8,128)(2,1)S(1)}, bf16[128,512]{1,0:T(8,128)(2,1)S(1)}, u32[]{:S(2)}, u32[]{:S(2)}) collective-permute-start(bf16[128,512]{1,0:T(8,128)(2,1)S(1)} %copy-done.4), channel_id=1, source_target_pairs={{0,0},{1,8},{2,16},{3,24},{4,32},{5,40},{6,48},{7,56},{8,64},{9,72... | collective-permute-start | bytes 393224 | tf_op jit(solution)/shard_map/ppermute | solution.py:192
  61.4 31.1 %copy-start = (bf16[128,1024]{1,0:T(8,128)(2,1)S(1)}, bf16[128,1024]{1,0:T(8,128)(2,1)}, u32[]{:S(2)}) copy-start(bf16[128,1024]{1,0:T(8,128)(2,1)} %adjacency.1) | copy-start | bytes 786436
  105.7 54.7 %copy-start.3 = (bf16[128,512]{1,0:T(8,128)(2,1)S(1)}, bf16[128,512]{1,0:T(8,128)(2,1)}, u32[]{:S(2)}) copy-start(bf16[128,512]{1,0:T(8,128)(2,1)} %nodes.1) | copy-start | bytes 393220
  135.7 24.6 %collective-permute-start.1 = (bf16[4,576,128]{2,1,0:T(8,128)(2,1)S(1)}, bf16[4,576,128]{2,1,0:T(8,128)(2,1)S(1)}, u32[]{:S(2)}, u32[]{:S(2)}) collective-permute-start(bf16[4,576,128]{2,1,0:T(8,128)(2,1)S(1)} %all_to_all.34.mine), channel_id=1, source_target_pairs={{0,1},{1,0},{2,3},{3,2},{4,5},{5,4},{6,7},{7,6},{8,9},{9,8},{10,11... | collective-permute-start | bytes 1769480 | tf_op jit(solution)/shard_map/ppermute | solution.py:215
  137.6 22.7 %collective-permute-start.2 = (bf16[128,512]{1,0:T(8,128)(2,1)S(1)}, bf16[128,512]{1,0:T(8,128)(2,1)S(1)}, u32[]{:S(2)}, u32[]{:S(2)}) collective-permute-start(bf16[128,512]{1,0:T(8,128)(2,1)S(1)} %get-tuple-element.21), channel_id=1, source_target_pairs={{0,0},{8,1},{16,2},{24,3},{32,4},{40,5},{48,6},{56,7},{64,8},{72,9... | collective-permute-start | bytes 393224 | tf_op jit(solution)/shard_map/ppermute | solution.py:205

commit v4 on v3

--- a/solution.py
+++ b/solution.py
@@ -59,17 +59,20 @@
     return total
 
 
-def sum_and_copy(got, send):
-    total = total_of(got).astype(BF)
+def sum_and_copy(got, cot, send):
+    total, piece = total_of(got).astype(BF), cot[...]
     for u in E8:
-        send[u] = total
-
-
-def update(at_ref, got, gain_ref, w_in_ref, w_out_ref, cot_ref, out_ref, send, gain_part, rows, columns):
-    summed = total_of(got)
+        send[u, 0:128, :] = total
+        send[u, 128:144, :] = piece
+
+
+def update(at_ref, got, gain_ref, w_in_ref, w_out_ref, out_ref, send, gain_part, change, rows, columns):
+    summed = got[0, 0:128, :].astype(F32)
+    for i in range(1, 8):
+        summed = summed + got[i, 0:128, :].astype(F32)
     gain = gain_ref[...]
     w_in, w_out = w_in_ref[...], w_out_ref[...]
-    cot = cot_ref[...]
+    cot = got[:, 128:144, :].reshape(128, 512)
     scale = lax.rsqrt(jnp.mean(summed * summed, axis=-1, keepdims=True) + 1e-05)
     normed = summed * scale
     lifted = (normed * gain).astype(BF)
@@ -79,7 +82,8 @@
     hidden = (pre * sigma).astype(BF)
     grad_pre = (grad_hidden * sigma * (1.0 + pre * (1.0 - sigma))).astype(BF)
     grad_lifted = dot(grad_pre, w_in, 1, 1)
-    out_ref[...] = dot(hidden, w_out, 1, 0).astype(BF)
+    change[...] = dot(hidden, w_out, 1, 0).astype(BF)
+    out_ref[...] = change[pl.ds(pl.multiple_of(at_ref[1] * 16, 16), 16), :]
     gain_row = jnp.sum(grad_lifted * normed, axis=0, keepdims=True) * 0.125
     gain_part[...] = jnp.zeros_like(gain_part)
     for j in range(4):
@@ -141,7 +145,7 @@
         send[r] = block
 
 
-def pack(got, grad, send, gain):
+def pack(got, grad, change, send, gain):
     total = jnp.zeros((8, 128), F32)
     for i in range(32):
         one, two = got[2 * i].astype(F32), got[2 * i + 1].astype(F32)
@@ -153,10 +157,11 @@
     grad = grad[...]
     for x in range(4):
         send[x, 512:576, :] = grad
-
-
-def unpack(c_ref, mine, other, nodes, change, grad_in, grad_out, node_grad, node_out):
-    node_out[...] = (nodes[...].astype(F32) + change[...].astype(F32)).astype(BF)
+        for j in range(4):
+            send[x, 576 + 16 * j : 592 + 16 * j, :] = change[:, 128 * j : 128 * j + 128]
+
+
+def unpack(c_ref, mine, other, nodes, grad_in, grad_out, node_grad, node_out):
     left = left_half()
 
     def lay(src, c):
@@ -173,6 +178,8 @@
             for j in range(4):
                 rows, cols = slice(16 * q, 16 * q + 16), slice(128 * j, 128 * j + 128)
                 node_grad[rows, cols] = src[x, 512 + 16 * j : 528 + 16 * j, :]
+                change = src[x, 576 + 16 * j : 592 + 16 * j, :].astype(F32)
+                node_out[rows, cols] = (nodes[rows, cols].astype(F32) + change).astype(BF)
 
     @pl.when(c_ref[0] == 0)
     def _():
@@ -189,18 +196,18 @@
     r, p = lax.axis_index("rows"), lax.axis_index("rep")
     core = p % 2
     u = jnp.where(core == 0, r % 8, r // 8)
-    cot = lax.ppermute(cotangent, ALL, OUT)
+    cot = lax.ppermute(lax.dynamic_slice_in_dim(cotangent, p * 16, 16, 0), ALL, OUT)
 
     part = dot(adjacency, nodes, 0, 0).astype(BF).reshape(8, 128, 512)
-    (part,) = call(sum_and_copy, [((8, 128, 512), BF)], trade(part, ALONG_V))
+    (part,) = call(sum_and_copy, [((8, 144, 512), BF)], trade(part, ALONG_V), cot)
     got = trade(part, ALONG_U)
 
     change, send, gain_part = call(
         update,
-        [((128, 512), BF), ((8, 160, 512), BF), ((8, 128), F32)],
-        got, gain.reshape(1, 512), w_in, w_out, cot,
+        [((16, 512), BF), ((8, 160, 512), BF), ((8, 128), F32)],
+        got, gain.reshape(1, 512), w_in, w_out,
         scalar=jnp.stack([core, u]),
-        scratch=[pltpu.VMEM((8, 128, 128), BF)] * 2,
+        scratch=[pltpu.VMEM((128, 512), BF)] + [pltpu.VMEM((8, 128, 128), BF)] * 2,
     )
     change = lax.ppermute(change, ALL, BACK)
     (send,) = call(back_and_tile, [((8, 80, 128), F32)], adjacency, trade(send, ALONG_V), gain_part)
@@ -210,13 +217,13 @@
         scalar=p.reshape(1),
     )
     table = lax.all_to_all(send, "rows", 0, 0)
-    send, grad_gain = call(pack, [((4, 576, 128), BF), ((8, 128), F32)], table, grad)
+    send, grad_gain = call(pack, [((4, 640, 128), BF), ((8, 128), F32)], table, grad, change)
     mine = trade(send, ALONG_X)
     other = lax.ppermute(mine, ALL, CORE)
     grad_in, grad_out, node_grad, node_out = call(
         unpack,
         [((512, 512), F32), ((512, 512), F32), ((128, 512), BF), ((128, 512), BF)],
-        mine, other, nodes, change,
+        mine, other, nodes,
         scalar=core.reshape(1),
     )
     return (node_out, node_grad, grad_in, grad_out, grad_gain[:4].reshape(512))

time: 163 us -> 140 us (0.86)
  the two profiles are of different devices: /device:TPU:18 before, /device:TPU:1 now
where the time goes in v4:
time: 140 us
  blocking collectives  50.2 us (36%)
  waiting for transfers between devices  41.7 us (30%)
  starting transfers between devices  38.3 us (27%)
  Pallas kernels  5.77 us (4%)
  matrix products  2.41 us (2%)
    all_to_all x2, blocking collectives, trade(): return lax.all_to_all(x, ALL, 0, 0, axis_index_groups=groups)  34.9 us
    all_to_all x2, waiting for transfers between devices, trade(): return lax.all_to_all(x, ALL, 0, 0, axis_index_groups=groups)  19.4 us
    all_to_all x2, starting transfers between devices, trade(): return lax.all_to_all(x, ALL, 0, 0, axis_index_groups=groups)  16.7 us
    all_to_all x1, blocking collectives, shards(): lax.all_to_all(send, 'rep', 0, 0)  15.3 us
    ppermute x1, waiting for transfers between devices, shards(): lax.ppermute(lax.dynamic_slice_in_dim(cotangent, p * 16, 16, 0), ALL, OUT)  12 us
    ppermute x1, starting transfers between devices, shards(): lax.ppermute(lax.dynamic_slice_in_dim(cotangent, p * 16, 16, 0), ALL, OUT)  7.26 us
    ppermute x1, starting transfers between devices, shards(): other = lax.ppermute(mine, ALL, CORE)  6.02 us
    pallas_call x6, Pallas kernels, call(): pl.pallas_call(body, out_shape=[jax.ShapeDtypeStruct(s, d) for s, d in ou...  5.77 us
  transfers between devices with their start and end apart: 6, of which 5 were waited for; matrix products, arithmetic and copies ran while one was open for 0% of the time, Pallas kernels for 0%

profile of v4, /device:TPU:1, one launch (start us, length us, event | category | flops | bytes accessed | tf_op | source)
XLA Modules:
  0.0 139.9 jit_solution(10003185848641804463)
XLA Ops:
  0.6 2.4 %convolution_convert_fusion = bf16[1024,512]{1,0:T(8,128)(2,1)} fusion(bf16[128,1024]{1,0:T(8,128)(2,1)} %adjacency.1, bf16[128,512]{1,0:T(8,128)(2,1)} %nodes.1), kind=kOutput, calls=%fused_computation | convolution fusion | flops 134742016 | bytes 1441792 | tf_op jit(solution)/shard_map/dot_general | solution.py:29
  3.0 7.8 %all-to-all-start = ((bf16[8,128,512]{2,1,0:T(8,128)(2,1)}), bf16[8,128,512]{2,1,0:T(8,128)(2,1)S(1)}, u32[]{:S(2)}, u32[]{:S(2)}) async-start(bf16[8,128,512]{2,1,0:T(8,128)(2,1)} %bitcast.3), calls=%async_computation | async-start | bytes 2097152 | tf_op jit(solution)/shard_map/all_to_all | solution.py:33
  10.8 7.3 %collective-permute-start = (bf16[16,512]{1,0:T(8,128)(2,1)S(1)}, bf16[16,512]{1,0:T(8,128)(2,1)S(1)}, u32[]{:S(2)}, u32[]{:S(2)}) collective-permute-start(bf16[16,512]{1,0:T(8,128)(2,1)S(1)} %constant_dynamic-slice_fusion), channel_id=1, source_target_pairs={{0,0},{1,8},{2,16},{3,24},{4,32},{5,40},{6,48},{7,56},{8,64},{9,72... | collective-permute-start | bytes 49160 | tf_op jit(solution)/shard_map/ppermute | solution.py:199
  18.1 12.0 %collective-permute-done.cot = bf16[16,512]{1,0:T(8,128)(2,1)S(1)} collective-permute-done((bf16[16,512]{1,0:T(8,128)(2,1)S(1)}, bf16[16,512]{1,0:T(8,128)(2,1)S(1)}, u32[]{:S(2)}, u32[]{:S(2)}) %collective-permute-start) | collective-permute-done | bytes 16416 | tf_op jit(solution)/shard_map/ppermute | solution.py:199
  30.1 1.2 shard_map.101
  31.3 8.9 %all-to-all-start.1 = ((bf16[8,144,512]{2,1,0:T(8,128)(2,1)}), bf16[8,144,512]{2,1,0:T(8,128)(2,1)S(1)}, u32[]{:S(2)}, u32[]{:S(2)}) async-start(bf16[8,144,512]{2,1,0:T(8,128)(2,1)} %shard_map.101), calls=%async_computation.1 | async-start | bytes 2359296 | tf_op jit(solution)/shard_map/all_to_all | solution.py:33
  40.2 0.1 pad_add_fusion.at_ref
  40.2 19.4 %all-to-all-done.1.got = bf16[8,144,512]{2,1,0:T(8,128)(2,1)S(1)} async-done(((bf16[8,144,512]{2,1,0:T(8,128)(2,1)}), bf16[8,144,512]{2,1,0:T(8,128)(2,1)S(1)}, u32[]{:S(2)}, u32[]{:S(2)}) %all-to-all-start.1) | async-done | bytes 1179680 | tf_op jit(solution)/shard_map/all_to_all | solution.py:33
  59.7 1.6 %shard_map.102 = (bf16[16,512]{1,0:T(8,128)(2,1)S(1)}, bf16[8,160,512]{2,1,0:T(8,128)(2,1)S(1)}, f32[8,128]{1,0:T(8,128)S(1)}) custom-call(s32[2]{0:T(128)S(1)} %pad_add_fusion.at_ref, bf16[8,144,512]{2,1,0:T(8,128)(2,1)S(1)} %all-to-all-done.1.got, f32[1,512]{1,0:T(1,128)S(1)} %bitcast.9, bf16[512,512]{1,0:T(8,128)(2,1)S(1)} %copy-done.1, ...), custom_call_target="tpu_custom_call" | custom-call | tf_op jit(solution)/shard_map/pallas_call | solution.py:41
  61.3 0.0 copy-start
  61.3 24.8 %all_to_all.30.got = bf16[8,160,512]{2,1,0:T(8,128)(2,1)S(1)} all-to-all(bf16[8,160,512]{2,1,0:T(8,128)(2,1)S(1)} %get-tuple-element.16), channel_id=1, replica_groups={{0,64,128,192,256,320,384,448},{1,9,17,25,33,41,49,57},{2,66,130,194,25..., dimensions={0} | all-to-all | bytes 2621440 | tf_op jit(solution)/shard_map/all_to_all | solution.py:33
  86.1 0.3 shard_map.103
  86.4 15.3 %all_to_all.31.got = f32[8,80,128]{2,1,0:T(8,128)S(1)} all-to-all(f32[8,80,128]{2,1,0:T(8,128)S(1)} %shard_map.103), channel_id=1, replica_groups=mesh['rows'=64,'rep'=8] {'rep'}, dimensions={0} | all-to-all | bytes 655360 | tf_op jit(solution)/shard_map/all_to_all | solution.py:216
  101.8 0.7 shard_map.104
  102.5 4.6 %all-to-all-start.4 = ((bf16[64,16,128]{2,1,0:T(8,128)(2,1)}), bf16[64,16,128]{2,1,0:T(8,128)(2,1)S(1)}, u32[]{:S(2)}, u32[]{:S(2)}) async-start(bf16[64,16,128]{2,1,0:T(8,128)(2,1)} %get-tuple-element.18), calls=%async_computation.4 | async-start | bytes 524288 | tf_op jit(solution)/shard_map/all_to_all | solution.py:219
  107.1 3.8 %collective-permute-start.1 = (bf16[16,512]{1,0:T(8,128)(2,1)S(1)}, bf16[16,512]{1,0:T(8,128)(2,1)S(1)}, u32[]{:S(2)}, u32[]{:S(2)}) collective-permute-start(bf16[16,512]{1,0:T(8,128)(2,1)S(1)} %get-tuple-element.20), channel_id=1, source_target_pairs={{0,0},{8,1},{16,2},{24,3},{32,4},{40,5},{48,6},{56,7},{64,8},{72,9... | collective-permute-start | bytes 49160 | tf_op jit(solution)/shard_map/ppermute | solution.py:212
  110.9 4.4 %collective-permute-done.1.change = bf16[16,512]{1,0:T(8,128)(2,1)S(1)} collective-permute-done((bf16[16,512]{1,0:T(8,128)(2,1)S(1)}, bf16[16,512]{1,0:T(8,128)(2,1)S(1)}, u32[]{:S(2)}, u32[]{:S(2)}) %collective-permute-start.1) | collective-permute-done | bytes 16416 | tf_op jit(solution)/shard_map/ppermute | solution.py:212
  115.3 4.8 %all-to-all-done.4.got = bf16[64,16,128]{2,1,0:T(8,128)(2,1)S(1)} async-done(((bf16[64,16,128]{2,1,0:T(8,128)(2,1)}), bf16[64,16,128]{2,1,0:T(8,128)(2,1)S(1)}, u32[]{:S(2)}, u32[]{:S(2)}) %all-to-all-start.4) | async-done | bytes 262176 | tf_op jit(solution)/shard_map/all_to_all | solution.py:219
  120.1 0.1 shard_map.105
  120.2 10.1 %all_to_all.32.mine = bf16[4,640,128]{2,1,0:T(8,128)(2,1)S(1)} all-to-all(bf16[4,640,128]{2,1,0:T(8,128)(2,1)S(1)} %get-tuple-element.21), channel_id=1, replica_groups={{0,2,4,6},{1,3,5,7},{8,10,12,14},{9,11,13,15},{16,18,20,22},{17,19,21,2..., dimensions={0} | all-to-all | bytes 1310720 | tf_op jit(solution)/shard_map/all_to_all | solution.py:33
  130.3 6.0 %collective-permute-start.2 = (bf16[4,640,128]{2,1,0:T(8,128)(2,1)S(1)}, bf16[4,640,128]{2,1,0:T(8,128)(2,1)S(1)}, u32[]{:S(2)}, u32[]{:S(2)}) collective-permute-start(bf16[4,640,128]{2,1,0:T(8,128)(2,1)S(1)} %all_to_all.32.mine), channel_id=1, source_target_pairs={{0,1},{1,0},{2,3},{3,2},{4,5},{5,4},{6,7},{7,6},{8,9},{9,8},{10,11... | collective-permute-start | bytes 1966088 | tf_op jit(solution)/shard_map/ppermute | solution.py:222
  136.4 0.6 slice_bitcast_fusion
  136.9 1.1 collective-permute-done.2.other
  138.1 1.8 %shard_map.106 = (f32[512,512]{1,0:T(8,128)}, f32[512,512]{1,0:T(8,128)}, bf16[128,512]{1,0:T(8,128)(2,1)}, bf16[128,512]{1,0:T(8,128)(2,1)}) custom-call(s32[1]{0:T(128)} %bitcast.c_ref, bf16[4,640,128]{2,1,0:T(8,128)(2,1)S(1)} %all_to_all.32.mine, bf16[4,640,128]{2,1,0:T(8,128)(2,1)S(1)} %collective-permute-done.2.other, bf16[128,512]{1,0:T(8,128)(2,1)S(1)} %copy-done.3), custom_call_target="tpu_custom_call" | custom-call | tf_op jit(solution)/shard_map/pallas_call | solution.py:41
  (13 shorter events, 0.0 us)
Async XLA Ops:
  3.0 7.8 %copy-start.4 = (bf16[128,512]{1,0:T(8,128)(2,1)S(1)}, bf16[128,512]{1,0:T(8,128)(2,1)}, u32[]{:S(2)}) copy-start(bf16[128,512]{1,0:T(8,128)(2,1)} %cotangent.1) | copy-start | bytes 393220
  3.0 27.0 %all-to-all-start = ((bf16[8,128,512]{2,1,0:T(8,128)(2,1)}), bf16[8,128,512]{2,1,0:T(8,128)(2,1)S(1)}, u32[]{:S(2)}, u32[]{:S(2)}) async-start(bf16[8,128,512]{2,1,0:T(8,128)(2,1)} %bitcast.3), calls=%async_computation | async-start | bytes 2097152 | tf_op jit(solution)/shard_map/all_to_all | solution.py:33
  10.8 19.2 %collective-permute-start = (bf16[16,512]{1,0:T(8,128)(2,1)S(1)}, bf16[16,512]{1,0:T(8,128)(2,1)S(1)}, u32[]{:S(2)}, u32[]{:S(2)}) collective-permute-start(bf16[16,512]{1,0:T(8,128)(2,1)S(1)} %constant_dynamic-slice_fusion), channel_id=1, source_target_pairs={{0,0},{1,8},{2,16},{3,24},{4,32},{5,40},{6,48},{7,56},{8,64},{9,72... | collective-permute-start | bytes 49160 | tf_op jit(solution)/shard_map/ppermute | solution.py:199
  31.3 28.4 %copy-start.1 = (bf16[512,512]{1,0:T(8,128)(2,1)S(1)}, bf16[512,512]{1,0:T(8,128)(2,1)}, u32[]{:S(2)}) copy-start(bf16[512,512]{1,0:T(8,128)(2,1)} %w_in_ref.1) | copy-start | bytes 1572868
  31.3 28.4 %copy-start.2 = (bf16[512,512]{1,0:T(8,128)(2,1)S(1)}, bf16[512,512]{1,0:T(8,128)(2,1)}, u32[]{:S(2)}) copy-start(bf16[512,512]{1,0:T(8,128)(2,1)} %w_out_ref.1) | copy-start | bytes 1572868
  31.3 28.4 %copy-start.5 = (f32[512]{0:T(512)S(1)}, f32[512]{0:T(512)}, u32[]{:S(2)}) copy-start(f32[512]{0:T(512)} %param.8) | copy-start | bytes 6148
  31.3 28.4 %all-to-all-start.1 = ((bf16[8,144,512]{2,1,0:T(8,128)(2,1)}), bf16[8,144,512]{2,1,0:T(8,128)(2,1)S(1)}, u32[]{:S(2)}, u32[]{:S(2)}) async-start(bf16[8,144,512]{2,1,0:T(8,128)(2,1)} %shard_map.101), calls=%async_computation.1 | async-start | bytes 2359296 | tf_op jit(solution)/shard_map/all_to_all | solution.py:33
  61.3 24.8 %copy-start = (bf16[128,1024]{1,0:T(8,128)(2,1)S(1)}, bf16[128,1024]{1,0:T(8,128)(2,1)}, u32[]{:S(2)}) copy-start(bf16[128,1024]{1,0:T(8,128)(2,1)} %adjacency.1) | copy-start | bytes 786436
  101.8 36.3 %copy-start.3 = (bf16[128,512]{1,0:T(8,128)(2,1)S(1)}, bf16[128,512]{1,0:T(8,128)(2,1)}, u32[]{:S(2)}) copy-start(bf16[128,512]{1,0:T(8,128)(2,1)} %nodes.1) | copy-start | bytes 393220
  102.5 17.6 %all-to-all-start.4 = ((bf16[64,16,128]{2,1,0:T(8,128)(2,1)}), bf16[64,16,128]{2,1,0:T(8,128)(2,1)S(1)}, u32[]{:S(2)}, u32[]{:S(2)}) async-start(bf16[64,16,128]{2,1,0:T(8,128)(2,1)} %get-tuple-element.18), calls=%async_computation.4 | async-start | bytes 524288 | tf_op jit(solution)/shard_map/all_to_all | solution.py:219
  107.1 8.1 %collective-permute-start.1 = (bf16[16,512]{1,0:T(8,128)(2,1)S(1)}, bf16[16,512]{1,0:T(8,128)(2,1)S(1)}, u32[]{:S(2)}, u32[]{:S(2)}) collective-permute-start(bf16[16,512]{1,0:T(8,128)(2,1)S(1)} %get-tuple-element.20), channel_id=1, source_target_pairs={{0,0},{8,1},{16,2},{24,3},{32,4},{40,5},{48,6},{56,7},{64,8},{72,9... | collective-permute-start | bytes 49160 | tf_op jit(solution)/shard_map/ppermute | solution.py:212
  130.3 7.7 %collective-permute-start.2 = (bf16[4,640,128]{2,1,0:T(8,128)(2,1)S(1)}, bf16[4,640,128]{2,1,0:T(8,128)(2,1)S(1)}, u32[]{:S(2)}, u32[]{:S(2)}) collective-permute-start(bf16[4,640,128]{2,1,0:T(8,128)(2,1)S(1)} %all_to_all.32.mine), channel_id=1, source_target_pairs={{0,1},{1,0},{2,3},{3,2},{4,5},{5,4},{6,7},{7,6},{8,9},{9,8},{10,11... | collective-permute-start | bytes 1966088 | tf_op jit(solution)/shard_map/ppermute | solution.py:222

commit v5 on v4

--- a/solution.py
+++ b/solution.py
@@ -11,16 +11,16 @@
 ALL = ("rows", "rep")
 
 
-def place(u, v, p):
-    z, y = (v, u) if p % 2 == 0 else (u, v)
+def place(k, e, a, p):
+    z, y = (k, 2 * a + e) if p % 2 == 0 else (2 * a + e, k)
     return (8 * z + y) * 8 + p
 
 
 E8 = range(8)
-ALONG_U = [[place(u, v, p) for u in E8] for v in E8 for p in E8]
-ALONG_V = [[place(u, v, p) for v in E8] for u in E8 for p in E8]
+WIDE = [[place(k, e, a, p) for k in E8 for e in range(2)] for a in range(4) for p in E8]
+NARROW = [[place(k, e, a, p) for a in range(4)] for k in E8 for e in range(2) for p in E8]
 ALONG_X = [[r * 8 + 2 * x + c for x in range(4)] for r in range(64) for c in range(2)]
-OUT = [((8 * z + y) * 8 + t, place(t, y, z)) for z in E8 for y in E8 for t in E8]
+OUT = [((8 * z + y) * 8 + t, place(y, t // 4, t % 4, z)) for z in E8 for y in E8 for t in E8]
 BACK = [(b, a) for a, b in OUT]
 CORE = [(i, i ^ 1) for i in range(512)]
 
@@ -54,25 +54,28 @@
 
 def total_of(got):
     total = got[0].astype(F32)
-    for i in range(1, 8):
+    for i in range(1, got.shape[0]):
         total = total + got[i].astype(F32)
     return total
 
 
 def sum_and_copy(got, cot, send):
-    total, piece = total_of(got).astype(BF), cot[...]
-    for u in E8:
-        send[u, 0:128, :] = total
-        send[u, 128:144, :] = piece
+    total, piece = total_of(got), cot[...]
+    high = total.astype(BF)
+    low = (total - high.astype(F32)).astype(BF)
+    for a in range(4):
+        send[a, 0:64, :] = high
+        send[a, 64:128, :] = low
+        send[a, 128:144, :] = piece
 
 
 def update(at_ref, got, gain_ref, w_in_ref, w_out_ref, out_ref, send, gain_part, change, rows, columns):
-    summed = got[0, 0:128, :].astype(F32)
-    for i in range(1, 8):
-        summed = summed + got[i, 0:128, :].astype(F32)
+    summed = got[0, 0:64, :].astype(F32) + got[0, 64:128, :].astype(F32)
+    for i in range(1, 4):
+        summed = summed + (got[i, 0:64, :].astype(F32) + got[i, 64:128, :].astype(F32))
     gain = gain_ref[...]
     w_in, w_out = w_in_ref[...], w_out_ref[...]
-    cot = got[:, 128:144, :].reshape(128, 512)
+    cot = got[:, 128:144, :].reshape(64, 512)
     scale = lax.rsqrt(jnp.mean(summed * summed, axis=-1, keepdims=True) + 1e-05)
     normed = summed * scale
     lifted = (normed * gain).astype(BF)
@@ -84,7 +87,7 @@
     grad_lifted = dot(grad_pre, w_in, 1, 1)
     change[...] = dot(hidden, w_out, 1, 0).astype(BF)
     out_ref[...] = change[pl.ds(pl.multiple_of(at_ref[1] * 16, 16), 16), :]
-    gain_row = jnp.sum(grad_lifted * normed, axis=0, keepdims=True) * 0.125
+    gain_row = jnp.sum(grad_lifted * normed, axis=0, keepdims=True) * 0.25
     gain_part[...] = jnp.zeros_like(gain_part)
     for j in range(4):
         gain_part[j : j + 1, :] = gain_row[:, 128 * j : 128 * j + 128]
@@ -92,8 +95,8 @@
     grad_summed = (
         scale * (grad_normed - normed * jnp.mean(grad_normed * normed, axis=-1, keepdims=True))
     ).astype(BF)
-    for v in E8:
-        send[v, 0:128, :] = grad_summed
+    for b in range(16):
+        send[b, 0:64, :] = grad_summed
     left = left_half()
 
     def pairs(a, b, ref):
@@ -105,27 +108,25 @@
 
     pairs(lifted, hidden, rows)
     pairs(grad_pre, cot, columns)
-    first, u = at_ref[0] == 0, at_ref[1]
+    first, a = at_ref[0] == 0, at_ref[1]
     for k in E8:
-        tile = dot(rows[jnp.where(first, k, u)], columns[jnp.where(first, u, k)], 0, 0)
-        tile = jnp.where(left, tile[0:64], tile[64:128])
-        high = tile.astype(BF)
-        low = (tile - high.astype(F32)).astype(BF)
-        for j in range(4):
-            at = slice(128 * j, 128 * j + 128)
-            send[k, 128:144, at] = high[16 * j : 16 * j + 16]
-            send[k, 144:160, at] = low[16 * j : 16 * j + 16]
+        for e in range(2):
+            other = 2 * a + e
+            tile = dot(rows[jnp.where(first, k, other)], columns[jnp.where(first, other, k)], 0, 0)
+            tile = jnp.where(left, tile[0:64], tile[64:128]).astype(BF)
+            for j in range(4):
+                send[2 * k + e, 64:80, 128 * j : 128 * j + 128] = tile[16 * j : 16 * j + 16]
 
 
 def back_and_tile(adjacency, got, gain_part, send):
-    field = got[:, 0:128, :].reshape(1024, 512)
+    field = got[:, 0:64, :].reshape(1024, 512)
     back = dot(adjacency[...], field, 1, 0)
     for q in E8:
         for j in range(4):
             send[q, 16 * j : 16 * j + 16, :] = back[16 * q : 16 * q + 16, 128 * j : 128 * j + 128]
     tile = jnp.zeros((16, 512), F32)
-    for v in E8:
-        tile = tile + (got[v, 128:144, :].astype(F32) + got[v, 144:160, :].astype(F32))
+    for b in range(16):
+        tile = tile + got[b, 64:80, :].astype(F32)
     part = gain_part[...]
     for q in E8:
         at = slice(128 * (q // 2), 128 * (q // 2) + 128)
@@ -195,22 +196,22 @@
 def shards(nodes, adjacency, gain, w_in, w_out, cotangent):
     r, p = lax.axis_index("rows"), lax.axis_index("rep")
     core = p % 2
-    u = jnp.where(core == 0, r % 8, r // 8)
+    a = jnp.where(core == 0, r % 8, r // 8) // 2
     cot = lax.ppermute(lax.dynamic_slice_in_dim(cotangent, p * 16, 16, 0), ALL, OUT)
 
-    part = dot(adjacency, nodes, 0, 0).astype(BF).reshape(8, 128, 512)
-    (part,) = call(sum_and_copy, [((8, 144, 512), BF)], trade(part, ALONG_V), cot)
-    got = trade(part, ALONG_U)
+    part = dot(adjacency, nodes, 0, 0).astype(BF).reshape(16, 64, 512)
+    (part,) = call(sum_and_copy, [((4, 144, 512), BF)], trade(part, WIDE), cot)
+    got = trade(part, NARROW)
 
     change, send, gain_part = call(
         update,
-        [((16, 512), BF), ((8, 160, 512), BF), ((8, 128), F32)],
+        [((16, 512), BF), ((16, 80, 512), BF), ((8, 128), F32)],
         got, gain.reshape(1, 512), w_in, w_out,
-        scalar=jnp.stack([core, u]),
-        scratch=[pltpu.VMEM((128, 512), BF)] + [pltpu.VMEM((8, 128, 128), BF)] * 2,
+        scalar=jnp.stack([core, a]),
+        scratch=[pltpu.VMEM((64, 512), BF)] + [pltpu.VMEM((8, 64, 128), BF)] * 2,
     )
     change = lax.ppermute(change, ALL, BACK)
-    (send,) = call(back_and_tile, [((8, 80, 128), F32)], adjacency, trade(send, ALONG_V), gain_part)
+    (send,) = call(back_and_tile, [((8, 80, 128), F32)], adjacency, trade(send, WIDE), gain_part)
     grad, send = call(
         add_up, [((64, 128), BF), ((64, 16, 128), BF)],
         lax.all_to_all(send, "rep", 0, 0), cotangent,

time: 140 us -> 144 us (1.029)
  starting transfers between devices: 38.3 us -> 43.9 us
  waiting for transfers between devices: 41.7 us -> 36.1 us
  blocking collectives: 50.2 us -> 54.5 us
    all_to_all x2, waiting for transfers between devices: 19.4 us -> 11 us  [trade(): return lax.all_to_all(x, ALL, 0, 0, axis_index_groups=groups)]
    all_to_all x2, blocking collectives: 34.9 us -> 41.4 us  [trade(): return lax.all_to_all(x, ALL, 0, 0, axis_index_groups=groups)]
    ppermute x1, waiting for transfers between devices: 12 us -> 15.5 us  [shards(): lax.ppermute(lax.dynamic_slice_in_dim(cotangent, p * 16, 16, 0), ALL, OUT)]
    all_to_all x1, starting transfers between devices: 4.62 us -> 7.54 us  [shards(): table = lax.all_to_all(send, 'rows', 0, 0)]
    all_to_all x1, blocking collectives: 15.3 us -> 13.1 us  [shards(): lax.all_to_all(send, 'rep', 0, 0)]
    all_to_all x2, starting transfers between devices: 16.7 us -> 18.4 us  [trade(): return lax.all_to_all(x, ALL, 0, 0, axis_index_groups=groups)]
where the time goes in v5:
time: 144 us
  blocking collectives  54.5 us (38%)
  starting transfers between devices  43.9 us (30%)
  waiting for transfers between devices  36.1 us (25%)
  Pallas kernels  5.45 us (4%)
  matrix products  2.41 us (2%)
    all_to_all x2, blocking collectives, trade(): return lax.all_to_all(x, ALL, 0, 0, axis_index_groups=groups)  41.4 us
    all_to_all x2, starting transfers between devices, trade(): return lax.all_to_all(x, ALL, 0, 0, axis_index_groups=groups)  18.4 us
    ppermute x1, waiting for transfers between devices, shards(): lax.ppermute(lax.dynamic_slice_in_dim(cotangent, p * 16, 16, 0), ALL, OUT)  15.5 us
    all_to_all x1, blocking collectives, shards(): lax.all_to_all(send, 'rep', 0, 0)  13.1 us
    all_to_all x2, waiting for transfers between devices, trade(): return lax.all_to_all(x, ALL, 0, 0, axis_index_groups=groups)  11 us
    ppermute x1, starting transfers between devices, shards(): lax.ppermute(lax.dynamic_slice_in_dim(cotangent, p * 16, 16, 0), ALL, OUT)  7.61 us
    all_to_all x1, starting transfers between devices, shards(): table = lax.all_to_all(send, 'rows', 0, 0)  7.54 us
    ppermute x1, starting transfers between devices, shards(): other = lax.ppermute(mine, ALL, CORE)  6.3 us
  transfers between devices with their start and end apart: 6, of which 5 were waited for; matrix products, arithmetic and copies ran while one was open for 0% of the time, Pallas kernels for 0%

profile of v5, /device:TPU:1, one launch (start us, length us, event | category | flops | bytes accessed | tf_op | source)
XLA Modules:
  0.0 143.8 jit_solution(13210884575807338274)
XLA Ops:
  0.6 2.4 %convolution_convert_fusion = bf16[1024,512]{1,0:T(8,128)(2,1)} fusion(bf16[128,1024]{1,0:T(8,128)(2,1)} %adjacency.1, bf16[128,512]{1,0:T(8,128)(2,1)} %nodes.1), kind=kOutput, calls=%fused_computation | convolution fusion | flops 134742016 | bytes 1441792 | tf_op jit(solution)/shard_map/dot_general | solution.py:29
  3.0 9.7 %all-to-all-start = ((bf16[16,64,512]{2,1,0:T(8,128)(2,1)}), bf16[16,64,512]{2,1,0:T(8,128)(2,1)S(1)}, u32[]{:S(2)}, u32[]{:S(2)}) async-start(bf16[16,64,512]{2,1,0:T(8,128)(2,1)} %bitcast.3), calls=%async_computation | async-start | bytes 2097152 | tf_op jit(solution)/shard_map/all_to_all | solution.py:33
  12.8 0.0 copy-start.1
  12.8 7.6 %collective-permute-start = (bf16[16,512]{1,0:T(8,128)(2,1)S(1)}, bf16[16,512]{1,0:T(8,128)(2,1)S(1)}, u32[]{:S(2)}, u32[]{:S(2)}) collective-permute-start(bf16[16,512]{1,0:T(8,128)(2,1)S(1)} %constant_dynamic-slice_fusion), channel_id=1, source_target_pairs={{0,0},{1,16},{2,32},{3,48},{4,8},{5,24},{6,40},{7,56},{8,64},{9,80... | collective-permute-start | bytes 49160 | tf_op jit(solution)/shard_map/ppermute | solution.py:200
  20.4 15.5 %collective-permute-done.cot = bf16[16,512]{1,0:T(8,128)(2,1)S(1)} collective-permute-done((bf16[16,512]{1,0:T(8,128)(2,1)S(1)}, bf16[16,512]{1,0:T(8,128)(2,1)S(1)}, u32[]{:S(2)}, u32[]{:S(2)}) %collective-permute-start) | collective-permute-done | bytes 16416 | tf_op jit(solution)/shard_map/ppermute | solution.py:200
  35.9 1.0 shard_map.101
  36.9 8.7 %all-to-all-start.1 = ((bf16[4,144,512]{2,1,0:T(8,128)(2,1)}), bf16[4,144,512]{2,1,0:T(8,128)(2,1)S(1)}, u32[]{:S(2)}, u32[]{:S(2)}) async-start(bf16[4,144,512]{2,1,0:T(8,128)(2,1)} %shard_map.101), calls=%async_computation.1 | async-start | bytes 1179648 | tf_op jit(solution)/shard_map/all_to_all | solution.py:33
  45.6 0.1 pad_add_fusion.at_ref
  45.7 11.0 %all-to-all-done.1.got = bf16[4,144,512]{2,1,0:T(8,128)(2,1)S(1)} async-done(((bf16[4,144,512]{2,1,0:T(8,128)(2,1)}), bf16[4,144,512]{2,1,0:T(8,128)(2,1)S(1)}, u32[]{:S(2)}, u32[]{:S(2)}) %all-to-all-start.1) | async-done | bytes 589856 | tf_op jit(solution)/shard_map/all_to_all | solution.py:33
  56.7 1.5 %shard_map.102 = (bf16[16,512]{1,0:T(8,128)(2,1)S(1)}, bf16[16,80,512]{2,1,0:T(8,128)(2,1)S(1)}, f32[8,128]{1,0:T(8,128)S(1)}) custom-call(s32[2]{0:T(128)S(1)} %pad_add_fusion.at_ref, bf16[4,144,512]{2,1,0:T(8,128)(2,1)S(1)} %all-to-all-done.1.got, f32[1,512]{1,0:T(1,128)S(1)} %bitcast.9, bf16[512,512]{1,0:T(8,128)(2,1)S(1)} %copy-done.1, ...), custom_call_target="tpu_custom_call" | custom-call | tf_op jit(solution)/shard_map/pallas_call | solution.py:41
  58.2 31.4 %all_to_all.30.got = bf16[16,80,512]{2,1,0:T(8,128)(2,1)S(1)} all-to-all(bf16[16,80,512]{2,1,0:T(8,128)(2,1)S(1)} %get-tuple-element.16), channel_id=1, replica_groups={{0,8,64,72,128,136,192,200,256,264,320,328,384,392,448,456},{1,65,9,73,..., dimensions={0} | all-to-all | bytes 2621440 | tf_op jit(solution)/shard_map/all_to_all | solution.py:33
  89.6 0.3 shard_map.103
  89.9 13.1 %all_to_all.31.got = f32[8,80,128]{2,1,0:T(8,128)S(1)} all-to-all(f32[8,80,128]{2,1,0:T(8,128)S(1)} %shard_map.103), channel_id=1, replica_groups=mesh['rows'=64,'rep'=8] {'rep'}, dimensions={0} | all-to-all | bytes 655360 | tf_op jit(solution)/shard_map/all_to_all | solution.py:217
  103.0 0.7 shard_map.104
  103.7 7.5 %all-to-all-start.4 = ((bf16[64,16,128]{2,1,0:T(8,128)(2,1)}), bf16[64,16,128]{2,1,0:T(8,128)(2,1)S(1)}, u32[]{:S(2)}, u32[]{:S(2)}) async-start(bf16[64,16,128]{2,1,0:T(8,128)(2,1)} %get-tuple-element.18), calls=%async_computation.4 | async-start | bytes 524288 | tf_op jit(solution)/shard_map/all_to_all | solution.py:220
  111.3 4.1 %collective-permute-start.1 = (bf16[16,512]{1,0:T(8,128)(2,1)S(1)}, bf16[16,512]{1,0:T(8,128)(2,1)S(1)}, u32[]{:S(2)}, u32[]{:S(2)}) collective-permute-start(bf16[16,512]{1,0:T(8,128)(2,1)S(1)} %get-tuple-element.20), channel_id=1, source_target_pairs={{0,0},{16,1},{32,2},{48,3},{8,4},{24,5},{40,6},{56,7},{64,8},{80,9... | collective-permute-start | bytes 49160 | tf_op jit(solution)/shard_map/ppermute | solution.py:213
  115.4 4.0 %collective-permute-done.1.change = bf16[16,512]{1,0:T(8,128)(2,1)S(1)} collective-permute-done((bf16[16,512]{1,0:T(8,128)(2,1)S(1)}, bf16[16,512]{1,0:T(8,128)(2,1)S(1)}, u32[]{:S(2)}, u32[]{:S(2)}) %collective-permute-start.1) | collective-permute-done | bytes 16416 | tf_op jit(solution)/shard_map/ppermute | solution.py:213
  119.4 4.5 %all-to-all-done.4.got = bf16[64,16,128]{2,1,0:T(8,128)(2,1)S(1)} async-done(((bf16[64,16,128]{2,1,0:T(8,128)(2,1)}), bf16[64,16,128]{2,1,0:T(8,128)(2,1)S(1)}, u32[]{:S(2)}, u32[]{:S(2)}) %all-to-all-start.4) | async-done | bytes 262176 | tf_op jit(solution)/shard_map/all_to_all | solution.py:220
  123.9 0.1 shard_map.105
  124.0 10.0 %all_to_all.32.mine = bf16[4,640,128]{2,1,0:T(8,128)(2,1)S(1)} all-to-all(bf16[4,640,128]{2,1,0:T(8,128)(2,1)S(1)} %get-tuple-element.21), channel_id=1, replica_groups={{0,2,4,6},{1,3,5,7},{8,10,12,14},{9,11,13,15},{16,18,20,22},{17,19,21,2..., dimensions={0} | all-to-all | bytes 1310720 | tf_op jit(solution)/shard_map/all_to_all | solution.py:33
  134.0 6.3 %collective-permute-start.2 = (bf16[4,640,128]{2,1,0:T(8,128)(2,1)S(1)}, bf16[4,640,128]{2,1,0:T(8,128)(2,1)S(1)}, u32[]{:S(2)}, u32[]{:S(2)}) collective-permute-start(bf16[4,640,128]{2,1,0:T(8,128)(2,1)S(1)} %all_to_all.32.mine), channel_id=1, source_target_pairs={{0,1},{1,0},{2,3},{3,2},{4,5},{5,4},{6,7},{7,6},{8,9},{9,8},{10,11... | collective-permute-start | bytes 1966088 | tf_op jit(solution)/shard_map/ppermute | solution.py:223
  140.3 0.6 slice_bitcast_fusion
  140.9 1.1 collective-permute-done.2.other
  142.0 1.8 %shard_map.106 = (f32[512,512]{1,0:T(8,128)}, f32[512,512]{1,0:T(8,128)}, bf16[128,512]{1,0:T(8,128)(2,1)}, bf16[128,512]{1,0:T(8,128)(2,1)}) custom-call(s32[1]{0:T(128)} %bitcast.c_ref, bf16[4,640,128]{2,1,0:T(8,128)(2,1)S(1)} %all_to_all.32.mine, bf16[4,640,128]{2,1,0:T(8,128)(2,1)S(1)} %collective-permute-done.2.other, bf16[128,512]{1,0:T(8,128)(2,1)S(1)} %copy-done.3), custom_call_target="tpu_custom_call" | custom-call | tf_op jit(solution)/shard_map/pallas_call | solution.py:41
  (13 shorter events, 0.0 us)
Async XLA Ops:
  3.0 9.7 %copy-start.4 = (bf16[128,512]{1,0:T(8,128)(2,1)S(1)}, bf16[128,512]{1,0:T(8,128)(2,1)}, u32[]{:S(2)}) copy-start(bf16[128,512]{1,0:T(8,128)(2,1)} %cotangent.1) | copy-start | bytes 393220
  3.0 32.9 %all-to-all-start = ((bf16[16,64,512]{2,1,0:T(8,128)(2,1)}), bf16[16,64,512]{2,1,0:T(8,128)(2,1)S(1)}, u32[]{:S(2)}, u32[]{:S(2)}) async-start(bf16[16,64,512]{2,1,0:T(8,128)(2,1)} %bitcast.3), calls=%async_computation | async-start | bytes 2097152 | tf_op jit(solution)/shard_map/all_to_all | solution.py:33
  12.8 43.9 %copy-start.1 = (bf16[512,512]{1,0:T(8,128)(2,1)S(1)}, bf16[512,512]{1,0:T(8,128)(2,1)}, u32[]{:S(2)}) copy-start(bf16[512,512]{1,0:T(8,128)(2,1)} %w_in_ref.1) | copy-start | bytes 1572868
  12.8 43.9 %copy-start.2 = (bf16[512,512]{1,0:T(8,128)(2,1)S(1)}, bf16[512,512]{1,0:T(8,128)(2,1)}, u32[]{:S(2)}) copy-start(bf16[512,512]{1,0:T(8,128)(2,1)} %w_out_ref.1) | copy-start | bytes 1572868
  12.8 43.9 %copy-start.5 = (f32[512]{0:T(512)S(1)}, f32[512]{0:T(512)}, u32[]{:S(2)}) copy-start(f32[512]{0:T(512)} %param.8) | copy-start | bytes 6148
  12.8 23.1 %collective-permute-start = (bf16[16,512]{1,0:T(8,128)(2,1)S(1)}, bf16[16,512]{1,0:T(8,128)(2,1)S(1)}, u32[]{:S(2)}, u32[]{:S(2)}) collective-permute-start(bf16[16,512]{1,0:T(8,128)(2,1)S(1)} %constant_dynamic-slice_fusion), channel_id=1, source_target_pairs={{0,0},{1,16},{2,32},{3,48},{4,8},{5,24},{6,40},{7,56},{8,64},{9,80... | collective-permute-start | bytes 49160 | tf_op jit(solution)/shard_map/ppermute | solution.py:200
  36.9 19.8 %all-to-all-start.1 = ((bf16[4,144,512]{2,1,0:T(8,128)(2,1)}), bf16[4,144,512]{2,1,0:T(8,128)(2,1)S(1)}, u32[]{:S(2)}, u32[]{:S(2)}) async-start(bf16[4,144,512]{2,1,0:T(8,128)(2,1)} %shard_map.101), calls=%async_computation.1 | async-start | bytes 1179648 | tf_op jit(solution)/shard_map/all_to_all | solution.py:33
  58.2 31.4 %copy-start = (bf16[128,1024]{1,0:T(8,128)(2,1)S(1)}, bf16[128,1024]{1,0:T(8,128)(2,1)}, u32[]{:S(2)}) copy-start(bf16[128,1024]{1,0:T(8,128)(2,1)} %adjacency.1) | copy-start | bytes 786436
  103.0 39.1 %copy-start.3 = (bf16[128,512]{1,0:T(8,128)(2,1)S(1)}, bf16[128,512]{1,0:T(8,128)(2,1)}, u32[]{:S(2)}) copy-start(bf16[128,512]{1,0:T(8,128)(2,1)} %nodes.1) | copy-start | bytes 393220
  103.7 20.2 %all-to-all-start.4 = ((bf16[64,16,128]{2,1,0:T(8,128)(2,1)}), bf16[64,16,128]{2,1,0:T(8,128)(2,1)S(1)}, u32[]{:S(2)}, u32[]{:S(2)}) async-start(bf16[64,16,128]{2,1,0:T(8,128)(2,1)} %get-tuple-element.18), calls=%async_computation.4 | async-start | bytes 524288 | tf_op jit(solution)/shard_map/all_to_all | solution.py:220
  111.3 8.1 %collective-permute-start.1 = (bf16[16,512]{1,0:T(8,128)(2,1)S(1)}, bf16[16,512]{1,0:T(8,128)(2,1)S(1)}, u32[]{:S(2)}, u32[]{:S(2)}) collective-permute-start(bf16[16,512]{1,0:T(8,128)(2,1)S(1)} %get-tuple-element.20), channel_id=1, source_target_pairs={{0,0},{16,1},{32,2},{48,3},{8,4},{24,5},{40,6},{56,7},{64,8},{80,9... | collective-permute-start | bytes 49160 | tf_op jit(solution)/shard_map/ppermute | solution.py:213
  134.0 8.0 %collective-permute-start.2 = (bf16[4,640,128]{2,1,0:T(8,128)(2,1)S(1)}, bf16[4,640,128]{2,1,0:T(8,128)(2,1)S(1)}, u32[]{:S(2)}, u32[]{:S(2)}) collective-permute-start(bf16[4,640,128]{2,1,0:T(8,128)(2,1)S(1)} %all_to_all.32.mine), channel_id=1, source_target_pairs={{0,1},{1,0},{2,3},{3,2},{4,5},{5,4},{6,7},{7,6},{8,9},{9,8},{10,11... | collective-permute-start | bytes 1966088 | tf_op jit(solution)/shard_map/ppermute | solution.py:223

commit v6 on v4

--- a/solution.py
+++ b/solution.py
@@ -33,19 +33,15 @@
     return lax.all_to_all(x, ALL, 0, 0, axis_index_groups=groups)
 
 
-def call(body, outs, *args, scalar=None, scratch=()):
-    specs = [pl.BlockSpec(memory_space=pltpu.VMEM)] * len(args)
-    if scalar is not None:
-        args = (scalar,) + args
-        specs = [pl.BlockSpec(memory_space=pltpu.SMEM)] + specs
+def call(body, outs, at, *args, scratch=()):
     return pl.pallas_call(
         body,
         out_shape=[jax.ShapeDtypeStruct(s, d) for s, d in outs],
-        in_specs=specs,
+        in_specs=[pl.BlockSpec(memory_space=pltpu.SMEM)] + [pl.BlockSpec(memory_space=pltpu.VMEM)] * len(args),
         out_specs=[pl.BlockSpec(memory_space=pltpu.VMEM)] * len(outs),
         scratch_shapes=list(scratch),
         compiler_params=pltpu.CompilerParams(vmem_limit_bytes=40 * 1024 * 1024),
-    )(*args)
+    )(at, *args)
 
 
 def left_half():
@@ -59,7 +55,7 @@
     return total
 
 
-def sum_and_copy(got, cot, send):
+def sum_and_copy(at_ref, got, cot, send):
     total, piece = total_of(got).astype(BF), cot[...]
     for u in E8:
         send[u, 0:128, :] = total
@@ -117,35 +113,37 @@
             send[k, 144:160, at] = low[16 * j : 16 * j + 16]
 
 
-def back_and_tile(adjacency, got, gain_part, send):
+def back_and_tile(at_ref, adjacency, got, gain_part, send):
     field = got[:, 0:128, :].reshape(1024, 512)
     back = dot(adjacency[...], field, 1, 0)
     for q in E8:
         for j in range(4):
-            send[q, 16 * j : 16 * j + 16, :] = back[16 * q : 16 * q + 16, 128 * j : 128 * j + 128]
+            send[q, 16 * j : 16 * j + 16, :] = back[16 * q : 16 * q + 16, 128 * j : 128 * j + 128].astype(BF)
     tile = jnp.zeros((16, 512), F32)
     for v in E8:
         tile = tile + (got[v, 128:144, :].astype(F32) + got[v, 144:160, :].astype(F32))
     part = gain_part[...]
     for q in E8:
         at = slice(128 * (q // 2), 128 * (q // 2) + 128)
-        send[q, 64:72, :] = tile[8 * (q % 2) : 8 * (q % 2) + 8, at]
-        send[q, 72:80, :] = part
-
-
-def add_up(p_ref, got, cotangent, grad, send):
+        exact = jnp.concatenate([tile[8 * (q % 2) : 8 * (q % 2) + 8, at], part], axis=0)
+        high = exact.astype(BF)
+        send[q, 64:80, :] = high
+        send[q, 80:96, :] = (exact - high.astype(F32)).astype(BF)
+
+
+def add_up(at_ref, got, cotangent, grad, send):
     total = total_of(got)
-    own = cotangent[pl.ds(pl.multiple_of(p_ref[0] * 16, 16), 16), :].astype(F32)
+    own = cotangent[pl.ds(pl.multiple_of(at_ref[2] * 16, 16), 16), :].astype(F32)
     for j in range(4):
         grad[16 * j : 16 * j + 16, :] = (
             own[:, 128 * j : 128 * j + 128] + total[16 * j : 16 * j + 16]
         ).astype(BF)
-    block = total[64:80].astype(BF)
+    block = (total[64:80] + total[80:96]).astype(BF)
     for r in range(64):
         send[r] = block
 
 
-def pack(got, grad, change, send, gain):
+def pack(at_ref, got, grad, change, send, gain):
     total = jnp.zeros((8, 128), F32)
     for i in range(32):
         one, two = got[2 * i].astype(F32), got[2 * i + 1].astype(F32)
@@ -161,7 +159,7 @@
             send[x, 576 + 16 * j : 592 + 16 * j, :] = change[:, 128 * j : 128 * j + 128]
 
 
-def unpack(c_ref, mine, other, nodes, grad_in, grad_out, node_grad, node_out):
+def unpack(at_ref, mine, other, nodes, grad_in, grad_out, node_grad, node_out):
     left = left_half()
 
     def lay(src, c):
@@ -181,12 +179,12 @@
                 change = src[x, 576 + 16 * j : 592 + 16 * j, :].astype(F32)
                 node_out[rows, cols] = (nodes[rows, cols].astype(F32) + change).astype(BF)
 
-    @pl.when(c_ref[0] == 0)
+    @pl.when(at_ref[0] == 0)
     def _():
         lay(mine, 0)
         lay(other, 1)
 
-    @pl.when(c_ref[0] == 1)
+    @pl.when(at_ref[0] == 1)
     def _():
         lay(other, 0)
         lay(mine, 1)
@@ -194,37 +192,34 @@
 
 def shards(nodes, adjacency, gain, w_in, w_out, cotangent):
     r, p = lax.axis_index("rows"), lax.axis_index("rep")
-    core = p % 2
-    u = jnp.where(core == 0, r % 8, r // 8)
+    core = p & 1
+    at = jnp.stack([core, jnp.where(core == 0, r & 7, r >> 3), p])
     cot = lax.ppermute(lax.dynamic_slice_in_dim(cotangent, p * 16, 16, 0), ALL, OUT)
 
     part = dot(adjacency, nodes, 0, 0).astype(BF).reshape(8, 128, 512)
-    (part,) = call(sum_and_copy, [((8, 144, 512), BF)], trade(part, ALONG_V), cot)
+    (part,) = call(sum_and_copy, [((8, 144, 512), BF)], at, trade(part, ALONG_V), cot)
     got = trade(part, ALONG_U)
 
     change, send, gain_part = call(
         update,
         [((16, 512), BF), ((8, 160, 512), BF), ((8, 128), F32)],
-        got, gain.reshape(1, 512), w_in, w_out,
-        scalar=jnp.stack([core, u]),
+        at, got, gain.reshape(1, 512), w_in, w_out,
         scratch=[pltpu.VMEM((128, 512), BF)] + [pltpu.VMEM((8, 128, 128), BF)] * 2,
     )
     change = lax.ppermute(change, ALL, BACK)
-    (send,) = call(back_and_tile, [((8, 80, 128), F32)], adjacency, trade(send, ALONG_V), gain_part)
+    (send,) = call(back_and_tile, [((8, 96, 128), BF)], at, adjacency, trade(send, ALONG_V), gain_part)
     grad, send = call(
         add_up, [((64, 128), BF), ((64, 16, 128), BF)],
-        lax.all_to_all(send, "rep", 0, 0), cotangent,
-        scalar=p.reshape(1),
+        at, lax.all_to_all(send, "rep", 0, 0), cotangent,
     )
     table = lax.all_to_all(send, "rows", 0, 0)
-    send, grad_gain = call(pack, [((4, 640, 128), BF), ((8, 128), F32)], table, grad, change)
+    send, grad_gain = call(pack, [((4, 640, 128), BF), ((8, 128), F32)], at, table, grad, change)
     mine = trade(send, ALONG_X)
     other = lax.ppermute(mine, ALL, CORE)
     grad_in, grad_out, node_grad, node_out = call(
         unpack,
         [((512, 512), F32), ((512, 512), F32), ((128, 512), BF), ((128, 512), BF)],
-        mine, other, nodes,
-        scalar=core.reshape(1),
+        at, mine, other, nodes,
     )
     return (node_out, node_grad, grad_in, grad_out, grad_gain[:4].reshape(512))
 

time: 140 us -> 140 us (level)
  blocking collectives: 50.2 us -> 76.7 us
  waiting for transfers between devices: 41.7 us -> 21.7 us
  starting transfers between devices: 38.3 us -> 29.9 us
  Pallas kernels: 5.77 us -> 7.45 us
    all_to_all x2 -> x3, blocking collectives: 34.9 us -> 63 us  [trade(): return lax.all_to_all(x, ALL, 0, 0, axis_index_groups=groups)]
    all_to_all x2 -> x1, waiting for transfers between devices: 19.4 us -> 0.01 us  [trade(): return lax.all_to_all(x, ALL, 0, 0, axis_index_groups=groups)]
    all_to_all x2 -> x1, starting transfers between devices: 16.7 us -> 7.78 us  [trade(): return lax.all_to_all(x, ALL, 0, 0, axis_index_groups=groups)]
    pallas_call x6, Pallas kernels: 5.77 us -> 7.45 us  [call(): pl.pallas_call(body, out_shape=[jax.ShapeDtypeStruct(s, d) for s, d in ou...]
    all_to_all x1, blocking collectives: 15.3 us -> 13.7 us  [shards(): lax.all_to_all(send, 'rep', 0, 0)]
  transfers between devices with their start and end apart: 6 -> 5, of which waited for: 5 -> 4; matrix products, arithmetic and copies ran while one was open for 0% -> 0% of each run, Pallas kernels for 0% -> 0%
where the time goes in v6:
time: 140 us
  blocking collectives  76.7 us (55%)
  starting transfers between devices  29.9 us (21%)
  waiting for transfers between devices  21.7 us (16%)
  Pallas kernels  7.45 us (5%)
  matrix products  2.41 us (2%)
    all_to_all x3, blocking collectives, trade(): return lax.all_to_all(x, ALL, 0, 0, axis_index_groups=groups)  63 us
    all_to_all x1, blocking collectives, shards(): lax.all_to_all(send, 'rep', 0, 0)  13.7 us
    ppermute x1, waiting for transfers between devices, shards(): lax.ppermute(lax.dynamic_slice_in_dim(cotangent, p * 16, 16, 0), ALL, OUT)  11.9 us
    all_to_all x1, starting transfers between devices, trade(): return lax.all_to_all(x, ALL, 0, 0, axis_index_groups=groups)  7.78 us
    pallas_call x6, Pallas kernels, call(): pl.pallas_call(body, out_shape=[jax.ShapeDtypeStruct(s, d) for s, d in ou...  7.45 us
    ppermute x1, starting transfers between devices, shards(): lax.ppermute(lax.dynamic_slice_in_dim(cotangent, p * 16, 16, 0), ALL, OUT)  7.26 us
    ppermute x1, starting transfers between devices, shards(): other = lax.ppermute(mine, ALL, CORE)  6.26 us
    all_to_all x1, starting transfers between devices, shards(): table = lax.all_to_all(send, 'rows', 0, 0)  4.62 us
  transfers between devices with their start and end apart: 5, of which 4 were waited for; matrix products, arithmetic and copies ran while one was open for 0% of the time, Pallas kernels for 0%

profile of v6, /device:TPU:1, one launch (start us, length us, event | category | flops | bytes accessed | tf_op | source)
XLA Modules:
  0.0 139.6 jit_solution(6277853205855064925)
XLA Ops:
  0.6 2.4 %convolution_convert_fusion = bf16[1024,512]{1,0:T(8,128)(2,1)} fusion(bf16[128,1024]{1,0:T(8,128)(2,1)} %adjacency.1, bf16[128,512]{1,0:T(8,128)(2,1)} %nodes.1), kind=kOutput, calls=%fused_computation | convolution fusion | flops 134742016 | bytes 1441792 | tf_op jit(solution)/shard_map/dot_general | solution.py:29
  3.0 7.8 %all-to-all-start = ((bf16[8,128,512]{2,1,0:T(8,128)(2,1)}), bf16[8,128,512]{2,1,0:T(8,128)(2,1)S(1)}, u32[]{:S(2)}, u32[]{:S(2)}) async-start(bf16[8,128,512]{2,1,0:T(8,128)(2,1)} %bitcast.3), calls=%async_computation | async-start | bytes 2097152 | tf_op jit(solution)/shard_map/all_to_all | solution.py:33
  10.8 7.3 %collective-permute-start = (bf16[16,512]{1,0:T(8,128)(2,1)S(1)}, bf16[16,512]{1,0:T(8,128)(2,1)S(1)}, u32[]{:S(2)}, u32[]{:S(2)}) collective-permute-start(bf16[16,512]{1,0:T(8,128)(2,1)S(1)} %constant_dynamic-slice_fusion), channel_id=1, source_target_pairs={{0,0},{1,8},{2,16},{3,24},{4,32},{5,40},{6,48},{7,56},{8,64},{9,72... | collective-permute-start | bytes 49160 | tf_op jit(solution)/shard_map/ppermute | solution.py:197
  18.1 0.1 pad_add_fusion.at_ref
  18.2 11.9 %collective-permute-done.cot = bf16[16,512]{1,0:T(8,128)(2,1)S(1)} collective-permute-done((bf16[16,512]{1,0:T(8,128)(2,1)S(1)}, bf16[16,512]{1,0:T(8,128)(2,1)S(1)}, u32[]{:S(2)}, u32[]{:S(2)}) %collective-permute-start) | collective-permute-done | bytes 16416 | tf_op jit(solution)/shard_map/ppermute | solution.py:197
  30.1 0.7 shard_map.101
  30.8 0.0 copy-start.1
  30.8 0.0 copy-start.2
  30.8 27.8 %all_to_all.30.got = bf16[8,144,512]{2,1,0:T(8,128)(2,1)S(1)} all-to-all(bf16[8,144,512]{2,1,0:T(8,128)(2,1)S(1)} %shard_map.101), channel_id=1, replica_groups={{0,8,16,24,32,40,48,56},{1,65,129,193,257,321,385,449},{2,10,18,26,34,4..., dimensions={0} | all-to-all | bytes 2359296 | tf_op jit(solution)/shard_map/all_to_all | solution.py:33
  58.7 1.6 %shard_map.102 = (bf16[16,512]{1,0:T(8,128)(2,1)S(1)}, bf16[8,160,512]{2,1,0:T(8,128)(2,1)S(1)}, f32[8,128]{1,0:T(8,128)S(1)}) custom-call(s32[3]{0:T(128)S(1)} %pad_add_fusion.at_ref, bf16[8,144,512]{2,1,0:T(8,128)(2,1)S(1)} %all_to_all.30.got, f32[1,512]{1,0:T(1,128)S(1)} %bitcast.9, bf16[512,512]{1,0:T(8,128)(2,1)S(1)} %copy-done.1, ...), custom_call_target="tpu_custom_call" | custom-call | tf_op jit(solution)/shard_map/pallas_call | solution.py:37
  60.3 25.1 %all_to_all.31.got = bf16[8,160,512]{2,1,0:T(8,128)(2,1)S(1)} all-to-all(bf16[8,160,512]{2,1,0:T(8,128)(2,1)S(1)} %get-tuple-element.16), channel_id=1, replica_groups={{0,64,128,192,256,320,384,448},{1,9,17,25,33,41,49,57},{2,66,130,194,25..., dimensions={0} | all-to-all | bytes 2621440 | tf_op jit(solution)/shard_map/all_to_all | solution.py:33
  85.4 0.9 shard_map.103
  86.3 13.7 %all_to_all.32.got = bf16[8,96,128]{2,1,0:T(8,128)(2,1)S(1)} all-to-all(bf16[8,96,128]{2,1,0:T(8,128)(2,1)S(1)} %shard_map.103), channel_id=1, replica_groups=mesh['rows'=64,'rep'=8] {'rep'}, dimensions={0} | all-to-all | bytes 393216 | tf_op jit(solution)/shard_map/all_to_all | solution.py:213
  100.0 1.3 shard_map.104
  101.3 4.6 %all-to-all-start.4 = ((bf16[64,16,128]{2,1,0:T(8,128)(2,1)}), bf16[64,16,128]{2,1,0:T(8,128)(2,1)S(1)}, u32[]{:S(2)}, u32[]{:S(2)}) async-start(bf16[64,16,128]{2,1,0:T(8,128)(2,1)} %get-tuple-element.18), calls=%async_computation.4 | async-start | bytes 524288 | tf_op jit(solution)/shard_map/all_to_all | solution.py:215
  105.9 4.0 %collective-permute-start.1 = (bf16[16,512]{1,0:T(8,128)(2,1)S(1)}, bf16[16,512]{1,0:T(8,128)(2,1)S(1)}, u32[]{:S(2)}, u32[]{:S(2)}) collective-permute-start(bf16[16,512]{1,0:T(8,128)(2,1)S(1)} %get-tuple-element.20), channel_id=1, source_target_pairs={{0,0},{8,1},{16,2},{24,3},{32,4},{40,5},{48,6},{56,7},{64,8},{72,9... | collective-permute-start | bytes 49160 | tf_op jit(solution)/shard_map/ppermute | solution.py:209
  109.9 4.1 %collective-permute-done.1.change = bf16[16,512]{1,0:T(8,128)(2,1)S(1)} collective-permute-done((bf16[16,512]{1,0:T(8,128)(2,1)S(1)}, bf16[16,512]{1,0:T(8,128)(2,1)S(1)}, u32[]{:S(2)}, u32[]{:S(2)}) %collective-permute-start.1) | collective-permute-done | bytes 16416 | tf_op jit(solution)/shard_map/ppermute | solution.py:209
  114.0 4.5 %all-to-all-done.4.got = bf16[64,16,128]{2,1,0:T(8,128)(2,1)S(1)} async-done(((bf16[64,16,128]{2,1,0:T(8,128)(2,1)}), bf16[64,16,128]{2,1,0:T(8,128)(2,1)S(1)}, u32[]{:S(2)}, u32[]{:S(2)}) %all-to-all-start.4) | async-done | bytes 262176 | tf_op jit(solution)/shard_map/all_to_all | solution.py:215
  118.5 0.7 shard_map.105
  119.2 10.0 %all_to_all.33.mine = bf16[4,640,128]{2,1,0:T(8,128)(2,1)S(1)} all-to-all(bf16[4,640,128]{2,1,0:T(8,128)(2,1)S(1)} %get-tuple-element.21), channel_id=1, replica_groups={{0,2,4,6},{1,3,5,7},{8,10,12,14},{9,11,13,15},{16,18,20,22},{17,19,21,2..., dimensions={0} | all-to-all | bytes 1310720 | tf_op jit(solution)/shard_map/all_to_all | solution.py:33
  129.3 6.3 %collective-permute-start.2 = (bf16[4,640,128]{2,1,0:T(8,128)(2,1)S(1)}, bf16[4,640,128]{2,1,0:T(8,128)(2,1)S(1)}, u32[]{:S(2)}, u32[]{:S(2)}) collective-permute-start(bf16[4,640,128]{2,1,0:T(8,128)(2,1)S(1)} %all_to_all.33.mine), channel_id=1, source_target_pairs={{0,1},{1,0},{2,3},{3,2},{4,5},{5,4},{6,7},{7,6},{8,9},{9,8},{10,11... | collective-permute-start | bytes 1966088 | tf_op jit(solution)/shard_map/ppermute | solution.py:218
  135.5 0.6 slice_bitcast_fusion
  136.1 1.1 collective-permute-done.2.other
  137.2 2.3 %shard_map.106 = (f32[512,512]{1,0:T(8,128)}, f32[512,512]{1,0:T(8,128)}, bf16[128,512]{1,0:T(8,128)(2,1)}, bf16[128,512]{1,0:T(8,128)(2,1)}) custom-call(s32[3]{0:T(128)S(1)} %pad_add_fusion.at_ref, bf16[4,640,128]{2,1,0:T(8,128)(2,1)S(1)} %all_to_all.33.mine, bf16[4,640,128]{2,1,0:T(8,128)(2,1)S(1)} %collective-permute-done.2.other, ...), custom_call_target="tpu_custom_call" | custom-call | tf_op jit(solution)/shard_map/pallas_call | solution.py:37
  (12 shorter events, 0.0 us)
Async XLA Ops:
  3.0 7.8 %copy-start.4 = (bf16[128,512]{1,0:T(8,128)(2,1)S(1)}, bf16[128,512]{1,0:T(8,128)(2,1)}, u32[]{:S(2)}) copy-start(bf16[128,512]{1,0:T(8,128)(2,1)} %cotangent.1) | copy-start | bytes 393220
  3.0 27.0 %all-to-all-start = ((bf16[8,128,512]{2,1,0:T(8,128)(2,1)}), bf16[8,128,512]{2,1,0:T(8,128)(2,1)S(1)}, u32[]{:S(2)}, u32[]{:S(2)}) async-start(bf16[8,128,512]{2,1,0:T(8,128)(2,1)} %bitcast.3), calls=%async_computation | async-start | bytes 2097152 | tf_op jit(solution)/shard_map/all_to_all | solution.py:33
  10.8 19.2 %collective-permute-start = (bf16[16,512]{1,0:T(8,128)(2,1)S(1)}, bf16[16,512]{1,0:T(8,128)(2,1)S(1)}, u32[]{:S(2)}, u32[]{:S(2)}) collective-permute-start(bf16[16,512]{1,0:T(8,128)(2,1)S(1)} %constant_dynamic-slice_fusion), channel_id=1, source_target_pairs={{0,0},{1,8},{2,16},{3,24},{4,32},{5,40},{6,48},{7,56},{8,64},{9,72... | collective-permute-start | bytes 49160 | tf_op jit(solution)/shard_map/ppermute | solution.py:197
  30.8 27.9 %copy-start.1 = (bf16[512,512]{1,0:T(8,128)(2,1)S(1)}, bf16[512,512]{1,0:T(8,128)(2,1)}, u32[]{:S(2)}) copy-start(bf16[512,512]{1,0:T(8,128)(2,1)} %w_in_ref.1) | copy-start | bytes 1572868
  30.8 27.9 %copy-start.2 = (bf16[512,512]{1,0:T(8,128)(2,1)S(1)}, bf16[512,512]{1,0:T(8,128)(2,1)}, u32[]{:S(2)}) copy-start(bf16[512,512]{1,0:T(8,128)(2,1)} %w_out_ref.1) | copy-start | bytes 1572868
  30.8 27.9 %copy-start.5 = (f32[512]{0:T(512)S(1)}, f32[512]{0:T(512)}, u32[]{:S(2)}) copy-start(f32[512]{0:T(512)} %param.8) | copy-start | bytes 6148
  60.3 25.1 %copy-start = (bf16[128,1024]{1,0:T(8,128)(2,1)S(1)}, bf16[128,1024]{1,0:T(8,128)(2,1)}, u32[]{:S(2)}) copy-start(bf16[128,1024]{1,0:T(8,128)(2,1)} %adjacency.1) | copy-start | bytes 786436
  100.0 37.2 %copy-start.3 = (bf16[128,512]{1,0:T(8,128)(2,1)S(1)}, bf16[128,512]{1,0:T(8,128)(2,1)}, u32[]{:S(2)}) copy-start(bf16[128,512]{1,0:T(8,128)(2,1)} %nodes.1) | copy-start | bytes 393220
  101.3 17.3 %all-to-all-start.4 = ((bf16[64,16,128]{2,1,0:T(8,128)(2,1)}), bf16[64,16,128]{2,1,0:T(8,128)(2,1)S(1)}, u32[]{:S(2)}, u32[]{:S(2)}) async-start(bf16[64,16,128]{2,1,0:T(8,128)(2,1)} %get-tuple-element.18), calls=%async_computation.4 | async-start | bytes 524288 | tf_op jit(solution)/shard_map/all_to_all | solution.py:215
  105.9 8.1 %collective-permute-start.1 = (bf16[16,512]{1,0:T(8,128)(2,1)S(1)}, bf16[16,512]{1,0:T(8,128)(2,1)S(1)}, u32[]{:S(2)}, u32[]{:S(2)}) collective-permute-start(bf16[16,512]{1,0:T(8,128)(2,1)S(1)} %get-tuple-element.20), channel_id=1, source_target_pairs={{0,0},{8,1},{16,2},{24,3},{32,4},{40,5},{48,6},{56,7},{64,8},{72,9... | collective-permute-start | bytes 49160 | tf_op jit(solution)/shard_map/ppermute | solution.py:209
  129.3 8.0 %collective-permute-start.2 = (bf16[4,640,128]{2,1,0:T(8,128)(2,1)S(1)}, bf16[4,640,128]{2,1,0:T(8,128)(2,1)S(1)}, u32[]{:S(2)}, u32[]{:S(2)}) collective-permute-start(bf16[4,640,128]{2,1,0:T(8,128)(2,1)S(1)} %all_to_all.33.mine), channel_id=1, source_target_pairs={{0,1},{1,0},{2,3},{3,2},{4,5},{5,4},{6,7},{7,6},{8,9},{9,8},{10,11... | collective-permute-start | bytes 1966088 | tf_op jit(solution)/shard_map/ppermute | solution.py:218

commit v7 on v4

v7 whole, which is shorter than its diff:
```python
import jax
import jax.numpy as jnp
from jax import lax
from jax.experimental import pallas as pl
from jax.experimental.pallas import tpu as pltpu
from jax.sharding import PartitionSpec as P


BF = jnp.bfloat16
F32 = jnp.float32
ALL = ("rows", "rep")


def place(u, v, p):
    z, y = (v, u) if p % 2 == 0 else (u, v)
    return (8 * z + y) * 8 + p


E8 = range(8)
ALONG_U = [[place(u, v, p) for u in E8] for v in E8 for p in E8]
ALONG_V = [[place(u, v, p) for v in E8] for u in E8 for p in E8]
OUT = [((8 * z + y) * 8 + t, place(t, y, z)) for z in E8 for y in E8 for t in E8]
BACK = [(b, a) for a, b in OUT]
CORE = [(i, i ^ 1) for i in range(512)]
SHIFT_X = [[(i, (i & ~7) | ((i + 2 * d) & 7)) for i in range(512)] for d in (1, 2, 3)]


def dot(a, b, ca, cb):
    return lax.dot_general(a, b, (((ca,), (cb,)), ((), ())), preferred_element_type=F32)


def trade(x, groups):
    return lax.all_to_all(x, ALL, 0, 0, axis_index_groups=groups)


def call(body, outs, *args, scratch=()):
    return pl.pallas_call(
        body,
        out_shape=[jax.ShapeDtypeStruct(s, d) for s, d in outs],
        in_specs=[pl.BlockSpec(memory_space=pltpu.VMEM)] * len(args),
        out_specs=[pl.BlockSpec(memory_space=pltpu.VMEM)] * len(outs),
        scratch_shapes=list(scratch),
        compiler_params=pltpu.CompilerParams(vmem_limit_bytes=40 * 1024 * 1024),
    )(*args)


def is_core_0():
    return (lax.axis_index("rep") & 1) == 0


def left_half():
    return lax.broadcasted_iota(jnp.int32, (1, 128), 1) < 64


def total_of(got):
    total = got[0].astype(F32)
    for i in range(1, 8):
        total = total + got[i].astype(F32)
    return total


def sum_and_copy(got, cot, send):
    total, piece = total_of(got).astype(BF), cot[...]
    for u in E8:
        send[u, 0:128, :] = total
        send[u, 128:144, :] = piece


def update(got, gain_ref, w_in_ref, w_out_ref, out_ref, send, change, rows, columns):
    summed = got[0, 0:128, :].astype(F32)
    for i in range(1, 8):
        summed = summed + got[i, 0:128, :].astype(F32)
    r = lax.axis_index("rows")
    first = is_core_0()
    u = jnp.where(first, r & 7, r >> 3)
    gain = gain_ref[...]
    w_in, w_out = w_in_ref[...], w_out_ref[...]
    cot = got[:, 128:144, :].reshape(128, 512)
    scale = lax.rsqrt(jnp.mean(summed * summed, axis=-1, keepdims=True) + 1e-05)
    normed = summed * scale
    lifted = (normed * gain).astype(BF)
    pre = dot(lifted, w_in, 1, 0)
    grad_hidden = dot(cot, w_out, 1, 1)
    sigma = jax.nn.sigmoid(pre)
    hidden = (pre * sigma).astype(BF)
    grad_pre = (grad_hidden * sigma * (1.0 + pre * (1.0 - sigma))).astype(BF)
    grad_lifted = dot(grad_pre, w_in, 1, 1)
    change[...] = dot(hidden, w_out, 1, 0).astype(BF)
    out_ref[...] = change[pl.ds(pl.multiple_of(u * 16, 16), 16), :]
    gain_row = jnp.sum(grad_lifted * normed, axis=0, keepdims=True)
    gain_high = gain_row.astype(BF).astype(F32)
    gain_rows = jnp.concatenate([gain_high, gain_row - gain_high, jnp.zeros((14, 512), F32)], axis=0).astype(BF)
    grad_normed = grad_lifted * gain
    grad_summed = (
        scale * (grad_normed - normed * jnp.mean(grad_normed * normed, axis=-1, keepdims=True))
    ).astype(BF)
    for v in E8:
        send[v, 0:128, :] = grad_summed
        send[v, 160:176, :] = gain_rows
    left = left_half()

    def pairs(a, b, ref):
        a, b = a.astype(F32), b.astype(F32)
        for m in range(4):
            one, two = a[:, 128 * m : 128 * m + 128], b[:, 128 * m : 128 * m + 128]
            ref[2 * m] = jnp.where(left, one, pltpu.roll(two, 64, 1)).astype(BF)
            ref[2 * m + 1] = jnp.where(left, pltpu.roll(one, 64, 1), two).astype(BF)

    pairs(lifted, hidden, rows)
    pairs(grad_pre, cot, columns)
    for k in E8:
        tile = dot(rows[jnp.where(first, k, u)], columns[jnp.where(first, u, k)], 0, 0)
        tile = jnp.where(left, tile[0:64], tile[64:128])
        high = tile.astype(BF)
        low = (tile - high.astype(F32)).astype(BF)
        for j in range(4):
            at = slice(128 * j, 128 * j + 128)
            send[k, 128:144, at] = high[16 * j : 16 * j + 16]
            send[k, 144:160, at] = low[16 * j : 16 * j + 16]


def back_and_tile(adjacency, got, nodes, change, send, out):
    own = nodes[pl.ds(pl.multiple_of(lax.axis_index("rep") * 16, 16), 16), :].astype(F32)
    final = (own + change[...].astype(F32)).astype(BF)
    for j in range(4):
        out[16 * j : 16 * j + 16, :] = final[:, 128 * j : 128 * j + 128]
    field = got[:, 0:128, :].reshape(1024, 512)
    back = dot(adjacency[...], field, 1, 0)
    for q in E8:
        for j in range(4):
            send[q, 16 * j : 16 * j + 16, :] = back[16 * q : 16 * q + 16, 128 * j : 128 * j + 128].astype(BF)
    exact = jnp.zeros((32, 512), F32)
    for v in E8:
        low = jnp.concatenate([got[v, 144:160, :], jnp.zeros((16, 512), BF)], axis=0)
        exact = exact + (jnp.concatenate([got[v, 128:144, :], got[v, 160:176, :]], axis=0).astype(F32) + low.astype(F32))
    gain = exact[16:17] + exact[17:18]
    gain = jnp.concatenate([gain[:, 128 * j : 128 * j + 128] for j in range(4)] + [jnp.zeros((4, 128), F32)], axis=0)
    high = exact[0:16].astype(BF)
    low = (exact[0:16] - high.astype(F32)).astype(BF)
    gain_high = gain.astype(BF).astype(F32)
    gain = jnp.concatenate([gain_high, gain - gain_high], axis=0).astype(BF)
    for q in E8:
        for i in range(2):
            j = 2 * (q % 2) + i
            send[q, 64 + 16 * i : 80 + 16 * i, :] = high[:, 128 * j : 128 * j + 128]
            send[q, 96 + 16 * i : 112 + 16 * i, :] = low[:, 128 * j : 128 * j + 128]
        send[q, 128:144, :] = gain


def add_up(got, cotangent, out, piece, send, gain):
    total = total_of(got)
    own = cotangent[pl.ds(pl.multiple_of(lax.axis_index("rep") * 16, 16), 16), :].astype(F32)
    for j in range(4):
        piece[16 * j : 16 * j + 16, :] = (
            own[:, 128 * j : 128 * j + 128] + total[16 * j : 16 * j + 16]
        ).astype(BF)
    piece[64:128, :] = out[...]
    block = (total[64:96] + total[96:128]).astype(BF)
    for r in range(64):
        send[r] = block
    gain[...] = total[128:136] + total[136:144]


def lay_rows(src, z, grad_in, grad_out):
    left = left_half()
    for m in range(4):
        even, odd = src[8 * z + 2 * m].astype(F32), src[8 * z + 2 * m + 1].astype(F32)
        cols = slice(128 * m, 128 * m + 128)
        grad_in[z, :, cols] = jnp.where(left, even, pltpu.roll(odd, 64, 1))
        grad_out[z, :, cols] = jnp.where(left, pltpu.roll(even, 64, 1), odd)


def lay(src, p0, p1, p2, p3, grad_in, grad_out, node_grad, node_out):
    for z in E8:
        lay_rows(src, z, grad_in, grad_out)
    p = lax.axis_index("rep")
    c = p & 1
    for d, pieces in enumerate((p0, p1, p2, p3)):
        for h in range(2):
            q = (((p >> 1) + 4 - d) & 3) * 2 + (c ^ h)
            rows = pl.ds(pl.multiple_of(16 * q, 16), 16)
            for j in range(4):
                cols = slice(128 * j, 128 * j + 128)
                node_grad[rows, cols] = pieces[h, 16 * j : 16 * j + 16, :]
                node_out[rows, cols] = pieces[h, 64 + 16 * j : 80 + 16 * j, :]


def lay_both(src, mine_in, mine_out, grad_in, grad_out, part_in, part_out, sems):
    c = lax.axis_index("rep") & 1
    copies = []

    def send(a, b, z, at):
        copies.append(pltpu.make_async_copy(a.at[z], b.at[z, at], sems.at[len(copies)]))
        copies[-1].start()

    for z in E8:
        send(mine_in, grad_in, z, c)
        send(mine_out, grad_out, z, c)
    for z in E8:
        lay_rows(src, z, part_in, part_out)
        send(part_in, grad_in, z, 1 - c)
        send(part_out, grad_out, z, 1 - c)
    for copy in copies:
        copy.wait()


def shards(nodes, adjacency, gain, w_in, w_out, cotangent):
    piece = lax.dynamic_slice_in_dim(cotangent, lax.axis_index("rep") * 16, 16, 0)
    cot = lax.ppermute(piece, ALL, OUT)

    part = dot(adjacency, nodes, 0, 0).astype(BF).reshape(8, 128, 512)
    (part,) = call(sum_and_copy, [((8, 144, 512), BF)], trade(part, ALONG_V), cot)
    got = trade(part, ALONG_U)

    change, send = call(
        update,
        [((16, 512), BF), ((8, 176, 512), BF)],
        got, gain.reshape(1, 512), w_in, w_out,
        scratch=[pltpu.VMEM((128, 512), BF)] + [pltpu.VMEM((8, 128, 128), BF)] * 2,
    )
    change = lax.ppermute(change, ALL, BACK)
    send, out = call(
        back_and_tile, [((8, 144, 128), BF), ((64, 128), BF)],
        adjacency, trade(send, ALONG_V), nodes, change,
    )
    piece, send, grad_gain = call(
        add_up, [((128, 128), BF), ((64, 32, 128), BF), ((8, 128), F32)],
        lax.all_to_all(send, "rep", 0, 0), cotangent, out,
    )
    mine = lax.all_to_all(send, "rows", 0, 0)
    pieces = jnp.stack([piece, lax.ppermute(piece, ALL, CORE)])
    pieces = [pieces] + [lax.ppermute(pieces, ALL, perm) for perm in SHIFT_X]
    mine, pieces = lax.optimization_barrier((mine, pieces))
    other = lax.ppermute(mine, ALL, CORE)
    half = ((8, 32, 512), F32)
    mine_in, mine_out, node_grad, node_out = call(
        lay, [half, half, ((128, 512), BF), ((128, 512), BF)], mine, *pieces
    )
    whole = jax.ShapeDtypeStruct((8, 2, 32, 512), F32)
    vmem = pl.BlockSpec(memory_space=pltpu.VMEM)
    grad_in, grad_out = pl.pallas_call(
        lay_both,
        out_shape=[whole, whole],
        in_specs=[vmem] * 3,
        out_specs=[pl.BlockSpec(memory_space=pl.ANY)] * 2,
        scratch_shapes=[pltpu.VMEM(*half)] * 2 + [pltpu.SemaphoreType.DMA((32,))],
        compiler_params=pltpu.CompilerParams(vmem_limit_bytes=40 * 1024 * 1024),
    )(other, mine_in, mine_out)
    return (node_out, node_grad, grad_in.reshape(512, 512), grad_out.reshape(512, 512), grad_gain[:4].reshape(512))


def solution(mesh):
    return jax.shard_map(
        shards,
        mesh=mesh,
        in_specs=(P("rows", None), P("rows", "rep"), P(), P(), P(), P("rows", None)),
        out_specs=(P("rows", None), P("rows", None), P(), P(), P()),
        check_vma=False,
    )
```

time: 140 us -> 135 us (0.964)
  starting transfers between devices: 38.3 us -> 46 us
  blocking collectives: 50.2 us -> 42.8 us
  waiting for transfers between devices: 41.7 us -> 35.5 us
    ppermute x1 -> x5, starting transfers between devices: 7.26 us -> 17.8 us  [the longest x3 7.8 us: shards(): pieces = [pieces] + [lax.ppermute(pieces, ALL, perm) for perm in SHIFT_X]]
    all_to_all x2 -> x1, blocking collectives: 34.9 us -> 27.8 us  [trade(): return lax.all_to_all(x, ALL, 0, 0, axis_index_groups=groups)]
    ppermute x1 -> x5, waiting for transfers between devices: 12 us -> 17.4 us  [the longest x1 12 us: shards(): cot = lax.ppermute(piece, ALL, OUT)]
    all_to_all x2, starting transfers between devices: 16.7 us -> 12.4 us  [trade(): return lax.all_to_all(x, ALL, 0, 0, axis_index_groups=groups)]
    all_to_all x2, waiting for transfers between devices: 19.4 us -> 15.2 us  [trade(): return lax.all_to_all(x, ALL, 0, 0, axis_index_groups=groups)]
    all_to_all x1, waiting for transfers between devices: 4.84 us -> 1.41 us  [shards(): mine = lax.all_to_all(send, 'rows', 0, 0)]
    ppermute x1, waiting for transfers between devices: 4.35 us -> 1.46 us  [shards(): change = lax.ppermute(change, ALL, BACK)]
    ppermute x1, starting transfers between devices: 3.77 us -> 5.79 us  [shards(): change = lax.ppermute(change, ALL, BACK)]
  transfers between devices with their start and end apart: 6 -> 10, of which waited for: 5 -> 7; matrix products, arithmetic and copies ran while one was open for 0% -> 0% of each run, Pallas kernels for 0% -> 1%
where the time goes in v7:
time: 135 us; the launch traced here: 134 us
  starting transfers between devices  46 us (34%)
  blocking collectives  42.8 us (32%)
  waiting for transfers between devices  35.5 us (26%)
  Pallas kernels  6.03 us (4%)
  matrix products  2.45 us (2%)
    all_to_all x1, blocking collectives, trade(): return lax.all_to_all(x, ALL, 0, 0, axis_index_groups=groups)  27.8 us
    all_to_all x2, waiting for transfers between devices, trade(): return lax.all_to_all(x, ALL, 0, 0, axis_index_groups=groups)  15.2 us
    all_to_all x1, blocking collectives, shards(): lax.all_to_all(send, 'rep', 0, 0)  14.9 us
    all_to_all x2, starting transfers between devices, trade(): return lax.all_to_all(x, ALL, 0, 0, axis_index_groups=groups)  12.4 us
    ppermute x1, waiting for transfers between devices, shards(): cot = lax.ppermute(piece, ALL, OUT)  12 us
    ppermute x3, starting transfers between devices, shards(): pieces = [pieces] + [lax.ppermute(pieces, ALL, perm) for perm in SHIFT_X]  7.8 us
    ppermute x1, starting transfers between devices, shards(): cot = lax.ppermute(piece, ALL, OUT)  7.26 us
    ppermute x1, starting transfers between devices, shards(): change = lax.ppermute(change, ALL, BACK)  5.79 us
  transfers between devices with their start and end apart: 10, of which 7 were waited for; matrix products, arithmetic and copies ran while one was open for 0% of the time, Pallas kernels for 1%

profile of v7, /device:TPU:1, one launch (start us, length us, event | category | flops | bytes accessed | tf_op | source)
XLA Modules:
  0.0 134.1 jit_solution(7652189004286482075)
XLA Ops:
  0.6 2.4 %convolution_convert_fusion = bf16[1024,512]{1,0:T(8,128)(2,1)} fusion(bf16[128,1024]{1,0:T(8,128)(2,1)} %adjacency.1, bf16[128,512]{1,0:T(8,128)(2,1)} %nodes.1), kind=kOutput, calls=%fused_computation | convolution fusion | flops 134742016 | bytes 1441792 | tf_op jit(solution)/shard_map/dot_general | solution.py:29
  3.1 7.7 %all-to-all-start = ((bf16[8,128,512]{2,1,0:T(8,128)(2,1)}), bf16[8,128,512]{2,1,0:T(8,128)(2,1)S(1)}, u32[]{:S(2)}, u32[]{:S(2)}) async-start(bf16[8,128,512]{2,1,0:T(8,128)(2,1)} %bitcast), calls=%async_computation | async-start | bytes 2097152 | tf_op jit(solution)/shard_map/all_to_all | solution.py:33
  10.8 7.3 %collective-permute-start = (bf16[16,512]{1,0:T(8,128)(2,1)S(1)}, bf16[16,512]{1,0:T(8,128)(2,1)S(1)}, u32[]{:S(2)}, u32[]{:S(2)}) collective-permute-start(bf16[16,512]{1,0:T(8,128)(2,1)S(1)} %constant_dynamic-slice_fusion), channel_id=1, source_target_pairs={{0,0},{1,8},{2,16},{3,24},{4,32},{5,40},{6,48},{7,56},{8,64},{9,72... | collective-permute-start | bytes 49160 | tf_op jit(solution)/shard_map/ppermute | solution.py:209
  18.0 12.0 %collective-permute-done.cot = bf16[16,512]{1,0:T(8,128)(2,1)S(1)} collective-permute-done((bf16[16,512]{1,0:T(8,128)(2,1)S(1)}, bf16[16,512]{1,0:T(8,128)(2,1)S(1)}, u32[]{:S(2)}, u32[]{:S(2)}) %collective-permute-start) | collective-permute-done | bytes 16416 | tf_op jit(solution)/shard_map/ppermute | solution.py:209
  30.2 27.8 %all_to_all.25.got = bf16[8,144,512]{2,1,0:T(8,128)(2,1)S(1)} all-to-all(bf16[8,144,512]{2,1,0:T(8,128)(2,1)S(1)} %shard_map.101), channel_id=1, replica_groups={{0,8,16,24,32,40,48,56},{1,65,129,193,257,321,385,449},{2,10,18,26,34,4..., dimensions={0} | all-to-all | bytes 2359296 | tf_op jit(solution)/shard_map/all_to_all | solution.py:33
  58.0 2.3 %shard_map.102 = (bf16[16,512]{1,0:T(8,128)(2,1)S(1)}, bf16[8,176,512]{2,1,0:T(8,128)(2,1)}) custom-call(bf16[8,144,512]{2,1,0:T(8,128)(2,1)S(1)} %all_to_all.25.got, f32[1,512]{1,0:T(1,128)S(1)} %bitcast.11, bf16[512,512]{1,0:T(8,128)(2,1)S(1)} %copy-done.2, bf16[512,512]{1,0:T(8,128)(2,1)S(1)} %copy-done.3), custom_call_target="tpu_custom_call" | custom-call | tf_op jit(solution)/shard_map/pallas_call | solution.py:37
  60.3 4.7 %all-to-all-start.2 = ((bf16[8,176,512]{2,1,0:T(8,128)(2,1)}), bf16[8,176,512]{2,1,0:T(8,128)(2,1)S(1)}, u32[]{:S(2)}, u32[]{:S(2)}) async-start(bf16[8,176,512]{2,1,0:T(8,128)(2,1)} %get-tuple-element.23), calls=%async_computation.2 | async-start | bytes 2883584 | tf_op jit(solution)/shard_map/all_to_all | solution.py:33
  65.0 5.8 %collective-permute-start.1 = (bf16[16,512]{1,0:T(8,128)(2,1)S(1)}, bf16[16,512]{1,0:T(8,128)(2,1)S(1)}, u32[]{:S(2)}, u32[]{:S(2)}) collective-permute-start(bf16[16,512]{1,0:T(8,128)(2,1)S(1)} %get-tuple-element.24), channel_id=1, source_target_pairs={{0,0},{8,1},{16,2},{24,3},{32,4},{40,5},{48,6},{56,7},{64,8},{72,9... | collective-permute-start | bytes 49160 | tf_op jit(solution)/shard_map/ppermute | solution.py:221
  70.8 1.5 %collective-permute-done.1.change = bf16[16,512]{1,0:T(8,128)(2,1)S(1)} collective-permute-done((bf16[16,512]{1,0:T(8,128)(2,1)S(1)}, bf16[16,512]{1,0:T(8,128)(2,1)S(1)}, u32[]{:S(2)}, u32[]{:S(2)}) %collective-permute-start.1) | collective-permute-done | bytes 16416 | tf_op jit(solution)/shard_map/ppermute | solution.py:221
  72.3 15.2 %all-to-all-done.2.got = bf16[8,176,512]{2,1,0:T(8,128)(2,1)S(1)} async-done(((bf16[8,176,512]{2,1,0:T(8,128)(2,1)}), bf16[8,176,512]{2,1,0:T(8,128)(2,1)S(1)}, u32[]{:S(2)}, u32[]{:S(2)}) %all-to-all-start.2) | async-done | bytes 1441824 | tf_op jit(solution)/shard_map/all_to_all | solution.py:33
  87.8 14.9 %all_to_all.26.got = bf16[8,144,128]{2,1,0:T(8,128)(2,1)S(1)} all-to-all(bf16[8,144,128]{2,1,0:T(8,128)(2,1)S(1)} %get-tuple-element.25), channel_id=1, replica_groups=mesh['rows'=64,'rep'=8] {'rep'}, dimensions={0} | all-to-all | bytes 589824 | tf_op jit(solution)/shard_map/all_to_all | solution.py:228
  102.7 0.8 shard_map.104
  103.5 4.9 %all-to-all-start.4 = ((bf16[64,32,128]{2,1,0:T(8,128)(2,1)}), bf16[64,32,128]{2,1,0:T(8,128)(2,1)S(1)}, u32[]{:S(2)}, u32[]{:S(2)}) async-start(bf16[64,32,128]{2,1,0:T(8,128)(2,1)} %get-tuple-element.27), calls=%async_computation.4 | async-start | bytes 1048576 | tf_op jit(solution)/shard_map/all_to_all | solution.py:230
  108.4 2.8 %collective-permute-start.2 = (bf16[128,128]{1,0:T(8,128)(2,1)S(1)}, bf16[128,128]{1,0:T(8,128)(2,1)S(1)}, u32[]{:S(2)}, u32[]{:S(2)}) collective-permute-start(bf16[128,128]{1,0:T(8,128)(2,1)S(1)} %get-tuple-element.28), channel_id=1, source_target_pairs={{0,1},{1,0},{2,3},{3,2},{4,5},{5,4},{6,7},{7,6},{8,9},{9,8},{10,11... | collective-permute-start | bytes 98312 | tf_op jit(solution)/shard_map/ppermute | solution.py:231
  111.2 0.8 collective-permute-done.2
  112.1 2.8 %collective-permute-start.5 = (bf16[2,128,128]{2,1,0:T(8,128)(2,1)S(1)}, bf16[2,128,128]{2,1,0:T(8,128)(2,1)S(1)}, u32[]{:S(2)}, u32[]{:S(2)}) collective-permute-start(bf16[2,128,128]{2,1,0:T(8,128)(2,1)S(1)} %pad_maximum_fusion.p0), channel_id=1, source_target_pairs={{0,6},{1,7},{2,0},{3,1},{4,2},{5,3},{6,4},{7,5},{8,14},{9,15},{10,... | collective-permute-start | bytes 196616 | tf_op jit(solution)/shard_map/ppermute | solution.py:232
  114.8 3.1 %collective-permute-start.4 = (bf16[2,128,128]{2,1,0:T(8,128)(2,1)S(1)}, bf16[2,128,128]{2,1,0:T(8,128)(2,1)S(1)}, u32[]{:S(2)}, u32[]{:S(2)}) collective-permute-start(bf16[2,128,128]{2,1,0:T(8,128)(2,1)S(1)} %pad_maximum_fusion.p0), channel_id=1, source_target_pairs={{0,4},{1,5},{2,6},{3,7},{4,0},{5,1},{6,2},{7,3},{8,12},{9,13},{10,... | collective-permute-start | bytes 196616 | tf_op jit(solution)/shard_map/ppermute | solution.py:232
  117.9 1.9 %collective-permute-start.3 = (bf16[2,128,128]{2,1,0:T(8,128)(2,1)S(1)}, bf16[2,128,128]{2,1,0:T(8,128)(2,1)S(1)}, u32[]{:S(2)}, u32[]{:S(2)}) collective-permute-start(bf16[2,128,128]{2,1,0:T(8,128)(2,1)S(1)} %pad_maximum_fusion.p0), channel_id=1, source_target_pairs={{0,2},{1,3},{2,4},{3,5},{4,6},{5,7},{6,0},{7,1},{8,10},{9,11},{10,... | collective-permute-start | bytes 196616 | tf_op jit(solution)/shard_map/ppermute | solution.py:232
  119.9 1.8 %collective-permute-done.4.p2 = bf16[2,128,128]{2,1,0:T(8,128)(2,1)S(1)} collective-permute-done((bf16[2,128,128]{2,1,0:T(8,128)(2,1)S(1)}, bf16[2,128,128]{2,1,0:T(8,128)(2,1)S(1)}, u32[]{:S(2)}, u32[]{:S(2)}) %collective-permute-start.4) | collective-permute-done | bytes 65568 | tf_op jit(solution)/shard_map/ppermute | solution.py:232
  121.7 2.8 %collective-permute-done.3.p1 = bf16[2,128,128]{2,1,0:T(8,128)(2,1)S(1)} collective-permute-done((bf16[2,128,128]{2,1,0:T(8,128)(2,1)S(1)}, bf16[2,128,128]{2,1,0:T(8,128)(2,1)S(1)}, u32[]{:S(2)}, u32[]{:S(2)}) %collective-permute-start.3) | collective-permute-done | bytes 65568 | tf_op jit(solution)/shard_map/ppermute | solution.py:232
  124.5 1.4 %all-to-all-done.4.src = bf16[64,32,128]{2,1,0:T(8,128)(2,1)S(1)} async-done(((bf16[64,32,128]{2,1,0:T(8,128)(2,1)}), bf16[64,32,128]{2,1,0:T(8,128)(2,1)S(1)}, u32[]{:S(2)}, u32[]{:S(2)}) %all-to-all-start.4) | async-done | bytes 524320 | tf_op jit(solution)/shard_map/all_to_all | solution.py:230
  125.9 5.2 %collective-permute-start.6 = (bf16[64,32,128]{2,1,0:T(8,128)(2,1)S(1)}, bf16[64,32,128]{2,1,0:T(8,128)(2,1)S(1)}, u32[]{:S(2)}, u32[]{:S(2)}) collective-permute-start(bf16[64,32,128]{2,1,0:T(8,128)(2,1)S(1)} %all-to-all-done.4.src), channel_id=1, source_target_pairs={{0,1},{1,0},{2,3},{3,2},{4,5},{5,4},{6,7},{7,6},{8,9},{9,8},{10,11... | collective-permute-start | bytes 1572872 | tf_op jit(solution)/shard_map/ppermute | solution.py:234
  131.6 0.9 shard_map.105
  132.6 1.6 %shard_map.106 = (f32[8,2,32,512]{3,2,1,0:T(8,128)}, f32[8,2,32,512]{3,2,1,0:T(8,128)}) custom-call(bf16[64,32,128]{2,1,0:T(8,128)(2,1)S(1)} %collective-permute-done.6.src, f32[8,32,512]{2,1,0:T(8,128)S(1)} %get-tuple-element.36.mine_in, f32[8,32,512]{2,1,0:T(8,128)S(1)} %get-tuple-element.37.mine_out), custom_call_target="tpu_custom_call" | custom-call | tf_op jit(solution)/shard_map/pallas_call | solution.py:241
  (20 shorter events, 1.1 us)
Async XLA Ops:
  0.6 10.1 %copy-start.4 = (bf16[128,512]{1,0:T(8,128)(2,1)S(1)}, bf16[128,512]{1,0:T(8,128)(2,1)}, u32[]{:S(2)}) copy-start(bf16[128,512]{1,0:T(8,128)(2,1)} %cotangent.1) | copy-start | bytes 393220
  3.1 26.9 %all-to-all-start = ((bf16[8,128,512]{2,1,0:T(8,128)(2,1)}), bf16[8,128,512]{2,1,0:T(8,128)(2,1)S(1)}, u32[]{:S(2)}, u32[]{:S(2)}) async-start(bf16[8,128,512]{2,1,0:T(8,128)(2,1)} %bitcast), calls=%async_computation | async-start | bytes 2097152 | tf_op jit(solution)/shard_map/all_to_all | solution.py:33
  10.8 19.2 %collective-permute-start = (bf16[16,512]{1,0:T(8,128)(2,1)S(1)}, bf16[16,512]{1,0:T(8,128)(2,1)S(1)}, u32[]{:S(2)}, u32[]{:S(2)}) collective-permute-start(bf16[16,512]{1,0:T(8,128)(2,1)S(1)} %constant_dynamic-slice_fusion), channel_id=1, source_target_pairs={{0,0},{1,8},{2,16},{3,24},{4,32},{5,40},{6,48},{7,56},{8,64},{9,72... | collective-permute-start | bytes 49160 | tf_op jit(solution)/shard_map/ppermute | solution.py:209
  30.1 27.9 %copy-start.2 = (bf16[512,512]{1,0:T(8,128)(2,1)S(1)}, bf16[512,512]{1,0:T(8,128)(2,1)}, u32[]{:S(2)}) copy-start(bf16[512,512]{1,0:T(8,128)(2,1)} %w_in_ref.1) | copy-start | bytes 1572868
  30.2 27.9 %copy-start.3 = (bf16[512,512]{1,0:T(8,128)(2,1)S(1)}, bf16[512,512]{1,0:T(8,128)(2,1)}, u32[]{:S(2)}) copy-start(bf16[512,512]{1,0:T(8,128)(2,1)} %w_out_ref.1) | copy-start | bytes 1572868
  30.2 27.9 %copy-start.5 = (f32[512]{0:T(512)S(1)}, f32[512]{0:T(512)}, u32[]{:S(2)}) copy-start(f32[512]{0:T(512)} %param.8) | copy-start | bytes 6148
  60.3 27.2 %copy-start = (bf16[128,1024]{1,0:T(8,128)(2,1)S(1)}, bf16[128,1024]{1,0:T(8,128)(2,1)}, u32[]{:S(2)}) copy-start(bf16[128,1024]{1,0:T(8,128)(2,1)} %adjacency.1) | copy-start | bytes 786436
  60.3 27.2 %copy-start.1 = (bf16[128,512]{1,0:T(8,128)(2,1)S(1)}, bf16[128,512]{1,0:T(8,128)(2,1)}, u32[]{:S(2)}) copy-start(bf16[128,512]{1,0:T(8,128)(2,1)} %nodes.1) | copy-start | bytes 393220
  60.3 27.2 %all-to-all-start.2 = ((bf16[8,176,512]{2,1,0:T(8,128)(2,1)}), bf16[8,176,512]{2,1,0:T(8,128)(2,1)S(1)}, u32[]{:S(2)}, u32[]{:S(2)}) async-start(bf16[8,176,512]{2,1,0:T(8,128)(2,1)} %get-tuple-element.23), calls=%async_computation.2 | async-start | bytes 2883584 | tf_op jit(solution)/shard_map/all_to_all | solution.py:33
  65.0 7.2 %collective-permute-start.1 = (bf16[16,512]{1,0:T(8,128)(2,1)S(1)}, bf16[16,512]{1,0:T(8,128)(2,1)S(1)}, u32[]{:S(2)}, u32[]{:S(2)}) collective-permute-start(bf16[16,512]{1,0:T(8,128)(2,1)S(1)} %get-tuple-element.24), channel_id=1, source_target_pairs={{0,0},{8,1},{16,2},{24,3},{32,4},{40,5},{48,6},{56,7},{64,8},{72,9... | collective-permute-start | bytes 49160 | tf_op jit(solution)/shard_map/ppermute | solution.py:221
  103.5 22.3 %all-to-all-start.4 = ((bf16[64,32,128]{2,1,0:T(8,128)(2,1)}), bf16[64,32,128]{2,1,0:T(8,128)(2,1)S(1)}, u32[]{:S(2)}, u32[]{:S(2)}) async-start(bf16[64,32,128]{2,1,0:T(8,128)(2,1)} %get-tuple-element.27), calls=%async_computation.4 | async-start | bytes 1048576 | tf_op jit(solution)/shard_map/all_to_all | solution.py:230
  108.4 3.6 %collective-permute-start.2 = (bf16[128,128]{1,0:T(8,128)(2,1)S(1)}, bf16[128,128]{1,0:T(8,128)(2,1)S(1)}, u32[]{:S(2)}, u32[]{:S(2)}) collective-permute-start(bf16[128,128]{1,0:T(8,128)(2,1)S(1)} %get-tuple-element.28), channel_id=1, source_target_pairs={{0,1},{1,0},{2,3},{3,2},{4,5},{5,4},{6,7},{7,6},{8,9},{9,8},{10,11... | collective-permute-start | bytes 98312 | tf_op jit(solution)/shard_map/ppermute | solution.py:231
  112.1 7.8 %collective-permute-start.5 = (bf16[2,128,128]{2,1,0:T(8,128)(2,1)S(1)}, bf16[2,128,128]{2,1,0:T(8,128)(2,1)S(1)}, u32[]{:S(2)}, u32[]{:S(2)}) collective-permute-start(bf16[2,128,128]{2,1,0:T(8,128)(2,1)S(1)} %pad_maximum_fusion.p0), channel_id=1, source_target_pairs={{0,6},{1,7},{2,0},{3,1},{4,2},{5,3},{6,4},{7,5},{8,14},{9,15},{10,... | collective-permute-start | bytes 196616 | tf_op jit(solution)/shard_map/ppermute | solution.py:232
  114.8 6.8 %collective-permute-start.4 = (bf16[2,128,128]{2,1,0:T(8,128)(2,1)S(1)}, bf16[2,128,128]{2,1,0:T(8,128)(2,1)S(1)}, u32[]{:S(2)}, u32[]{:S(2)}) collective-permute-start(bf16[2,128,128]{2,1,0:T(8,128)(2,1)S(1)} %pad_maximum_fusion.p0), channel_id=1, source_target_pairs={{0,4},{1,5},{2,6},{3,7},{4,0},{5,1},{6,2},{7,3},{8,12},{9,13},{10,... | collective-permute-start | bytes 196616 | tf_op jit(solution)/shard_map/ppermute | solution.py:232
  117.9 6.5 %collective-permute-start.3 = (bf16[2,128,128]{2,1,0:T(8,128)(2,1)S(1)}, bf16[2,128,128]{2,1,0:T(8,128)(2,1)S(1)}, u32[]{:S(2)}, u32[]{:S(2)}) collective-permute-start(bf16[2,128,128]{2,1,0:T(8,128)(2,1)S(1)} %pad_maximum_fusion.p0), channel_id=1, source_target_pairs={{0,2},{1,3},{2,4},{3,5},{4,6},{5,7},{6,0},{7,1},{8,10},{9,11},{10,... | collective-permute-start | bytes 196616 | tf_op jit(solution)/shard_map/ppermute | solution.py:232
  125.9 6.7 %collective-permute-start.6 = (bf16[64,32,128]{2,1,0:T(8,128)(2,1)S(1)}, bf16[64,32,128]{2,1,0:T(8,128)(2,1)S(1)}, u32[]{:S(2)}, u32[]{:S(2)}) collective-permute-start(bf16[64,32,128]{2,1,0:T(8,128)(2,1)S(1)} %all-to-all-done.4.src), channel_id=1, source_target_pairs={{0,1},{1,0},{2,3},{3,2},{4,5},{5,4},{6,7},{7,6},{8,9},{9,8},{10,11... | collective-permute-start | bytes 1572872 | tf_op jit(solution)/shard_map/ppermute | solution.py:234

commit v8 on v7

--- a/solution.py
+++ b/solution.py
@@ -89,15 +89,15 @@
     out_ref[...] = change[pl.ds(pl.multiple_of(u * 16, 16), 16), :]
     gain_row = jnp.sum(grad_lifted * normed, axis=0, keepdims=True)
     gain_high = gain_row.astype(BF).astype(F32)
-    gain_rows = jnp.concatenate([gain_high, gain_row - gain_high, jnp.zeros((14, 512), F32)], axis=0).astype(BF)
+    gain_rows = jnp.concatenate([jnp.zeros((14, 512), F32), gain_high, gain_row - gain_high], axis=0)
     grad_normed = grad_lifted * gain
     grad_summed = (
         scale * (grad_normed - normed * jnp.mean(grad_normed * normed, axis=-1, keepdims=True))
     ).astype(BF)
     for v in E8:
         send[v, 0:128, :] = grad_summed
-        send[v, 160:176, :] = gain_rows
     left = left_half()
+    top = lax.broadcasted_iota(jnp.int32, (16, 1), 0) < 14
 
     def pairs(a, b, ref):
         a, b = a.astype(F32), b.astype(F32)
@@ -112,11 +112,11 @@
         tile = dot(rows[jnp.where(first, k, u)], columns[jnp.where(first, u, k)], 0, 0)
         tile = jnp.where(left, tile[0:64], tile[64:128])
         high = tile.astype(BF)
-        low = (tile - high.astype(F32)).astype(BF)
+        low = tile - high.astype(F32)
         for j in range(4):
             at = slice(128 * j, 128 * j + 128)
             send[k, 128:144, at] = high[16 * j : 16 * j + 16]
-            send[k, 144:160, at] = low[16 * j : 16 * j + 16]
+            send[k, 144:160, at] = jnp.where(top, low[16 * j : 16 * j + 16], gain_rows[:, at]).astype(BF)
 
 
 def back_and_tile(adjacency, got, nodes, change, send, out):
@@ -129,14 +129,15 @@
     for q in E8:
         for j in range(4):
             send[q, 16 * j : 16 * j + 16, :] = back[16 * q : 16 * q + 16, 128 * j : 128 * j + 128].astype(BF)
-    exact = jnp.zeros((32, 512), F32)
+    exact, lows = jnp.zeros((16, 512), F32), jnp.zeros((16, 512), F32)
     for v in E8:
-        low = jnp.concatenate([got[v, 144:160, :], jnp.zeros((16, 512), BF)], axis=0)
-        exact = exact + (jnp.concatenate([got[v, 128:144, :], got[v, 160:176, :]], axis=0).astype(F32) + low.astype(F32))
-    gain = exact[16:17] + exact[17:18]
+        exact = exact + got[v, 128:144, :].astype(F32)
+        lows = lows + got[v, 144:160, :].astype(F32)
+    exact = exact + jnp.where(lax.broadcasted_iota(jnp.int32, (16, 1), 0) < 14, lows, 0.0)
+    gain = lows[14:15] + lows[15:16]
     gain = jnp.concatenate([gain[:, 128 * j : 128 * j + 128] for j in range(4)] + [jnp.zeros((4, 128), F32)], axis=0)
-    high = exact[0:16].astype(BF)
-    low = (exact[0:16] - high.astype(F32)).astype(BF)
+    high = exact.astype(BF)
+    low = (exact - high.astype(F32)).astype(BF)
     gain_high = gain.astype(BF).astype(F32)
     gain = jnp.concatenate([gain_high, gain - gain_high], axis=0).astype(BF)
     for q in E8:
@@ -214,7 +215,7 @@
 
     change, send = call(
         update,
-        [((16, 512), BF), ((8, 176, 512), BF)],
+        [((16, 512), BF), ((8, 160, 512), BF)],
         got, gain.reshape(1, 512), w_in, w_out,
         scratch=[pltpu.VMEM((128, 512), BF)] + [pltpu.VMEM((8, 128, 128), BF)] * 2,
     )

time: 135 us -> 133 us (0.985)
  waiting for transfers between devices: 35.5 us -> 34.1 us
where the time goes in v8:
time: 133 us
  starting transfers between devices  46.2 us (35%)
  blocking collectives  42.7 us (32%)
  waiting for transfers between devices  34.1 us (26%)
  Pallas kernels  5.98 us (4%)
  matrix products  2.41 us (2%)
    all_to_all x1, blocking collectives, trade(): return lax.all_to_all(x, ALL, 0, 0, axis_index_groups=groups)  27.8 us
    all_to_all x1, blocking collectives, shards(): lax.all_to_all(send, 'rep', 0, 0)  14.9 us
    all_to_all x2, waiting for transfers between devices, trade(): return lax.all_to_all(x, ALL, 0, 0, axis_index_groups=groups)  14 us
    all_to_all x2, starting transfers between devices, trade(): return lax.all_to_all(x, ALL, 0, 0, axis_index_groups=groups)  12.5 us
    ppermute x1, waiting for transfers between devices, shards(): cot = lax.ppermute(piece, ALL, OUT)  12 us
    ppermute x3, starting transfers between devices, shards(): pieces = [pieces] + [lax.ppermute(pieces, ALL, perm) for perm in SHIFT_X]  7.8 us
    ppermute x1, starting transfers between devices, shards(): cot = lax.ppermute(piece, ALL, OUT)  7.26 us
    ppermute x1, starting transfers between devices, shards(): change = lax.ppermute(change, ALL, BACK)  5.78 us
  transfers between devices with their start and end apart: 10, of which 7 were waited for; matrix products, arithmetic and copies ran while one was open for 0% of the time, Pallas kernels for 1%

profile of v8, /device:TPU:1, one launch (start us, length us, event | category | flops | bytes accessed | tf_op | source)
XLA Modules:
  0.0 132.8 jit_solution(8025756298936747584)
XLA Ops:
  0.6 2.4 %convolution_convert_fusion = bf16[1024,512]{1,0:T(8,128)(2,1)} fusion(bf16[128,1024]{1,0:T(8,128)(2,1)} %adjacency.1, bf16[128,512]{1,0:T(8,128)(2,1)} %nodes.1), kind=kOutput, calls=%fused_computation | convolution fusion | flops 134742016 | bytes 1441792 | tf_op jit(solution)/shard_map/dot_general | solution.py:29
  3.0 7.8 %all-to-all-start = ((bf16[8,128,512]{2,1,0:T(8,128)(2,1)}), bf16[8,128,512]{2,1,0:T(8,128)(2,1)S(1)}, u32[]{:S(2)}, u32[]{:S(2)}) async-start(bf16[8,128,512]{2,1,0:T(8,128)(2,1)} %bitcast), calls=%async_computation | async-start | bytes 2097152 | tf_op jit(solution)/shard_map/all_to_all | solution.py:33
  10.8 7.3 %collective-permute-start = (bf16[16,512]{1,0:T(8,128)(2,1)S(1)}, bf16[16,512]{1,0:T(8,128)(2,1)S(1)}, u32[]{:S(2)}, u32[]{:S(2)}) collective-permute-start(bf16[16,512]{1,0:T(8,128)(2,1)S(1)} %constant_dynamic-slice_fusion), channel_id=1, source_target_pairs={{0,0},{1,8},{2,16},{3,24},{4,32},{5,40},{6,48},{7,56},{8,64},{9,72... | collective-permute-start | bytes 49160 | tf_op jit(solution)/shard_map/ppermute | solution.py:210
  18.1 12.0 %collective-permute-done.cot = bf16[16,512]{1,0:T(8,128)(2,1)S(1)} collective-permute-done((bf16[16,512]{1,0:T(8,128)(2,1)S(1)}, bf16[16,512]{1,0:T(8,128)(2,1)S(1)}, u32[]{:S(2)}, u32[]{:S(2)}) %collective-permute-start) | collective-permute-done | bytes 16416 | tf_op jit(solution)/shard_map/ppermute | solution.py:210
  30.3 27.8 %all_to_all.25.got = bf16[8,144,512]{2,1,0:T(8,128)(2,1)S(1)} all-to-all(bf16[8,144,512]{2,1,0:T(8,128)(2,1)S(1)} %shard_map.101), channel_id=1, replica_groups={{0,8,16,24,32,40,48,56},{1,65,129,193,257,321,385,449},{2,10,18,26,34,4..., dimensions={0} | all-to-all | bytes 2359296 | tf_op jit(solution)/shard_map/all_to_all | solution.py:33
  58.1 2.2 %shard_map.102 = (bf16[16,512]{1,0:T(8,128)(2,1)S(1)}, bf16[8,160,512]{2,1,0:T(8,128)(2,1)}) custom-call(bf16[8,144,512]{2,1,0:T(8,128)(2,1)S(1)} %all_to_all.25.got, f32[1,512]{1,0:T(1,128)S(1)} %bitcast.11, bf16[512,512]{1,0:T(8,128)(2,1)S(1)} %copy-done.1, bf16[512,512]{1,0:T(8,128)(2,1)S(1)} %copy-done.2), custom_call_target="tpu_custom_call" | custom-call | tf_op jit(solution)/shard_map/pallas_call | solution.py:37
  60.4 4.7 %all-to-all-start.2 = ((bf16[8,160,512]{2,1,0:T(8,128)(2,1)}), bf16[8,160,512]{2,1,0:T(8,128)(2,1)S(1)}, u32[]{:S(2)}, u32[]{:S(2)}) async-start(bf16[8,160,512]{2,1,0:T(8,128)(2,1)} %get-tuple-element.23), calls=%async_computation.2 | async-start | bytes 2621440 | tf_op jit(solution)/shard_map/all_to_all | solution.py:33
  65.1 5.8 %collective-permute-start.1 = (bf16[16,512]{1,0:T(8,128)(2,1)S(1)}, bf16[16,512]{1,0:T(8,128)(2,1)S(1)}, u32[]{:S(2)}, u32[]{:S(2)}) collective-permute-start(bf16[16,512]{1,0:T(8,128)(2,1)S(1)} %get-tuple-element.24), channel_id=1, source_target_pairs={{0,0},{8,1},{16,2},{24,3},{32,4},{40,5},{48,6},{56,7},{64,8},{72,9... | collective-permute-start | bytes 49160 | tf_op jit(solution)/shard_map/ppermute | solution.py:222
  70.9 1.3 collective-permute-done.1.change
  72.2 14.0 %all-to-all-done.2.got = bf16[8,160,512]{2,1,0:T(8,128)(2,1)S(1)} async-done(((bf16[8,160,512]{2,1,0:T(8,128)(2,1)}), bf16[8,160,512]{2,1,0:T(8,128)(2,1)S(1)}, u32[]{:S(2)}, u32[]{:S(2)}) %all-to-all-start.2) | async-done | bytes 1310752 | tf_op jit(solution)/shard_map/all_to_all | solution.py:33
  86.4 14.9 %all_to_all.26.got = bf16[8,144,128]{2,1,0:T(8,128)(2,1)S(1)} all-to-all(bf16[8,144,128]{2,1,0:T(8,128)(2,1)S(1)} %get-tuple-element.25), channel_id=1, replica_groups=mesh['rows'=64,'rep'=8] {'rep'}, dimensions={0} | all-to-all | bytes 589824 | tf_op jit(solution)/shard_map/all_to_all | solution.py:229
  101.3 0.8 shard_map.104
  102.2 4.9 %all-to-all-start.4 = ((bf16[64,32,128]{2,1,0:T(8,128)(2,1)}), bf16[64,32,128]{2,1,0:T(8,128)(2,1)S(1)}, u32[]{:S(2)}, u32[]{:S(2)}) async-start(bf16[64,32,128]{2,1,0:T(8,128)(2,1)} %get-tuple-element.27), calls=%async_computation.4 | async-start | bytes 1048576 | tf_op jit(solution)/shard_map/all_to_all | solution.py:231
  107.1 2.8 %collective-permute-start.2 = (bf16[128,128]{1,0:T(8,128)(2,1)S(1)}, bf16[128,128]{1,0:T(8,128)(2,1)S(1)}, u32[]{:S(2)}, u32[]{:S(2)}) collective-permute-start(bf16[128,128]{1,0:T(8,128)(2,1)S(1)} %get-tuple-element.28), channel_id=1, source_target_pairs={{0,1},{1,0},{2,3},{3,2},{4,5},{5,4},{6,7},{7,6},{8,9},{9,8},{10,11... | collective-permute-start | bytes 98312 | tf_op jit(solution)/shard_map/ppermute | solution.py:232
  109.8 0.8 collective-permute-done.2
  110.7 2.8 %collective-permute-start.5 = (bf16[2,128,128]{2,1,0:T(8,128)(2,1)S(1)}, bf16[2,128,128]{2,1,0:T(8,128)(2,1)S(1)}, u32[]{:S(2)}, u32[]{:S(2)}) collective-permute-start(bf16[2,128,128]{2,1,0:T(8,128)(2,1)S(1)} %pad_maximum_fusion.p0), channel_id=1, source_target_pairs={{0,6},{1,7},{2,0},{3,1},{4,2},{5,3},{6,4},{7,5},{8,14},{9,15},{10,... | collective-permute-start | bytes 196616 | tf_op jit(solution)/shard_map/ppermute | solution.py:233
  113.5 3.1 %collective-permute-start.4 = (bf16[2,128,128]{2,1,0:T(8,128)(2,1)S(1)}, bf16[2,128,128]{2,1,0:T(8,128)(2,1)S(1)}, u32[]{:S(2)}, u32[]{:S(2)}) collective-permute-start(bf16[2,128,128]{2,1,0:T(8,128)(2,1)S(1)} %pad_maximum_fusion.p0), channel_id=1, source_target_pairs={{0,4},{1,5},{2,6},{3,7},{4,0},{5,1},{6,2},{7,3},{8,12},{9,13},{10,... | collective-permute-start | bytes 196616 | tf_op jit(solution)/shard_map/ppermute | solution.py:233
  116.6 1.9 %collective-permute-start.3 = (bf16[2,128,128]{2,1,0:T(8,128)(2,1)S(1)}, bf16[2,128,128]{2,1,0:T(8,128)(2,1)S(1)}, u32[]{:S(2)}, u32[]{:S(2)}) collective-permute-start(bf16[2,128,128]{2,1,0:T(8,128)(2,1)S(1)} %pad_maximum_fusion.p0), channel_id=1, source_target_pairs={{0,2},{1,3},{2,4},{3,5},{4,6},{5,7},{6,0},{7,1},{8,10},{9,11},{10,... | collective-permute-start | bytes 196616 | tf_op jit(solution)/shard_map/ppermute | solution.py:233
  118.5 1.8 %collective-permute-done.4.p2 = bf16[2,128,128]{2,1,0:T(8,128)(2,1)S(1)} collective-permute-done((bf16[2,128,128]{2,1,0:T(8,128)(2,1)S(1)}, bf16[2,128,128]{2,1,0:T(8,128)(2,1)S(1)}, u32[]{:S(2)}, u32[]{:S(2)}) %collective-permute-start.4) | collective-permute-done | bytes 65568 | tf_op jit(solution)/shard_map/ppermute | solution.py:233
  120.3 2.8 %collective-permute-done.3.p1 = bf16[2,128,128]{2,1,0:T(8,128)(2,1)S(1)} collective-permute-done((bf16[2,128,128]{2,1,0:T(8,128)(2,1)S(1)}, bf16[2,128,128]{2,1,0:T(8,128)(2,1)S(1)}, u32[]{:S(2)}, u32[]{:S(2)}) %collective-permute-start.3) | collective-permute-done | bytes 65568 | tf_op jit(solution)/shard_map/ppermute | solution.py:233
  123.1 1.4 %all-to-all-done.4.src = bf16[64,32,128]{2,1,0:T(8,128)(2,1)S(1)} async-done(((bf16[64,32,128]{2,1,0:T(8,128)(2,1)}), bf16[64,32,128]{2,1,0:T(8,128)(2,1)S(1)}, u32[]{:S(2)}, u32[]{:S(2)}) %all-to-all-start.4) | async-done | bytes 524320 | tf_op jit(solution)/shard_map/all_to_all | solution.py:231
  124.5 5.2 %collective-permute-start.6 = (bf16[64,32,128]{2,1,0:T(8,128)(2,1)S(1)}, bf16[64,32,128]{2,1,0:T(8,128)(2,1)S(1)}, u32[]{:S(2)}, u32[]{:S(2)}) collective-permute-start(bf16[64,32,128]{2,1,0:T(8,128)(2,1)S(1)} %all-to-all-done.4.src), channel_id=1, source_target_pairs={{0,1},{1,0},{2,3},{3,2},{4,5},{5,4},{6,7},{7,6},{8,9},{9,8},{10,11... | collective-permute-start | bytes 1572872 | tf_op jit(solution)/shard_map/ppermute | solution.py:235
  130.3 0.9 shard_map.105
  131.2 1.6 %shard_map.106 = (f32[8,2,32,512]{3,2,1,0:T(8,128)}, f32[8,2,32,512]{3,2,1,0:T(8,128)}) custom-call(bf16[64,32,128]{2,1,0:T(8,128)(2,1)S(1)} %collective-permute-done.6.src, f32[8,32,512]{2,1,0:T(8,128)S(1)} %get-tuple-element.36.mine_in, f32[8,32,512]{2,1,0:T(8,128)S(1)} %get-tuple-element.37.mine_out), custom_call_target="tpu_custom_call" | custom-call | tf_op jit(solution)/shard_map/pallas_call | solution.py:242
  (20 shorter events, 1.1 us)
Async XLA Ops:
  3.0 7.8 %copy-start.4 = (bf16[128,512]{1,0:T(8,128)(2,1)S(1)}, bf16[128,512]{1,0:T(8,128)(2,1)}, u32[]{:S(2)}) copy-start(bf16[128,512]{1,0:T(8,128)(2,1)} %cotangent.1) | copy-start | bytes 393220
  3.0 27.0 %all-to-all-start = ((bf16[8,128,512]{2,1,0:T(8,128)(2,1)}), bf16[8,128,512]{2,1,0:T(8,128)(2,1)S(1)}, u32[]{:S(2)}, u32[]{:S(2)}) async-start(bf16[8,128,512]{2,1,0:T(8,128)(2,1)} %bitcast), calls=%async_computation | async-start | bytes 2097152 | tf_op jit(solution)/shard_map/all_to_all | solution.py:33
  10.8 19.2 %collective-permute-start = (bf16[16,512]{1,0:T(8,128)(2,1)S(1)}, bf16[16,512]{1,0:T(8,128)(2,1)S(1)}, u32[]{:S(2)}, u32[]{:S(2)}) collective-permute-start(bf16[16,512]{1,0:T(8,128)(2,1)S(1)} %constant_dynamic-slice_fusion), channel_id=1, source_target_pairs={{0,0},{1,8},{2,16},{3,24},{4,32},{5,40},{6,48},{7,56},{8,64},{9,72... | collective-permute-start | bytes 49160 | tf_op jit(solution)/shard_map/ppermute | solution.py:210
  30.2 27.9 %copy-start.1 = (bf16[512,512]{1,0:T(8,128)(2,1)S(1)}, bf16[512,512]{1,0:T(8,128)(2,1)}, u32[]{:S(2)}) copy-start(bf16[512,512]{1,0:T(8,128)(2,1)} %w_in_ref.1) | copy-start | bytes 1572868
  30.2 27.9 %copy-start.2 = (bf16[512,512]{1,0:T(8,128)(2,1)S(1)}, bf16[512,512]{1,0:T(8,128)(2,1)}, u32[]{:S(2)}) copy-start(bf16[512,512]{1,0:T(8,128)(2,1)} %w_out_ref.1) | copy-start | bytes 1572868
  30.3 27.9 %copy-start.5 = (f32[512]{0:T(512)S(1)}, f32[512]{0:T(512)}, u32[]{:S(2)}) copy-start(f32[512]{0:T(512)} %param.8) | copy-start | bytes 6148
  60.4 25.8 %copy-start = (bf16[128,1024]{1,0:T(8,128)(2,1)S(1)}, bf16[128,1024]{1,0:T(8,128)(2,1)}, u32[]{:S(2)}) copy-start(bf16[128,1024]{1,0:T(8,128)(2,1)} %adjacency.1) | copy-start | bytes 786436
  60.4 25.8 %copy-start.3 = (bf16[128,512]{1,0:T(8,128)(2,1)S(1)}, bf16[128,512]{1,0:T(8,128)(2,1)}, u32[]{:S(2)}) copy-start(bf16[128,512]{1,0:T(8,128)(2,1)} %nodes.1) | copy-start | bytes 393220
  60.4 25.8 %all-to-all-start.2 = ((bf16[8,160,512]{2,1,0:T(8,128)(2,1)}), bf16[8,160,512]{2,1,0:T(8,128)(2,1)S(1)}, u32[]{:S(2)}, u32[]{:S(2)}) async-start(bf16[8,160,512]{2,1,0:T(8,128)(2,1)} %get-tuple-element.23), calls=%async_computation.2 | async-start | bytes 2621440 | tf_op jit(solution)/shard_map/all_to_all | solution.py:33
  65.1 7.1 %collective-permute-start.1 = (bf16[16,512]{1,0:T(8,128)(2,1)S(1)}, bf16[16,512]{1,0:T(8,128)(2,1)S(1)}, u32[]{:S(2)}, u32[]{:S(2)}) collective-permute-start(bf16[16,512]{1,0:T(8,128)(2,1)S(1)} %get-tuple-element.24), channel_id=1, source_target_pairs={{0,0},{8,1},{16,2},{24,3},{32,4},{40,5},{48,6},{56,7},{64,8},{72,9... | collective-permute-start | bytes 49160 | tf_op jit(solution)/shard_map/ppermute | solution.py:222
  102.2 22.3 %all-to-all-start.4 = ((bf16[64,32,128]{2,1,0:T(8,128)(2,1)}), bf16[64,32,128]{2,1,0:T(8,128)(2,1)S(1)}, u32[]{:S(2)}, u32[]{:S(2)}) async-start(bf16[64,32,128]{2,1,0:T(8,128)(2,1)} %get-tuple-element.27), calls=%async_computation.4 | async-start | bytes 1048576 | tf_op jit(solution)/shard_map/all_to_all | solution.py:231
  107.1 3.6 %collective-permute-start.2 = (bf16[128,128]{1,0:T(8,128)(2,1)S(1)}, bf16[128,128]{1,0:T(8,128)(2,1)S(1)}, u32[]{:S(2)}, u32[]{:S(2)}) collective-permute-start(bf16[128,128]{1,0:T(8,128)(2,1)S(1)} %get-tuple-element.28), channel_id=1, source_target_pairs={{0,1},{1,0},{2,3},{3,2},{4,5},{5,4},{6,7},{7,6},{8,9},{9,8},{10,11... | collective-permute-start | bytes 98312 | tf_op jit(solution)/shard_map/ppermute | solution.py:232
  110.7 7.8 %collective-permute-start.5 = (bf16[2,128,128]{2,1,0:T(8,128)(2,1)S(1)}, bf16[2,128,128]{2,1,0:T(8,128)(2,1)S(1)}, u32[]{:S(2)}, u32[]{:S(2)}) collective-permute-start(bf16[2,128,128]{2,1,0:T(8,128)(2,1)S(1)} %pad_maximum_fusion.p0), channel_id=1, source_target_pairs={{0,6},{1,7},{2,0},{3,1},{4,2},{5,3},{6,4},{7,5},{8,14},{9,15},{10,... | collective-permute-start | bytes 196616 | tf_op jit(solution)/shard_map/ppermute | solution.py:233
  113.5 6.8 %collective-permute-start.4 = (bf16[2,128,128]{2,1,0:T(8,128)(2,1)S(1)}, bf16[2,128,128]{2,1,0:T(8,128)(2,1)S(1)}, u32[]{:S(2)}, u32[]{:S(2)}) collective-permute-start(bf16[2,128,128]{2,1,0:T(8,128)(2,1)S(1)} %pad_maximum_fusion.p0), channel_id=1, source_target_pairs={{0,4},{1,5},{2,6},{3,7},{4,0},{5,1},{6,2},{7,3},{8,12},{9,13},{10,... | collective-permute-start | bytes 196616 | tf_op jit(solution)/shard_map/ppermute | solution.py:233
  116.6 6.5 %collective-permute-start.3 = (bf16[2,128,128]{2,1,0:T(8,128)(2,1)S(1)}, bf16[2,128,128]{2,1,0:T(8,128)(2,1)S(1)}, u32[]{:S(2)}, u32[]{:S(2)}) collective-permute-start(bf16[2,128,128]{2,1,0:T(8,128)(2,1)S(1)} %pad_maximum_fusion.p0), channel_id=1, source_target_pairs={{0,2},{1,3},{2,4},{3,5},{4,6},{5,7},{6,0},{7,1},{8,10},{9,11},{10,... | collective-permute-start | bytes 196616 | tf_op jit(solution)/shard_map/ppermute | solution.py:233
  124.5 6.7 %collective-permute-start.6 = (bf16[64,32,128]{2,1,0:T(8,128)(2,1)S(1)}, bf16[64,32,128]{2,1,0:T(8,128)(2,1)S(1)}, u32[]{:S(2)}, u32[]{:S(2)}) collective-permute-start(bf16[64,32,128]{2,1,0:T(8,128)(2,1)S(1)} %all-to-all-done.4.src), channel_id=1, source_target_pairs={{0,1},{1,0},{2,3},{3,2},{4,5},{5,4},{6,7},{7,6},{8,9},{9,8},{10,11... | collective-permute-start | bytes 1572872 | tf_op jit(solution)/shard_map/ppermute | solution.py:235

commit v9 on v8

--- a/solution.py
+++ b/solution.py
@@ -11,13 +11,22 @@
 ALL = ("rows", "rep")
 
 
+E8 = range(8)
+ORDER = (0, 2, 4, 6, 1, 3, 5, 7)
+
+
+def label(i):
+    return (i >> 1) | ((i & 1) << 2)
+
+
 def place(u, v, p):
-    z, y = (v, u) if p % 2 == 0 else (u, v)
+    z, y = (ORDER[v], ORDER[u]) if p % 2 == 0 else (ORDER[u], ORDER[v])
     return (8 * z + y) * 8 + p
 
 
-E8 = range(8)
+assert all(label(ORDER[i]) == i for i in E8)
 ALONG_U = [[place(u, v, p) for u in E8] for v in E8 for p in E8]
+PLANES = [[(8 * z + y) * 8 + p for z in ORDER for y in ORDER] for p in E8]
 ALONG_V = [[place(u, v, p) for v in E8] for u in E8 for p in E8]
 OUT = [((8 * z + y) * 8 + t, place(t, y, z)) for z in E8 for y in E8 for t in E8]
 BACK = [(b, a) for a, b in OUT]
@@ -72,7 +81,7 @@
         summed = summed + got[i, 0:128, :].astype(F32)
     r = lax.axis_index("rows")
     first = is_core_0()
-    u = jnp.where(first, r & 7, r >> 3)
+    u = label(jnp.where(first, r & 7, r >> 3))
     gain = gain_ref[...]
     w_in, w_out = w_in_ref[...], w_out_ref[...]
     cot = got[:, 128:144, :].reshape(128, 512)
@@ -228,7 +237,7 @@
         add_up, [((128, 128), BF), ((64, 32, 128), BF), ((8, 128), F32)],
         lax.all_to_all(send, "rep", 0, 0), cotangent, out,
     )
-    mine = lax.all_to_all(send, "rows", 0, 0)
+    mine = trade(send, PLANES)
     pieces = jnp.stack([piece, lax.ppermute(piece, ALL, CORE)])
     pieces = [pieces] + [lax.ppermute(pieces, ALL, perm) for perm in SHIFT_X]
     mine, pieces = lax.optimization_barrier((mine, pieces))

time: 133 us -> 131 us (0.985)
  starting transfers between devices: 46.2 us -> 50.4 us
  waiting for transfers between devices: 34.1 us -> 30 us
  blocking collectives: 42.7 us -> 40.1 us
    all_to_all x2 -> x3, starting transfers between devices: 12.5 us -> 20.7 us  [trade(): return lax.all_to_all(x, ALL, 0, 0, axis_index_groups=groups)]
    all_to_all x1 -> x0, starting transfers between devices: 4.88 us -> none  [shards(): mine = lax.all_to_all(send, 'rows', 0, 0)]
    all_to_all x2 -> x3, waiting for transfers between devices: 14 us -> 11.2 us  [trade(): return lax.all_to_all(x, ALL, 0, 0, axis_index_groups=groups)]
    all_to_all x1, blocking collectives: 27.8 us -> 25.3 us  [trade(): return lax.all_to_all(x, ALL, 0, 0, axis_index_groups=groups)]
    all_to_all x1 -> x0, waiting for transfers between devices: 1.41 us -> none  [shards(): mine = lax.all_to_all(send, 'rows', 0, 0)]
where the time goes in v9:
time: 131 us; the launch traced here: 130 us
  starting transfers between devices  50.4 us (38%)
  blocking collectives  40.1 us (31%)
  waiting for transfers between devices  30 us (23%)
  Pallas kernels  5.95 us (5%)
  matrix products  2.41 us (2%)
    all_to_all x1, blocking collectives, trade(): return lax.all_to_all(x, ALL, 0, 0, axis_index_groups=groups)  25.3 us
    all_to_all x3, starting transfers between devices, trade(): return lax.all_to_all(x, ALL, 0, 0, axis_index_groups=groups)  20.7 us
    all_to_all x1, blocking collectives, shards(): lax.all_to_all(send, 'rep', 0, 0)  14.9 us
    ppermute x1, waiting for transfers between devices, shards(): cot = lax.ppermute(piece, ALL, OUT)  11.5 us
    all_to_all x3, waiting for transfers between devices, trade(): return lax.all_to_all(x, ALL, 0, 0, axis_index_groups=groups)  11.2 us
    ppermute x1, starting transfers between devices, shards(): cot = lax.ppermute(piece, ALL, OUT)  8.27 us
    ppermute x3, starting transfers between devices, shards(): pieces = [pieces] + [lax.ppermute(pieces, ALL, perm) for perm in SHIFT_X]  7.8 us
    ppermute x1, starting transfers between devices, shards(): change = lax.ppermute(change, ALL, BACK)  6.51 us
  transfers between devices with their start and end apart: 10, of which 7 were waited for; matrix products, arithmetic and copies ran while one was open for 0% of the time, Pallas kernels for 1%

profile of v9, /device:TPU:1, one launch (start us, length us, event | category | flops | bytes accessed | tf_op | source)
XLA Modules:
  0.0 130.3 jit_solution(7803187320841265364)
XLA Ops:
  0.6 2.4 %convolution_convert_fusion = bf16[1024,512]{1,0:T(8,128)(2,1)} fusion(bf16[128,1024]{1,0:T(8,128)(2,1)} %adjacency.1, bf16[128,512]{1,0:T(8,128)(2,1)} %nodes.1), kind=kOutput, calls=%fused_computation | convolution fusion | flops 134742016 | bytes 1441792 | tf_op jit(solution)/shard_map/dot_general | solution.py:38
  3.0 7.8 %all-to-all-start = ((bf16[8,128,512]{2,1,0:T(8,128)(2,1)}), bf16[8,128,512]{2,1,0:T(8,128)(2,1)S(1)}, u32[]{:S(2)}, u32[]{:S(2)}) async-start(bf16[8,128,512]{2,1,0:T(8,128)(2,1)} %bitcast), calls=%async_computation | async-start | bytes 2097152 | tf_op jit(solution)/shard_map/all_to_all | solution.py:42
  10.8 8.3 %collective-permute-start = (bf16[16,512]{1,0:T(8,128)(2,1)S(1)}, bf16[16,512]{1,0:T(8,128)(2,1)S(1)}, u32[]{:S(2)}, u32[]{:S(2)}) collective-permute-start(bf16[16,512]{1,0:T(8,128)(2,1)S(1)} %constant_dynamic-slice_fusion), channel_id=1, source_target_pairs={{0,0},{1,16},{2,32},{3,48},{4,8},{5,24},{6,40},{7,56},{8,128},{9,1... | collective-permute-start | bytes 49160 | tf_op jit(solution)/shard_map/ppermute | solution.py:219
  19.1 11.5 %collective-permute-done.cot = bf16[16,512]{1,0:T(8,128)(2,1)S(1)} collective-permute-done((bf16[16,512]{1,0:T(8,128)(2,1)S(1)}, bf16[16,512]{1,0:T(8,128)(2,1)S(1)}, u32[]{:S(2)}, u32[]{:S(2)}) %collective-permute-start) | collective-permute-done | bytes 16416 | tf_op jit(solution)/shard_map/ppermute | solution.py:219
  30.8 25.3 %all_to_all.25.got = bf16[8,144,512]{2,1,0:T(8,128)(2,1)S(1)} all-to-all(bf16[8,144,512]{2,1,0:T(8,128)(2,1)S(1)} %shard_map.101), channel_id=1, replica_groups={{0,16,32,48,8,24,40,56},{1,129,257,385,65,193,321,449},{2,18,34,50,10,2..., dimensions={0} | all-to-all | bytes 2359296 | tf_op jit(solution)/shard_map/all_to_all | solution.py:42
  56.1 2.2 %shard_map.102 = (bf16[16,512]{1,0:T(8,128)(2,1)S(1)}, bf16[8,160,512]{2,1,0:T(8,128)(2,1)}) custom-call(bf16[8,144,512]{2,1,0:T(8,128)(2,1)S(1)} %all_to_all.25.got, f32[1,512]{1,0:T(1,128)S(1)} %bitcast.11, bf16[512,512]{1,0:T(8,128)(2,1)S(1)} %copy-done.1, bf16[512,512]{1,0:T(8,128)(2,1)S(1)} %copy-done.2), custom_call_target="tpu_custom_call" | custom-call | tf_op jit(solution)/shard_map/pallas_call | solution.py:46
  58.3 5.1 %all-to-all-start.2 = ((bf16[8,160,512]{2,1,0:T(8,128)(2,1)}), bf16[8,160,512]{2,1,0:T(8,128)(2,1)S(1)}, u32[]{:S(2)}, u32[]{:S(2)}) async-start(bf16[8,160,512]{2,1,0:T(8,128)(2,1)} %get-tuple-element.23), calls=%async_computation.2 | async-start | bytes 2621440 | tf_op jit(solution)/shard_map/all_to_all | solution.py:42
  63.4 6.5 %collective-permute-start.1 = (bf16[16,512]{1,0:T(8,128)(2,1)S(1)}, bf16[16,512]{1,0:T(8,128)(2,1)S(1)}, u32[]{:S(2)}, u32[]{:S(2)}) collective-permute-start(bf16[16,512]{1,0:T(8,128)(2,1)S(1)} %get-tuple-element.24), channel_id=1, source_target_pairs={{0,0},{16,1},{32,2},{48,3},{8,4},{24,5},{40,6},{56,7},{128,8},{144... | collective-permute-start | bytes 49160 | tf_op jit(solution)/shard_map/ppermute | solution.py:231
  69.9 1.9 %collective-permute-done.1.change = bf16[16,512]{1,0:T(8,128)(2,1)S(1)} collective-permute-done((bf16[16,512]{1,0:T(8,128)(2,1)S(1)}, bf16[16,512]{1,0:T(8,128)(2,1)S(1)}, u32[]{:S(2)}, u32[]{:S(2)}) %collective-permute-start.1) | collective-permute-done | bytes 16416 | tf_op jit(solution)/shard_map/ppermute | solution.py:231
  71.8 10.1 %all-to-all-done.2.got = bf16[8,160,512]{2,1,0:T(8,128)(2,1)S(1)} async-done(((bf16[8,160,512]{2,1,0:T(8,128)(2,1)}), bf16[8,160,512]{2,1,0:T(8,128)(2,1)S(1)}, u32[]{:S(2)}, u32[]{:S(2)}) %all-to-all-start.2) | async-done | bytes 1310752 | tf_op jit(solution)/shard_map/all_to_all | solution.py:42
  82.3 14.9 %all_to_all.26.got = bf16[8,144,128]{2,1,0:T(8,128)(2,1)S(1)} all-to-all(bf16[8,144,128]{2,1,0:T(8,128)(2,1)S(1)} %get-tuple-element.25), channel_id=1, replica_groups=mesh['rows'=64,'rep'=8] {'rep'}, dimensions={0} | all-to-all | bytes 589824 | tf_op jit(solution)/shard_map/all_to_all | solution.py:238
  97.1 0.8 shard_map.104
  98.0 7.8 %all-to-all-start.4 = ((bf16[64,32,128]{2,1,0:T(8,128)(2,1)}), bf16[64,32,128]{2,1,0:T(8,128)(2,1)S(1)}, u32[]{:S(2)}, u32[]{:S(2)}) async-start(bf16[64,32,128]{2,1,0:T(8,128)(2,1)} %get-tuple-element.27), calls=%async_computation.4 | async-start | bytes 1048576 | tf_op jit(solution)/shard_map/all_to_all | solution.py:42
  105.8 2.8 %collective-permute-start.2 = (bf16[128,128]{1,0:T(8,128)(2,1)S(1)}, bf16[128,128]{1,0:T(8,128)(2,1)S(1)}, u32[]{:S(2)}, u32[]{:S(2)}) collective-permute-start(bf16[128,128]{1,0:T(8,128)(2,1)S(1)} %get-tuple-element.28), channel_id=1, source_target_pairs={{0,1},{1,0},{2,3},{3,2},{4,5},{5,4},{6,7},{7,6},{8,9},{9,8},{10,11... | collective-permute-start | bytes 98312 | tf_op jit(solution)/shard_map/ppermute | solution.py:241
  108.6 0.8 collective-permute-done.2
  109.4 2.8 %collective-permute-start.5 = (bf16[2,128,128]{2,1,0:T(8,128)(2,1)S(1)}, bf16[2,128,128]{2,1,0:T(8,128)(2,1)S(1)}, u32[]{:S(2)}, u32[]{:S(2)}) collective-permute-start(bf16[2,128,128]{2,1,0:T(8,128)(2,1)S(1)} %pad_maximum_fusion.p0), channel_id=1, source_target_pairs={{0,6},{1,7},{2,0},{3,1},{4,2},{5,3},{6,4},{7,5},{8,14},{9,15},{10,... | collective-permute-start | bytes 196616 | tf_op jit(solution)/shard_map/ppermute | solution.py:242
  112.2 3.1 %collective-permute-start.4 = (bf16[2,128,128]{2,1,0:T(8,128)(2,1)S(1)}, bf16[2,128,128]{2,1,0:T(8,128)(2,1)S(1)}, u32[]{:S(2)}, u32[]{:S(2)}) collective-permute-start(bf16[2,128,128]{2,1,0:T(8,128)(2,1)S(1)} %pad_maximum_fusion.p0), channel_id=1, source_target_pairs={{0,4},{1,5},{2,6},{3,7},{4,0},{5,1},{6,2},{7,3},{8,12},{9,13},{10,... | collective-permute-start | bytes 196616 | tf_op jit(solution)/shard_map/ppermute | solution.py:242
  115.3 1.9 %collective-permute-start.3 = (bf16[2,128,128]{2,1,0:T(8,128)(2,1)S(1)}, bf16[2,128,128]{2,1,0:T(8,128)(2,1)S(1)}, u32[]{:S(2)}, u32[]{:S(2)}) collective-permute-start(bf16[2,128,128]{2,1,0:T(8,128)(2,1)S(1)} %pad_maximum_fusion.p0), channel_id=1, source_target_pairs={{0,2},{1,3},{2,4},{3,5},{4,6},{5,7},{6,0},{7,1},{8,10},{9,11},{10,... | collective-permute-start | bytes 196616 | tf_op jit(solution)/shard_map/ppermute | solution.py:242
  117.3 1.8 %collective-permute-done.4.p2 = bf16[2,128,128]{2,1,0:T(8,128)(2,1)S(1)} collective-permute-done((bf16[2,128,128]{2,1,0:T(8,128)(2,1)S(1)}, bf16[2,128,128]{2,1,0:T(8,128)(2,1)S(1)}, u32[]{:S(2)}, u32[]{:S(2)}) %collective-permute-start.4) | collective-permute-done | bytes 65568 | tf_op jit(solution)/shard_map/ppermute | solution.py:242
  119.0 2.8 %collective-permute-done.3.p1 = bf16[2,128,128]{2,1,0:T(8,128)(2,1)S(1)} collective-permute-done((bf16[2,128,128]{2,1,0:T(8,128)(2,1)S(1)}, bf16[2,128,128]{2,1,0:T(8,128)(2,1)S(1)}, u32[]{:S(2)}, u32[]{:S(2)}) %collective-permute-start.3) | collective-permute-done | bytes 65568 | tf_op jit(solution)/shard_map/ppermute | solution.py:242
  121.8 1.0 all-to-all-done.4.src
  122.9 4.3 %collective-permute-start.6 = (bf16[64,32,128]{2,1,0:T(8,128)(2,1)S(1)}, bf16[64,32,128]{2,1,0:T(8,128)(2,1)S(1)}, u32[]{:S(2)}, u32[]{:S(2)}) collective-permute-start(bf16[64,32,128]{2,1,0:T(8,128)(2,1)S(1)} %all-to-all-done.4.src), channel_id=1, source_target_pairs={{0,1},{1,0},{2,3},{3,2},{4,5},{5,4},{6,7},{7,6},{8,9},{9,8},{10,11... | collective-permute-start | bytes 1572872 | tf_op jit(solution)/shard_map/ppermute | solution.py:244
  127.8 0.9 shard_map.105
  128.7 1.6 %shard_map.106 = (f32[8,2,32,512]{3,2,1,0:T(8,128)}, f32[8,2,32,512]{3,2,1,0:T(8,128)}) custom-call(bf16[64,32,128]{2,1,0:T(8,128)(2,1)S(1)} %collective-permute-done.6.src, f32[8,32,512]{2,1,0:T(8,128)S(1)} %get-tuple-element.36.mine_in, f32[8,32,512]{2,1,0:T(8,128)S(1)} %get-tuple-element.37.mine_out), custom_call_target="tpu_custom_call" | custom-call | tf_op jit(solution)/shard_map/pallas_call | solution.py:251
  (20 shorter events, 1.1 us)
Async XLA Ops:
  3.0 7.8 %copy-start.4 = (bf16[128,512]{1,0:T(8,128)(2,1)S(1)}, bf16[128,512]{1,0:T(8,128)(2,1)}, u32[]{:S(2)}) copy-start(bf16[128,512]{1,0:T(8,128)(2,1)} %cotangent.1) | copy-start | bytes 393220
  3.0 27.6 %all-to-all-start = ((bf16[8,128,512]{2,1,0:T(8,128)(2,1)}), bf16[8,128,512]{2,1,0:T(8,128)(2,1)S(1)}, u32[]{:S(2)}, u32[]{:S(2)}) async-start(bf16[8,128,512]{2,1,0:T(8,128)(2,1)} %bitcast), calls=%async_computation | async-start | bytes 2097152 | tf_op jit(solution)/shard_map/all_to_all | solution.py:42
  10.8 19.8 %collective-permute-start = (bf16[16,512]{1,0:T(8,128)(2,1)S(1)}, bf16[16,512]{1,0:T(8,128)(2,1)S(1)}, u32[]{:S(2)}, u32[]{:S(2)}) collective-permute-start(bf16[16,512]{1,0:T(8,128)(2,1)S(1)} %constant_dynamic-slice_fusion), channel_id=1, source_target_pairs={{0,0},{1,16},{2,32},{3,48},{4,8},{5,24},{6,40},{7,56},{8,128},{9,1... | collective-permute-start | bytes 49160 | tf_op jit(solution)/shard_map/ppermute | solution.py:219
  30.8 25.3 %copy-start.1 = (bf16[512,512]{1,0:T(8,128)(2,1)S(1)}, bf16[512,512]{1,0:T(8,128)(2,1)}, u32[]{:S(2)}) copy-start(bf16[512,512]{1,0:T(8,128)(2,1)} %w_in_ref.1) | copy-start | bytes 1572868
  30.8 25.3 %copy-start.2 = (bf16[512,512]{1,0:T(8,128)(2,1)S(1)}, bf16[512,512]{1,0:T(8,128)(2,1)}, u32[]{:S(2)}) copy-start(bf16[512,512]{1,0:T(8,128)(2,1)} %w_out_ref.1) | copy-start | bytes 1572868
  30.8 25.3 %copy-start.5 = (f32[512]{0:T(512)S(1)}, f32[512]{0:T(512)}, u32[]{:S(2)}) copy-start(f32[512]{0:T(512)} %param.8) | copy-start | bytes 6148
  58.3 23.7 %copy-start = (bf16[128,1024]{1,0:T(8,128)(2,1)S(1)}, bf16[128,1024]{1,0:T(8,128)(2,1)}, u32[]{:S(2)}) copy-start(bf16[128,1024]{1,0:T(8,128)(2,1)} %adjacency.1) | copy-start | bytes 786436
  58.3 23.7 %copy-start.3 = (bf16[128,512]{1,0:T(8,128)(2,1)S(1)}, bf16[128,512]{1,0:T(8,128)(2,1)}, u32[]{:S(2)}) copy-start(bf16[128,512]{1,0:T(8,128)(2,1)} %nodes.1) | copy-start | bytes 393220
  58.3 23.7 %all-to-all-start.2 = ((bf16[8,160,512]{2,1,0:T(8,128)(2,1)}), bf16[8,160,512]{2,1,0:T(8,128)(2,1)S(1)}, u32[]{:S(2)}, u32[]{:S(2)}) async-start(bf16[8,160,512]{2,1,0:T(8,128)(2,1)} %get-tuple-element.23), calls=%async_computation.2 | async-start | bytes 2621440 | tf_op jit(solution)/shard_map/all_to_all | solution.py:42
  63.4 8.4 %collective-permute-start.1 = (bf16[16,512]{1,0:T(8,128)(2,1)S(1)}, bf16[16,512]{1,0:T(8,128)(2,1)S(1)}, u32[]{:S(2)}, u32[]{:S(2)}) collective-permute-start(bf16[16,512]{1,0:T(8,128)(2,1)S(1)} %get-tuple-element.24), channel_id=1, source_target_pairs={{0,0},{16,1},{32,2},{48,3},{8,4},{24,5},{40,6},{56,7},{128,8},{144... | collective-permute-start | bytes 49160 | tf_op jit(solution)/shard_map/ppermute | solution.py:231
  98.0 24.9 %all-to-all-start.4 = ((bf16[64,32,128]{2,1,0:T(8,128)(2,1)}), bf16[64,32,128]{2,1,0:T(8,128)(2,1)S(1)}, u32[]{:S(2)}, u32[]{:S(2)}) async-start(bf16[64,32,128]{2,1,0:T(8,128)(2,1)} %get-tuple-element.27), calls=%async_computation.4 | async-start | bytes 1048576 | tf_op jit(solution)/shard_map/all_to_all | solution.py:42
  105.8 3.6 %collective-permute-start.2 = (bf16[128,128]{1,0:T(8,128)(2,1)S(1)}, bf16[128,128]{1,0:T(8,128)(2,1)S(1)}, u32[]{:S(2)}, u32[]{:S(2)}) collective-permute-start(bf16[128,128]{1,0:T(8,128)(2,1)S(1)} %get-tuple-element.28), channel_id=1, source_target_pairs={{0,1},{1,0},{2,3},{3,2},{4,5},{5,4},{6,7},{7,6},{8,9},{9,8},{10,11... | collective-permute-start | bytes 98312 | tf_op jit(solution)/shard_map/ppermute | solution.py:241
  109.4 7.8 %collective-permute-start.5 = (bf16[2,128,128]{2,1,0:T(8,128)(2,1)S(1)}, bf16[2,128,128]{2,1,0:T(8,128)(2,1)S(1)}, u32[]{:S(2)}, u32[]{:S(2)}) collective-permute-start(bf16[2,128,128]{2,1,0:T(8,128)(2,1)S(1)} %pad_maximum_fusion.p0), channel_id=1, source_target_pairs={{0,6},{1,7},{2,0},{3,1},{4,2},{5,3},{6,4},{7,5},{8,14},{9,15},{10,... | collective-permute-start | bytes 196616 | tf_op jit(solution)/shard_map/ppermute | solution.py:242
  112.2 6.8 %collective-permute-start.4 = (bf16[2,128,128]{2,1,0:T(8,128)(2,1)S(1)}, bf16[2,128,128]{2,1,0:T(8,128)(2,1)S(1)}, u32[]{:S(2)}, u32[]{:S(2)}) collective-permute-start(bf16[2,128,128]{2,1,0:T(8,128)(2,1)S(1)} %pad_maximum_fusion.p0), channel_id=1, source_target_pairs={{0,4},{1,5},{2,6},{3,7},{4,0},{5,1},{6,2},{7,3},{8,12},{9,13},{10,... | collective-permute-start | bytes 196616 | tf_op jit(solution)/shard_map/ppermute | solution.py:242
  115.3 6.5 %collective-permute-start.3 = (bf16[2,128,128]{2,1,0:T(8,128)(2,1)S(1)}, bf16[2,128,128]{2,1,0:T(8,128)(2,1)S(1)}, u32[]{:S(2)}, u32[]{:S(2)}) collective-permute-start(bf16[2,128,128]{2,1,0:T(8,128)(2,1)S(1)} %pad_maximum_fusion.p0), channel_id=1, source_target_pairs={{0,2},{1,3},{2,4},{3,5},{4,6},{5,7},{6,0},{7,1},{8,10},{9,11},{10,... | collective-permute-start | bytes 196616 | tf_op jit(solution)/shard_map/ppermute | solution.py:242
  122.9 5.8 %collective-permute-start.6 = (bf16[64,32,128]{2,1,0:T(8,128)(2,1)S(1)}, bf16[64,32,128]{2,1,0:T(8,128)(2,1)S(1)}, u32[]{:S(2)}, u32[]{:S(2)}) collective-permute-start(bf16[64,32,128]{2,1,0:T(8,128)(2,1)S(1)} %all-to-all-done.4.src), channel_id=1, source_target_pairs={{0,1},{1,0},{2,3},{3,2},{4,5},{5,4},{6,7},{7,6},{8,9},{9,8},{10,11... | collective-permute-start | bytes 1572872 | tf_op jit(solution)/shard_map/ppermute | solution.py:244

commit v10 on v9

--- a/solution.py
+++ b/solution.py
@@ -144,17 +144,17 @@
         lows = lows + got[v, 144:160, :].astype(F32)
     exact = exact + jnp.where(lax.broadcasted_iota(jnp.int32, (16, 1), 0) < 14, lows, 0.0)
     gain = lows[14:15] + lows[15:16]
-    gain = jnp.concatenate([gain[:, 128 * j : 128 * j + 128] for j in range(4)] + [jnp.zeros((4, 128), F32)], axis=0)
+    gain = jnp.concatenate([gain[:, 128 * j : 128 * j + 128] for j in range(4)], axis=0)
+    gain_high = gain.astype(BF).astype(F32)
+    gain = jnp.concatenate([jnp.zeros((8, 128), F32), gain_high, gain - gain_high], axis=0)
     high = exact.astype(BF)
-    low = (exact - high.astype(F32)).astype(BF)
-    gain_high = gain.astype(BF).astype(F32)
-    gain = jnp.concatenate([gain_high, gain - gain_high], axis=0).astype(BF)
+    low = exact - high.astype(F32)
+    top = lax.broadcasted_iota(jnp.int32, (16, 1), 0) < 8
     for q in E8:
         for i in range(2):
-            j = 2 * (q % 2) + i
-            send[q, 64 + 16 * i : 80 + 16 * i, :] = high[:, 128 * j : 128 * j + 128]
-            send[q, 96 + 16 * i : 112 + 16 * i, :] = low[:, 128 * j : 128 * j + 128]
-        send[q, 128:144, :] = gain
+            at = slice(128 * (2 * (q % 2) + i), 128 * (2 * (q % 2) + i) + 128)
+            send[q, 64 + 16 * i : 80 + 16 * i, :] = high[:, at]
+            send[q, 96 + 16 * i : 112 + 16 * i, :] = (low[:, at] if i == 0 else jnp.where(top, low[:, at], gain)).astype(BF)
 
 
 def add_up(got, cotangent, out, piece, send, gain):
@@ -165,10 +165,11 @@
             own[:, 128 * j : 128 * j + 128] + total[16 * j : 16 * j + 16]
         ).astype(BF)
     piece[64:128, :] = out[...]
-    block = (total[64:96] + total[96:128]).astype(BF)
+    block = jnp.concatenate([total[64:88] + total[96:120], total[88:96]], axis=0).astype(BF)
     for r in range(64):
         send[r] = block
-    gain[...] = total[128:136] + total[136:144]
+    for j in range(4):
+        gain[0:1, 128 * j : 128 * j + 128] = total[120 + j : 121 + j] + total[124 + j : 125 + j]
 
 
 def lay_rows(src, z, grad_in, grad_out):
@@ -230,11 +231,11 @@
     )
     change = lax.ppermute(change, ALL, BACK)
     send, out = call(
-        back_and_tile, [((8, 144, 128), BF), ((64, 128), BF)],
+        back_and_tile, [((8, 128, 128), BF), ((64, 128), BF)],
         adjacency, trade(send, ALONG_V), nodes, change,
     )
     piece, send, grad_gain = call(
-        add_up, [((128, 128), BF), ((64, 32, 128), BF), ((8, 128), F32)],
+        add_up, [((128, 128), BF), ((64, 32, 128), BF), ((1, 512), F32)],
         lax.all_to_all(send, "rep", 0, 0), cotangent, out,
     )
     mine = trade(send, PLANES)
@@ -256,7 +257,7 @@
         scratch_shapes=[pltpu.VMEM(*half)] * 2 + [pltpu.SemaphoreType.DMA((32,))],
         compiler_params=pltpu.CompilerParams(vmem_limit_bytes=40 * 1024 * 1024),
     )(other, mine_in, mine_out)
-    return (node_out, node_grad, grad_in.reshape(512, 512), grad_out.reshape(512, 512), grad_gain[:4].reshape(512))
+    return (node_out, node_grad, grad_in.reshape(512, 512), grad_out.reshape(512, 512), grad_gain.reshape(512))
 
 
 def solution(mesh):

time: 131 us -> 130 us (level)
  transfers between devices with their start and end apart: 10 -> 10, of which waited for: 7 -> 8; matrix products, arithmetic and copies ran while one was open for 0% -> 0% of each run, Pallas kernels for 1% -> 1%
where the time goes in v10:
time: 130 us; the launch traced here: 129 us
  starting transfers between devices  51.2 us (39%)
  blocking collectives  39.3 us (30%)
  waiting for transfers between devices  29.7 us (23%)
  Pallas kernels  5.96 us (5%)
  matrix products  2.41 us (2%)
    all_to_all x1, blocking collectives, trade(): return lax.all_to_all(x, ALL, 0, 0, axis_index_groups=groups)  25.3 us
    all_to_all x3, starting transfers between devices, trade(): return lax.all_to_all(x, ALL, 0, 0, axis_index_groups=groups)  20.7 us
    all_to_all x1, blocking collectives, shards(): lax.all_to_all(send, 'rep', 0, 0)  14 us
    ppermute x1, waiting for transfers between devices, shards(): cot = lax.ppermute(piece, ALL, OUT)  11.5 us
    all_to_all x3, waiting for transfers between devices, trade(): return lax.all_to_all(x, ALL, 0, 0, axis_index_groups=groups)  10.3 us
    ppermute x1, starting transfers between devices, shards(): cot = lax.ppermute(piece, ALL, OUT)  8.27 us
    ppermute x3, starting transfers between devices, shards(): pieces = [pieces] + [lax.ppermute(pieces, ALL, perm) for perm in SHIFT_X]  7.8 us
    ppermute x1, starting transfers between devices, shards(): change = lax.ppermute(change, ALL, BACK)  6.51 us
  transfers between devices with their start and end apart: 10, of which 8 were waited for; matrix products, arithmetic and copies ran while one was open for 0% of the time, Pallas kernels for 1%

profile of v10, /device:TPU:1, one launch (start us, length us, event | category | flops | bytes accessed | tf_op | source)
XLA Modules:
  0.0 129.4 jit_solution(17702175159344497698)
XLA Ops:
  0.6 2.4 %convolution_convert_fusion = bf16[1024,512]{1,0:T(8,128)(2,1)} fusion(bf16[128,1024]{1,0:T(8,128)(2,1)} %adjacency.1, bf16[128,512]{1,0:T(8,128)(2,1)} %nodes.1), kind=kOutput, calls=%fused_computation | convolution fusion | flops 134742016 | bytes 1441792 | tf_op jit(solution)/shard_map/dot_general | solution.py:38
  3.0 7.8 %all-to-all-start = ((bf16[8,128,512]{2,1,0:T(8,128)(2,1)}), bf16[8,128,512]{2,1,0:T(8,128)(2,1)S(1)}, u32[]{:S(2)}, u32[]{:S(2)}) async-start(bf16[8,128,512]{2,1,0:T(8,128)(2,1)} %bitcast), calls=%async_computation | async-start | bytes 2097152 | tf_op jit(solution)/shard_map/all_to_all | solution.py:42
  10.8 8.3 %collective-permute-start = (bf16[16,512]{1,0:T(8,128)(2,1)S(1)}, bf16[16,512]{1,0:T(8,128)(2,1)S(1)}, u32[]{:S(2)}, u32[]{:S(2)}) collective-permute-start(bf16[16,512]{1,0:T(8,128)(2,1)S(1)} %constant_dynamic-slice_fusion), channel_id=1, source_target_pairs={{0,0},{1,16},{2,32},{3,48},{4,8},{5,24},{6,40},{7,56},{8,128},{9,1... | collective-permute-start | bytes 49160 | tf_op jit(solution)/shard_map/ppermute | solution.py:220
  19.1 11.5 %collective-permute-done.cot = bf16[16,512]{1,0:T(8,128)(2,1)S(1)} collective-permute-done((bf16[16,512]{1,0:T(8,128)(2,1)S(1)}, bf16[16,512]{1,0:T(8,128)(2,1)S(1)}, u32[]{:S(2)}, u32[]{:S(2)}) %collective-permute-start) | collective-permute-done | bytes 16416 | tf_op jit(solution)/shard_map/ppermute | solution.py:220
  30.8 25.3 %all_to_all.25.got = bf16[8,144,512]{2,1,0:T(8,128)(2,1)S(1)} all-to-all(bf16[8,144,512]{2,1,0:T(8,128)(2,1)S(1)} %shard_map.101), channel_id=1, replica_groups={{0,16,32,48,8,24,40,56},{1,129,257,385,65,193,321,449},{2,18,34,50,10,2..., dimensions={0} | all-to-all | bytes 2359296 | tf_op jit(solution)/shard_map/all_to_all | solution.py:42
  56.1 2.2 %shard_map.102 = (bf16[16,512]{1,0:T(8,128)(2,1)S(1)}, bf16[8,160,512]{2,1,0:T(8,128)(2,1)}) custom-call(bf16[8,144,512]{2,1,0:T(8,128)(2,1)S(1)} %all_to_all.25.got, f32[1,512]{1,0:T(1,128)S(1)} %bitcast.10, bf16[512,512]{1,0:T(8,128)(2,1)S(1)} %copy-done.1, bf16[512,512]{1,0:T(8,128)(2,1)S(1)} %copy-done.2), custom_call_target="tpu_custom_call" | custom-call | tf_op jit(solution)/shard_map/pallas_call | solution.py:46
  58.3 5.1 %all-to-all-start.2 = ((bf16[8,160,512]{2,1,0:T(8,128)(2,1)}), bf16[8,160,512]{2,1,0:T(8,128)(2,1)S(1)}, u32[]{:S(2)}, u32[]{:S(2)}) async-start(bf16[8,160,512]{2,1,0:T(8,128)(2,1)} %get-tuple-element.23), calls=%async_computation.2 | async-start | bytes 2621440 | tf_op jit(solution)/shard_map/all_to_all | solution.py:42
  63.4 6.5 %collective-permute-start.1 = (bf16[16,512]{1,0:T(8,128)(2,1)S(1)}, bf16[16,512]{1,0:T(8,128)(2,1)S(1)}, u32[]{:S(2)}, u32[]{:S(2)}) collective-permute-start(bf16[16,512]{1,0:T(8,128)(2,1)S(1)} %get-tuple-element.24), channel_id=1, source_target_pairs={{0,0},{16,1},{32,2},{48,3},{8,4},{24,5},{40,6},{56,7},{128,8},{144... | collective-permute-start | bytes 49160 | tf_op jit(solution)/shard_map/ppermute | solution.py:232
  69.9 1.9 %collective-permute-done.1.change = bf16[16,512]{1,0:T(8,128)(2,1)S(1)} collective-permute-done((bf16[16,512]{1,0:T(8,128)(2,1)S(1)}, bf16[16,512]{1,0:T(8,128)(2,1)S(1)}, u32[]{:S(2)}, u32[]{:S(2)}) %collective-permute-start.1) | collective-permute-done | bytes 16416 | tf_op jit(solution)/shard_map/ppermute | solution.py:232
  71.8 10.1 %all-to-all-done.2.got = bf16[8,160,512]{2,1,0:T(8,128)(2,1)S(1)} async-done(((bf16[8,160,512]{2,1,0:T(8,128)(2,1)}), bf16[8,160,512]{2,1,0:T(8,128)(2,1)S(1)}, u32[]{:S(2)}, u32[]{:S(2)}) %all-to-all-start.2) | async-done | bytes 1310752 | tf_op jit(solution)/shard_map/all_to_all | solution.py:42
  82.3 14.0 %all_to_all.26.got = bf16[8,128,128]{2,1,0:T(8,128)(2,1)S(1)} all-to-all(bf16[8,128,128]{2,1,0:T(8,128)(2,1)S(1)} %get-tuple-element.25), channel_id=1, replica_groups=mesh['rows'=64,'rep'=8] {'rep'}, dimensions={0} | all-to-all | bytes 524288 | tf_op jit(solution)/shard_map/all_to_all | solution.py:239
  96.3 0.8 shard_map.104
  97.2 7.8 %all-to-all-start.4 = ((bf16[64,32,128]{2,1,0:T(8,128)(2,1)}), bf16[64,32,128]{2,1,0:T(8,128)(2,1)S(1)}, u32[]{:S(2)}, u32[]{:S(2)}) async-start(bf16[64,32,128]{2,1,0:T(8,128)(2,1)} %get-tuple-element.27), calls=%async_computation.4 | async-start | bytes 1048576 | tf_op jit(solution)/shard_map/all_to_all | solution.py:42
  105.0 3.2 %collective-permute-start.2 = (bf16[128,128]{1,0:T(8,128)(2,1)S(1)}, bf16[128,128]{1,0:T(8,128)(2,1)S(1)}, u32[]{:S(2)}, u32[]{:S(2)}) collective-permute-start(bf16[128,128]{1,0:T(8,128)(2,1)S(1)} %get-tuple-element.28), channel_id=1, source_target_pairs={{0,1},{1,0},{2,3},{3,2},{4,5},{5,4},{6,7},{7,6},{8,9},{9,8},{10,11... | collective-permute-start | bytes 98312 | tf_op jit(solution)/shard_map/ppermute | solution.py:242
  108.2 0.8 collective-permute-done.2
  109.1 2.8 %collective-permute-start.5 = (bf16[2,128,128]{2,1,0:T(8,128)(2,1)S(1)}, bf16[2,128,128]{2,1,0:T(8,128)(2,1)S(1)}, u32[]{:S(2)}, u32[]{:S(2)}) collective-permute-start(bf16[2,128,128]{2,1,0:T(8,128)(2,1)S(1)} %pad_maximum_fusion.p0), channel_id=1, source_target_pairs={{0,6},{1,7},{2,0},{3,1},{4,2},{5,3},{6,4},{7,5},{8,14},{9,15},{10,... | collective-permute-start | bytes 196616 | tf_op jit(solution)/shard_map/ppermute | solution.py:243
  111.9 3.1 %collective-permute-start.4 = (bf16[2,128,128]{2,1,0:T(8,128)(2,1)S(1)}, bf16[2,128,128]{2,1,0:T(8,128)(2,1)S(1)}, u32[]{:S(2)}, u32[]{:S(2)}) collective-permute-start(bf16[2,128,128]{2,1,0:T(8,128)(2,1)S(1)} %pad_maximum_fusion.p0), channel_id=1, source_target_pairs={{0,4},{1,5},{2,6},{3,7},{4,0},{5,1},{6,2},{7,3},{8,12},{9,13},{10,... | collective-permute-start | bytes 196616 | tf_op jit(solution)/shard_map/ppermute | solution.py:243
  115.0 1.9 %collective-permute-start.3 = (bf16[2,128,128]{2,1,0:T(8,128)(2,1)S(1)}, bf16[2,128,128]{2,1,0:T(8,128)(2,1)S(1)}, u32[]{:S(2)}, u32[]{:S(2)}) collective-permute-start(bf16[2,128,128]{2,1,0:T(8,128)(2,1)S(1)} %pad_maximum_fusion.p0), channel_id=1, source_target_pairs={{0,2},{1,3},{2,4},{3,5},{4,6},{5,7},{6,0},{7,1},{8,10},{9,11},{10,... | collective-permute-start | bytes 196616 | tf_op jit(solution)/shard_map/ppermute | solution.py:243
  116.9 1.8 %collective-permute-done.4.p2 = bf16[2,128,128]{2,1,0:T(8,128)(2,1)S(1)} collective-permute-done((bf16[2,128,128]{2,1,0:T(8,128)(2,1)S(1)}, bf16[2,128,128]{2,1,0:T(8,128)(2,1)S(1)}, u32[]{:S(2)}, u32[]{:S(2)}) %collective-permute-start.4) | collective-permute-done | bytes 65568 | tf_op jit(solution)/shard_map/ppermute | solution.py:243
  118.7 2.8 %collective-permute-done.3.p1 = bf16[2,128,128]{2,1,0:T(8,128)(2,1)S(1)} collective-permute-done((bf16[2,128,128]{2,1,0:T(8,128)(2,1)S(1)}, bf16[2,128,128]{2,1,0:T(8,128)(2,1)S(1)}, u32[]{:S(2)}, u32[]{:S(2)}) %collective-permute-start.3) | collective-permute-done | bytes 65568 | tf_op jit(solution)/shard_map/ppermute | solution.py:243
  121.6 4.7 %collective-permute-start.6 = (bf16[64,32,128]{2,1,0:T(8,128)(2,1)S(1)}, bf16[64,32,128]{2,1,0:T(8,128)(2,1)S(1)}, u32[]{:S(2)}, u32[]{:S(2)}) collective-permute-start(bf16[64,32,128]{2,1,0:T(8,128)(2,1)S(1)} %all-to-all-done.4.src), channel_id=1, source_target_pairs={{0,1},{1,0},{2,3},{3,2},{4,5},{5,4},{6,7},{7,6},{8,9},{9,8},{10,11... | collective-permute-start | bytes 1572872 | tf_op jit(solution)/shard_map/ppermute | solution.py:245
  126.3 0.9 shard_map.105
  127.2 0.6 collective-permute-done.6.src
  127.8 1.6 %shard_map.106 = (f32[8,2,32,512]{3,2,1,0:T(8,128)}, f32[8,2,32,512]{3,2,1,0:T(8,128)}) custom-call(bf16[64,32,128]{2,1,0:T(8,128)(2,1)S(1)} %collective-permute-done.6.src, f32[8,32,512]{2,1,0:T(8,128)S(1)} %get-tuple-element.36.mine_in, f32[8,32,512]{2,1,0:T(8,128)S(1)} %get-tuple-element.37.mine_out), custom_call_target="tpu_custom_call" | custom-call | tf_op jit(solution)/shard_map/pallas_call | solution.py:252
  (19 shorter events, 0.6 us)
Async XLA Ops:
  3.0 7.8 %copy-start.4 = (bf16[128,512]{1,0:T(8,128)(2,1)S(1)}, bf16[128,512]{1,0:T(8,128)(2,1)}, u32[]{:S(2)}) copy-start(bf16[128,512]{1,0:T(8,128)(2,1)} %cotangent.1) | copy-start | bytes 393220
  3.0 27.6 %all-to-all-start = ((bf16[8,128,512]{2,1,0:T(8,128)(2,1)}), bf16[8,128,512]{2,1,0:T(8,128)(2,1)S(1)}, u32[]{:S(2)}, u32[]{:S(2)}) async-start(bf16[8,128,512]{2,1,0:T(8,128)(2,1)} %bitcast), calls=%async_computation | async-start | bytes 2097152 | tf_op jit(solution)/shard_map/all_to_all | solution.py:42
  10.8 19.8 %collective-permute-start = (bf16[16,512]{1,0:T(8,128)(2,1)S(1)}, bf16[16,512]{1,0:T(8,128)(2,1)S(1)}, u32[]{:S(2)}, u32[]{:S(2)}) collective-permute-start(bf16[16,512]{1,0:T(8,128)(2,1)S(1)} %constant_dynamic-slice_fusion), channel_id=1, source_target_pairs={{0,0},{1,16},{2,32},{3,48},{4,8},{5,24},{6,40},{7,56},{8,128},{9,1... | collective-permute-start | bytes 49160 | tf_op jit(solution)/shard_map/ppermute | solution.py:220
  30.8 25.3 %copy-start.1 = (bf16[512,512]{1,0:T(8,128)(2,1)S(1)}, bf16[512,512]{1,0:T(8,128)(2,1)}, u32[]{:S(2)}) copy-start(bf16[512,512]{1,0:T(8,128)(2,1)} %w_in_ref.1) | copy-start | bytes 1572868
  30.8 25.3 %copy-start.2 = (bf16[512,512]{1,0:T(8,128)(2,1)S(1)}, bf16[512,512]{1,0:T(8,128)(2,1)}, u32[]{:S(2)}) copy-start(bf16[512,512]{1,0:T(8,128)(2,1)} %w_out_ref.1) | copy-start | bytes 1572868
  30.8 25.3 %copy-start.5 = (f32[512]{0:T(512)S(1)}, f32[512]{0:T(512)}, u32[]{:S(2)}) copy-start(f32[512]{0:T(512)} %param.8) | copy-start | bytes 6148
  58.3 23.7 %copy-start = (bf16[128,1024]{1,0:T(8,128)(2,1)S(1)}, bf16[128,1024]{1,0:T(8,128)(2,1)}, u32[]{:S(2)}) copy-start(bf16[128,1024]{1,0:T(8,128)(2,1)} %adjacency.1) | copy-start | bytes 786436
  58.3 23.7 %copy-start.3 = (bf16[128,512]{1,0:T(8,128)(2,1)S(1)}, bf16[128,512]{1,0:T(8,128)(2,1)}, u32[]{:S(2)}) copy-start(bf16[128,512]{1,0:T(8,128)(2,1)} %nodes.1) | copy-start | bytes 393220
  58.3 23.7 %all-to-all-start.2 = ((bf16[8,160,512]{2,1,0:T(8,128)(2,1)}), bf16[8,160,512]{2,1,0:T(8,128)(2,1)S(1)}, u32[]{:S(2)}, u32[]{:S(2)}) async-start(bf16[8,160,512]{2,1,0:T(8,128)(2,1)} %get-tuple-element.23), calls=%async_computation.2 | async-start | bytes 2621440 | tf_op jit(solution)/shard_map/all_to_all | solution.py:42
  63.4 8.4 %collective-permute-start.1 = (bf16[16,512]{1,0:T(8,128)(2,1)S(1)}, bf16[16,512]{1,0:T(8,128)(2,1)S(1)}, u32[]{:S(2)}, u32[]{:S(2)}) collective-permute-start(bf16[16,512]{1,0:T(8,128)(2,1)S(1)} %get-tuple-element.24), channel_id=1, source_target_pairs={{0,0},{16,1},{32,2},{48,3},{8,4},{24,5},{40,6},{56,7},{128,8},{144... | collective-permute-start | bytes 49160 | tf_op jit(solution)/shard_map/ppermute | solution.py:232
  97.2 24.5 %all-to-all-start.4 = ((bf16[64,32,128]{2,1,0:T(8,128)(2,1)}), bf16[64,32,128]{2,1,0:T(8,128)(2,1)S(1)}, u32[]{:S(2)}, u32[]{:S(2)}) async-start(bf16[64,32,128]{2,1,0:T(8,128)(2,1)} %get-tuple-element.27), calls=%async_computation.4 | async-start | bytes 1048576 | tf_op jit(solution)/shard_map/all_to_all | solution.py:42
  105.0 4.1 %collective-permute-start.2 = (bf16[128,128]{1,0:T(8,128)(2,1)S(1)}, bf16[128,128]{1,0:T(8,128)(2,1)S(1)}, u32[]{:S(2)}, u32[]{:S(2)}) collective-permute-start(bf16[128,128]{1,0:T(8,128)(2,1)S(1)} %get-tuple-element.28), channel_id=1, source_target_pairs={{0,1},{1,0},{2,3},{3,2},{4,5},{5,4},{6,7},{7,6},{8,9},{9,8},{10,11... | collective-permute-start | bytes 98312 | tf_op jit(solution)/shard_map/ppermute | solution.py:242
  109.1 7.8 %collective-permute-start.5 = (bf16[2,128,128]{2,1,0:T(8,128)(2,1)S(1)}, bf16[2,128,128]{2,1,0:T(8,128)(2,1)S(1)}, u32[]{:S(2)}, u32[]{:S(2)}) collective-permute-start(bf16[2,128,128]{2,1,0:T(8,128)(2,1)S(1)} %pad_maximum_fusion.p0), channel_id=1, source_target_pairs={{0,6},{1,7},{2,0},{3,1},{4,2},{5,3},{6,4},{7,5},{8,14},{9,15},{10,... | collective-permute-start | bytes 196616 | tf_op jit(solution)/shard_map/ppermute | solution.py:243
  111.9 6.8 %collective-permute-start.4 = (bf16[2,128,128]{2,1,0:T(8,128)(2,1)S(1)}, bf16[2,128,128]{2,1,0:T(8,128)(2,1)S(1)}, u32[]{:S(2)}, u32[]{:S(2)}) collective-permute-start(bf16[2,128,128]{2,1,0:T(8,128)(2,1)S(1)} %pad_maximum_fusion.p0), channel_id=1, source_target_pairs={{0,4},{1,5},{2,6},{3,7},{4,0},{5,1},{6,2},{7,3},{8,12},{9,13},{10,... | collective-permute-start | bytes 196616 | tf_op jit(solution)/shard_map/ppermute | solution.py:243
  115.0 6.5 %collective-permute-start.3 = (bf16[2,128,128]{2,1,0:T(8,128)(2,1)S(1)}, bf16[2,128,128]{2,1,0:T(8,128)(2,1)S(1)}, u32[]{:S(2)}, u32[]{:S(2)}) collective-permute-start(bf16[2,128,128]{2,1,0:T(8,128)(2,1)S(1)} %pad_maximum_fusion.p0), channel_id=1, source_target_pairs={{0,2},{1,3},{2,4},{3,5},{4,6},{5,7},{6,0},{7,1},{8,10},{9,11},{10,... | collective-permute-start | bytes 196616 | tf_op jit(solution)/shard_map/ppermute | solution.py:243
  121.6 6.2 %collective-permute-start.6 = (bf16[64,32,128]{2,1,0:T(8,128)(2,1)S(1)}, bf16[64,32,128]{2,1,0:T(8,128)(2,1)S(1)}, u32[]{:S(2)}, u32[]{:S(2)}) collective-permute-start(bf16[64,32,128]{2,1,0:T(8,128)(2,1)S(1)} %all-to-all-done.4.src), channel_id=1, source_target_pairs={{0,1},{1,0},{2,3},{3,2},{4,5},{5,4},{6,7},{7,6},{8,9},{9,8},{10,11... | collective-permute-start | bytes 1572872 | tf_op jit(solution)/shard_map/ppermute | solution.py:245

commit v11 on v10

--- a/solution.py
+++ b/solution.py
@@ -42,12 +42,12 @@
     return lax.all_to_all(x, ALL, 0, 0, axis_index_groups=groups)
 
 
-def call(body, outs, *args, scratch=()):
+def call(body, outs, *args, scratch=(), free=()):
     return pl.pallas_call(
         body,
         out_shape=[jax.ShapeDtypeStruct(s, d) for s, d in outs],
         in_specs=[pl.BlockSpec(memory_space=pltpu.VMEM)] * len(args),
-        out_specs=[pl.BlockSpec(memory_space=pltpu.VMEM)] * len(outs),
+        out_specs=[pl.BlockSpec(memory_space=pl.ANY if i in free else pltpu.VMEM) for i in range(len(outs))],
         scratch_shapes=list(scratch),
         compiler_params=pltpu.CompilerParams(vmem_limit_bytes=40 * 1024 * 1024),
     )(*args)
@@ -75,7 +75,7 @@
         send[u, 128:144, :] = piece
 
 
-def update(got, gain_ref, w_in_ref, w_out_ref, out_ref, send, change, rows, columns):
+def update(got, gain_ref, w_in_ref, w_out_ref, out_ref, send, change, rows, columns, field, tiles, sems):
     summed = got[0, 0:128, :].astype(F32)
     for i in range(1, 8):
         summed = summed + got[i, 0:128, :].astype(F32)
@@ -103,8 +103,10 @@
     grad_summed = (
         scale * (grad_normed - normed * jnp.mean(grad_normed * normed, axis=-1, keepdims=True))
     ).astype(BF)
-    for v in E8:
-        send[v, 0:128, :] = grad_summed
+    field[...] = grad_summed
+    copies = [pltpu.make_async_copy(field, send.at[v, 0:128], sems.at[v]) for v in E8]
+    for copy in copies:
+        copy.start()
     left = left_half()
     top = lax.broadcasted_iota(jnp.int32, (16, 1), 0) < 14
 
@@ -124,8 +126,12 @@
         low = tile - high.astype(F32)
         for j in range(4):
             at = slice(128 * j, 128 * j + 128)
-            send[k, 128:144, at] = high[16 * j : 16 * j + 16]
-            send[k, 144:160, at] = jnp.where(top, low[16 * j : 16 * j + 16], gain_rows[:, at]).astype(BF)
+            tiles[k, 0:16, at] = high[16 * j : 16 * j + 16]
+            tiles[k, 16:32, at] = jnp.where(top, low[16 * j : 16 * j + 16], gain_rows[:, at]).astype(BF)
+        copies.append(pltpu.make_async_copy(tiles.at[k], send.at[k, 128:160], sems.at[8 + k]))
+        copies[-1].start()
+    for copy in copies:
+        copy.wait()
 
 
 def back_and_tile(adjacency, got, nodes, change, send, out):
@@ -227,7 +233,9 @@
         update,
         [((16, 512), BF), ((8, 160, 512), BF)],
         got, gain.reshape(1, 512), w_in, w_out,
-        scratch=[pltpu.VMEM((128, 512), BF)] + [pltpu.VMEM((8, 128, 128), BF)] * 2,
+        scratch=[pltpu.VMEM((128, 512), BF)] + [pltpu.VMEM((8, 128, 128), BF)] * 2
+        + [pltpu.VMEM((128, 512), BF), pltpu.VMEM((8, 32, 512), BF), pltpu.SemaphoreType.DMA((16,))],
+        free=(1,),
     )
     change = lax.ppermute(change, ALL, BACK)
     send, out = call(

time: 130 us -> 130 us (level)
  no operation moved by 1% of the time
where the time goes in v11:
time: 130 us; the launch traced here: 129 us
  starting transfers between devices  51.2 us (39%)
  blocking collectives  39.3 us (30%)
  waiting for transfers between devices  29.7 us (23%)
  Pallas kernels  5.93 us (5%)
  matrix products  2.41 us (2%)
    all_to_all x1, blocking collectives, trade(): return lax.all_to_all(x, ALL, 0, 0, axis_index_groups=groups)  25.3 us
    all_to_all x3, starting transfers between devices, trade(): return lax.all_to_all(x, ALL, 0, 0, axis_index_groups=groups)  20.7 us
    all_to_all x1, blocking collectives, shards(): lax.all_to_all(send, 'rep', 0, 0)  14 us
    ppermute x1, waiting for transfers between devices, shards(): cot = lax.ppermute(piece, ALL, OUT)  11.5 us
    all_to_all x3, waiting for transfers between devices, trade(): return lax.all_to_all(x, ALL, 0, 0, axis_index_groups=groups)  10.3 us
    ppermute x1, starting transfers between devices, shards(): cot = lax.ppermute(piece, ALL, OUT)  8.27 us
    ppermute x3, starting transfers between devices, shards(): pieces = [pieces] + [lax.ppermute(pieces, ALL, perm) for perm in SHIFT_X]  7.8 us
    ppermute x1, starting transfers between devices, shards(): change = lax.ppermute(change, ALL, BACK)  6.52 us
  transfers between devices with their start and end apart: 10, of which 8 were waited for; matrix products, arithmetic and copies ran while one was open for 0% of the time, Pallas kernels for 1%

profile of v11, /device:TPU:1, one launch (start us, length us, event | category | flops | bytes accessed | tf_op | source)
XLA Modules:
  0.0 129.4 jit_solution(8176178196704186465)
XLA Ops:
  0.6 2.4 %convolution_convert_fusion = bf16[1024,512]{1,0:T(8,128)(2,1)} fusion(bf16[128,1024]{1,0:T(8,128)(2,1)} %adjacency.1, bf16[128,512]{1,0:T(8,128)(2,1)} %nodes.1), kind=kOutput, calls=%fused_computation | convolution fusion | flops 134742016 | bytes 1441792 | tf_op jit(solution)/shard_map/dot_general | solution.py:38
  3.0 7.8 %all-to-all-start = ((bf16[8,128,512]{2,1,0:T(8,128)(2,1)}), bf16[8,128,512]{2,1,0:T(8,128)(2,1)S(1)}, u32[]{:S(2)}, u32[]{:S(2)}) async-start(bf16[8,128,512]{2,1,0:T(8,128)(2,1)} %bitcast), calls=%async_computation | async-start | bytes 2097152 | tf_op jit(solution)/shard_map/all_to_all | solution.py:42
  10.8 8.3 %collective-permute-start = (bf16[16,512]{1,0:T(8,128)(2,1)S(1)}, bf16[16,512]{1,0:T(8,128)(2,1)S(1)}, u32[]{:S(2)}, u32[]{:S(2)}) collective-permute-start(bf16[16,512]{1,0:T(8,128)(2,1)S(1)} %constant_dynamic-slice_fusion), channel_id=1, source_target_pairs={{0,0},{1,16},{2,32},{3,48},{4,8},{5,24},{6,40},{7,56},{8,128},{9,1... | collective-permute-start | bytes 49160 | tf_op jit(solution)/shard_map/ppermute | solution.py:226
  19.1 11.5 %collective-permute-done.cot = bf16[16,512]{1,0:T(8,128)(2,1)S(1)} collective-permute-done((bf16[16,512]{1,0:T(8,128)(2,1)S(1)}, bf16[16,512]{1,0:T(8,128)(2,1)S(1)}, u32[]{:S(2)}, u32[]{:S(2)}) %collective-permute-start) | collective-permute-done | bytes 16416 | tf_op jit(solution)/shard_map/ppermute | solution.py:226
  30.8 25.3 %all_to_all.25.got = bf16[8,144,512]{2,1,0:T(8,128)(2,1)S(1)} all-to-all(bf16[8,144,512]{2,1,0:T(8,128)(2,1)S(1)} %shard_map.101), channel_id=1, replica_groups={{0,16,32,48,8,24,40,56},{1,129,257,385,65,193,321,449},{2,18,34,50,10,2..., dimensions={0} | all-to-all | bytes 2359296 | tf_op jit(solution)/shard_map/all_to_all | solution.py:42
  56.1 2.2 %shard_map.102 = (bf16[16,512]{1,0:T(8,128)(2,1)S(1)}, bf16[8,160,512]{2,1,0:T(8,128)(2,1)}) custom-call(bf16[8,144,512]{2,1,0:T(8,128)(2,1)S(1)} %all_to_all.25.got, f32[1,512]{1,0:T(1,128)S(1)} %bitcast.10, bf16[512,512]{1,0:T(8,128)(2,1)S(1)} %copy-done.1, bf16[512,512]{1,0:T(8,128)(2,1)S(1)} %copy-done.2), custom_call_target="tpu_custom_call" | custom-call | tf_op jit(solution)/shard_map/pallas_call | solution.py:46
  58.3 5.1 %all-to-all-start.2 = ((bf16[8,160,512]{2,1,0:T(8,128)(2,1)}), bf16[8,160,512]{2,1,0:T(8,128)(2,1)S(1)}, u32[]{:S(2)}, u32[]{:S(2)}) async-start(bf16[8,160,512]{2,1,0:T(8,128)(2,1)} %get-tuple-element.23), calls=%async_computation.2 | async-start | bytes 2621440 | tf_op jit(solution)/shard_map/all_to_all | solution.py:42
  63.4 6.5 %collective-permute-start.1 = (bf16[16,512]{1,0:T(8,128)(2,1)S(1)}, bf16[16,512]{1,0:T(8,128)(2,1)S(1)}, u32[]{:S(2)}, u32[]{:S(2)}) collective-permute-start(bf16[16,512]{1,0:T(8,128)(2,1)S(1)} %get-tuple-element.24), channel_id=1, source_target_pairs={{0,0},{16,1},{32,2},{48,3},{8,4},{24,5},{40,6},{56,7},{128,8},{144... | collective-permute-start | bytes 49160 | tf_op jit(solution)/shard_map/ppermute | solution.py:240
  69.9 1.9 %collective-permute-done.1.change = bf16[16,512]{1,0:T(8,128)(2,1)S(1)} collective-permute-done((bf16[16,512]{1,0:T(8,128)(2,1)S(1)}, bf16[16,512]{1,0:T(8,128)(2,1)S(1)}, u32[]{:S(2)}, u32[]{:S(2)}) %collective-permute-start.1) | collective-permute-done | bytes 16416 | tf_op jit(solution)/shard_map/ppermute | solution.py:240
  71.8 10.1 %all-to-all-done.2.got = bf16[8,160,512]{2,1,0:T(8,128)(2,1)S(1)} async-done(((bf16[8,160,512]{2,1,0:T(8,128)(2,1)}), bf16[8,160,512]{2,1,0:T(8,128)(2,1)S(1)}, u32[]{:S(2)}, u32[]{:S(2)}) %all-to-all-start.2) | async-done | bytes 1310752 | tf_op jit(solution)/shard_map/all_to_all | solution.py:42
  82.3 14.0 %all_to_all.26.got = bf16[8,128,128]{2,1,0:T(8,128)(2,1)S(1)} all-to-all(bf16[8,128,128]{2,1,0:T(8,128)(2,1)S(1)} %get-tuple-element.25), channel_id=1, replica_groups=mesh['rows'=64,'rep'=8] {'rep'}, dimensions={0} | all-to-all | bytes 524288 | tf_op jit(solution)/shard_map/all_to_all | solution.py:247
  96.3 0.8 shard_map.104
  97.2 7.9 %all-to-all-start.4 = ((bf16[64,32,128]{2,1,0:T(8,128)(2,1)}), bf16[64,32,128]{2,1,0:T(8,128)(2,1)S(1)}, u32[]{:S(2)}, u32[]{:S(2)}) async-start(bf16[64,32,128]{2,1,0:T(8,128)(2,1)} %get-tuple-element.27), calls=%async_computation.4 | async-start | bytes 1048576 | tf_op jit(solution)/shard_map/all_to_all | solution.py:42
  105.0 3.2 %collective-permute-start.2 = (bf16[128,128]{1,0:T(8,128)(2,1)S(1)}, bf16[128,128]{1,0:T(8,128)(2,1)S(1)}, u32[]{:S(2)}, u32[]{:S(2)}) collective-permute-start(bf16[128,128]{1,0:T(8,128)(2,1)S(1)} %get-tuple-element.28), channel_id=1, source_target_pairs={{0,1},{1,0},{2,3},{3,2},{4,5},{5,4},{6,7},{7,6},{8,9},{9,8},{10,11... | collective-permute-start | bytes 98312 | tf_op jit(solution)/shard_map/ppermute | solution.py:250
  108.3 0.8 collective-permute-done.2
  109.1 2.8 %collective-permute-start.5 = (bf16[2,128,128]{2,1,0:T(8,128)(2,1)S(1)}, bf16[2,128,128]{2,1,0:T(8,128)(2,1)S(1)}, u32[]{:S(2)}, u32[]{:S(2)}) collective-permute-start(bf16[2,128,128]{2,1,0:T(8,128)(2,1)S(1)} %pad_maximum_fusion.p0), channel_id=1, source_target_pairs={{0,6},{1,7},{2,0},{3,1},{4,2},{5,3},{6,4},{7,5},{8,14},{9,15},{10,... | collective-permute-start | bytes 196616 | tf_op jit(solution)/shard_map/ppermute | solution.py:251
  111.9 3.1 %collective-permute-start.4 = (bf16[2,128,128]{2,1,0:T(8,128)(2,1)S(1)}, bf16[2,128,128]{2,1,0:T(8,128)(2,1)S(1)}, u32[]{:S(2)}, u32[]{:S(2)}) collective-permute-start(bf16[2,128,128]{2,1,0:T(8,128)(2,1)S(1)} %pad_maximum_fusion.p0), channel_id=1, source_target_pairs={{0,4},{1,5},{2,6},{3,7},{4,0},{5,1},{6,2},{7,3},{8,12},{9,13},{10,... | collective-permute-start | bytes 196616 | tf_op jit(solution)/shard_map/ppermute | solution.py:251
  115.0 1.9 %collective-permute-start.3 = (bf16[2,128,128]{2,1,0:T(8,128)(2,1)S(1)}, bf16[2,128,128]{2,1,0:T(8,128)(2,1)S(1)}, u32[]{:S(2)}, u32[]{:S(2)}) collective-permute-start(bf16[2,128,128]{2,1,0:T(8,128)(2,1)S(1)} %pad_maximum_fusion.p0), channel_id=1, source_target_pairs={{0,2},{1,3},{2,4},{3,5},{4,6},{5,7},{6,0},{7,1},{8,10},{9,11},{10,... | collective-permute-start | bytes 196616 | tf_op jit(solution)/shard_map/ppermute | solution.py:251
  116.9 1.8 %collective-permute-done.4.p2 = bf16[2,128,128]{2,1,0:T(8,128)(2,1)S(1)} collective-permute-done((bf16[2,128,128]{2,1,0:T(8,128)(2,1)S(1)}, bf16[2,128,128]{2,1,0:T(8,128)(2,1)S(1)}, u32[]{:S(2)}, u32[]{:S(2)}) %collective-permute-start.4) | collective-permute-done | bytes 65568 | tf_op jit(solution)/shard_map/ppermute | solution.py:251
  118.7 2.8 %collective-permute-done.3.p1 = bf16[2,128,128]{2,1,0:T(8,128)(2,1)S(1)} collective-permute-done((bf16[2,128,128]{2,1,0:T(8,128)(2,1)S(1)}, bf16[2,128,128]{2,1,0:T(8,128)(2,1)S(1)}, u32[]{:S(2)}, u32[]{:S(2)}) %collective-permute-start.3) | collective-permute-done | bytes 65568 | tf_op jit(solution)/shard_map/ppermute | solution.py:251
  121.7 4.7 %collective-permute-start.6 = (bf16[64,32,128]{2,1,0:T(8,128)(2,1)S(1)}, bf16[64,32,128]{2,1,0:T(8,128)(2,1)S(1)}, u32[]{:S(2)}, u32[]{:S(2)}) collective-permute-start(bf16[64,32,128]{2,1,0:T(8,128)(2,1)S(1)} %all-to-all-done.4.src), channel_id=1, source_target_pairs={{0,1},{1,0},{2,3},{3,2},{4,5},{5,4},{6,7},{7,6},{8,9},{9,8},{10,11... | collective-permute-start | bytes 1572872 | tf_op jit(solution)/shard_map/ppermute | solution.py:253
  126.3 0.9 shard_map.105
  127.2 0.6 collective-permute-done.6.src
  127.9 1.6 %shard_map.106 = (f32[8,2,32,512]{3,2,1,0:T(8,128)}, f32[8,2,32,512]{3,2,1,0:T(8,128)}) custom-call(bf16[64,32,128]{2,1,0:T(8,128)(2,1)S(1)} %collective-permute-done.6.src, f32[8,32,512]{2,1,0:T(8,128)S(1)} %get-tuple-element.36.mine_in, f32[8,32,512]{2,1,0:T(8,128)S(1)} %get-tuple-element.37.mine_out), custom_call_target="tpu_custom_call" | custom-call | tf_op jit(solution)/shard_map/pallas_call | solution.py:260
  (19 shorter events, 0.6 us)
Async XLA Ops:
  3.0 7.8 %copy-start.4 = (bf16[128,512]{1,0:T(8,128)(2,1)S(1)}, bf16[128,512]{1,0:T(8,128)(2,1)}, u32[]{:S(2)}) copy-start(bf16[128,512]{1,0:T(8,128)(2,1)} %cotangent.1) | copy-start | bytes 393220
  3.0 27.6 %all-to-all-start = ((bf16[8,128,512]{2,1,0:T(8,128)(2,1)}), bf16[8,128,512]{2,1,0:T(8,128)(2,1)S(1)}, u32[]{:S(2)}, u32[]{:S(2)}) async-start(bf16[8,128,512]{2,1,0:T(8,128)(2,1)} %bitcast), calls=%async_computation | async-start | bytes 2097152 | tf_op jit(solution)/shard_map/all_to_all | solution.py:42
  10.8 19.8 %collective-permute-start = (bf16[16,512]{1,0:T(8,128)(2,1)S(1)}, bf16[16,512]{1,0:T(8,128)(2,1)S(1)}, u32[]{:S(2)}, u32[]{:S(2)}) collective-permute-start(bf16[16,512]{1,0:T(8,128)(2,1)S(1)} %constant_dynamic-slice_fusion), channel_id=1, source_target_pairs={{0,0},{1,16},{2,32},{3,48},{4,8},{5,24},{6,40},{7,56},{8,128},{9,1... | collective-permute-start | bytes 49160 | tf_op jit(solution)/shard_map/ppermute | solution.py:226
  30.8 25.3 %copy-start.1 = (bf16[512,512]{1,0:T(8,128)(2,1)S(1)}, bf16[512,512]{1,0:T(8,128)(2,1)}, u32[]{:S(2)}) copy-start(bf16[512,512]{1,0:T(8,128)(2,1)} %w_in_ref.1) | copy-start | bytes 1572868
  30.8 25.3 %copy-start.2 = (bf16[512,512]{1,0:T(8,128)(2,1)S(1)}, bf16[512,512]{1,0:T(8,128)(2,1)}, u32[]{:S(2)}) copy-start(bf16[512,512]{1,0:T(8,128)(2,1)} %w_out_ref.1) | copy-start | bytes 1572868
  30.8 25.3 %copy-start.5 = (f32[512]{0:T(512)S(1)}, f32[512]{0:T(512)}, u32[]{:S(2)}) copy-start(f32[512]{0:T(512)} %param.8) | copy-start | bytes 6148
  58.3 23.7 %copy-start = (bf16[128,1024]{1,0:T(8,128)(2,1)S(1)}, bf16[128,1024]{1,0:T(8,128)(2,1)}, u32[]{:S(2)}) copy-start(bf16[128,1024]{1,0:T(8,128)(2,1)} %adjacency.1) | copy-start | bytes 786436
  58.3 23.7 %copy-start.3 = (bf16[128,512]{1,0:T(8,128)(2,1)S(1)}, bf16[128,512]{1,0:T(8,128)(2,1)}, u32[]{:S(2)}) copy-start(bf16[128,512]{1,0:T(8,128)(2,1)} %nodes.1) | copy-start | bytes 393220
  58.3 23.7 %all-to-all-start.2 = ((bf16[8,160,512]{2,1,0:T(8,128)(2,1)}), bf16[8,160,512]{2,1,0:T(8,128)(2,1)S(1)}, u32[]{:S(2)}, u32[]{:S(2)}) async-start(bf16[8,160,512]{2,1,0:T(8,128)(2,1)} %get-tuple-element.23), calls=%async_computation.2 | async-start | bytes 2621440 | tf_op jit(solution)/shard_map/all_to_all | solution.py:42
  63.4 8.4 %collective-permute-start.1 = (bf16[16,512]{1,0:T(8,128)(2,1)S(1)}, bf16[16,512]{1,0:T(8,128)(2,1)S(1)}, u32[]{:S(2)}, u32[]{:S(2)}) collective-permute-start(bf16[16,512]{1,0:T(8,128)(2,1)S(1)} %get-tuple-element.24), channel_id=1, source_target_pairs={{0,0},{16,1},{32,2},{48,3},{8,4},{24,5},{40,6},{56,7},{128,8},{144... | collective-permute-start | bytes 49160 | tf_op jit(solution)/shard_map/ppermute | solution.py:240
  97.2 24.5 %all-to-all-start.4 = ((bf16[64,32,128]{2,1,0:T(8,128)(2,1)}), bf16[64,32,128]{2,1,0:T(8,128)(2,1)S(1)}, u32[]{:S(2)}, u32[]{:S(2)}) async-start(bf16[64,32,128]{2,1,0:T(8,128)(2,1)} %get-tuple-element.27), calls=%async_computation.4 | async-start | bytes 1048576 | tf_op jit(solution)/shard_map/all_to_all | solution.py:42
  105.0 4.1 %collective-permute-start.2 = (bf16[128,128]{1,0:T(8,128)(2,1)S(1)}, bf16[128,128]{1,0:T(8,128)(2,1)S(1)}, u32[]{:S(2)}, u32[]{:S(2)}) collective-permute-start(bf16[128,128]{1,0:T(8,128)(2,1)S(1)} %get-tuple-element.28), channel_id=1, source_target_pairs={{0,1},{1,0},{2,3},{3,2},{4,5},{5,4},{6,7},{7,6},{8,9},{9,8},{10,11... | collective-permute-start | bytes 98312 | tf_op jit(solution)/shard_map/ppermute | solution.py:250
  109.1 7.8 %collective-permute-start.5 = (bf16[2,128,128]{2,1,0:T(8,128)(2,1)S(1)}, bf16[2,128,128]{2,1,0:T(8,128)(2,1)S(1)}, u32[]{:S(2)}, u32[]{:S(2)}) collective-permute-start(bf16[2,128,128]{2,1,0:T(8,128)(2,1)S(1)} %pad_maximum_fusion.p0), channel_id=1, source_target_pairs={{0,6},{1,7},{2,0},{3,1},{4,2},{5,3},{6,4},{7,5},{8,14},{9,15},{10,... | collective-permute-start | bytes 196616 | tf_op jit(solution)/shard_map/ppermute | solution.py:251
  111.9 6.8 %collective-permute-start.4 = (bf16[2,128,128]{2,1,0:T(8,128)(2,1)S(1)}, bf16[2,128,128]{2,1,0:T(8,128)(2,1)S(1)}, u32[]{:S(2)}, u32[]{:S(2)}) collective-permute-start(bf16[2,128,128]{2,1,0:T(8,128)(2,1)S(1)} %pad_maximum_fusion.p0), channel_id=1, source_target_pairs={{0,4},{1,5},{2,6},{3,7},{4,0},{5,1},{6,2},{7,3},{8,12},{9,13},{10,... | collective-permute-start | bytes 196616 | tf_op jit(solution)/shard_map/ppermute | solution.py:251
  115.0 6.5 %collective-permute-start.3 = (bf16[2,128,128]{2,1,0:T(8,128)(2,1)S(1)}, bf16[2,128,128]{2,1,0:T(8,128)(2,1)S(1)}, u32[]{:S(2)}, u32[]{:S(2)}) collective-permute-start(bf16[2,128,128]{2,1,0:T(8,128)(2,1)S(1)} %pad_maximum_fusion.p0), channel_id=1, source_target_pairs={{0,2},{1,3},{2,4},{3,5},{4,6},{5,7},{6,0},{7,1},{8,10},{9,11},{10,... | collective-permute-start | bytes 196616 | tf_op jit(solution)/shard_map/ppermute | solution.py:251
  121.7 6.2 %collective-permute-start.6 = (bf16[64,32,128]{2,1,0:T(8,128)(2,1)S(1)}, bf16[64,32,128]{2,1,0:T(8,128)(2,1)S(1)}, u32[]{:S(2)}, u32[]{:S(2)}) collective-permute-start(bf16[64,32,128]{2,1,0:T(8,128)(2,1)S(1)} %all-to-all-done.4.src), channel_id=1, source_target_pairs={{0,1},{1,0},{2,3},{3,2},{4,5},{5,4},{6,7},{7,6},{8,9},{9,8},{10,11... | collective-permute-start | bytes 1572872 | tf_op jit(solution)/shard_map/ppermute | solution.py:253
